TPU v7x, 32 devices: a whole 2x2x4 slice. The times are simulated.
32 devices in a mesh: dp: 8 (over z, y), expert: 4 (over x, core).
Axes of the slice: x: 2, y: 2, z: 4, core: 2. Of those that a mesh axis runs over, the one named last changes fastest.
Arguments:
- tokens: bfloat16 [16, 1024, 2048], P('dp', 'expert'), may hold values from -6 to 6
- lengths: int32 [16], P('dp'), may hold values from 256 to 1024, as said below
- routes: int32 [8, 4, 512, 8], P('dp', 'expert'), may hold values from 0 to 15, all different within a row; in each aligned block of 512 rows (0 to 511, 512 to 1023, ..., all dimensions but the last counted through in order) at most 288 rows name the same one
- w_query: bfloat16 [2048, 2048], P(('dp', 'expert')), may hold values from -0.125 to 0.125
- w_key: bfloat16 [2048, 2048], P(('dp', 'expert')), may hold values from -0.125 to 0.125
- w_value: bfloat16 [2048, 2048], P(('dp', 'expert')), may hold values from -0.125 to 0.125
- w_out: bfloat16 [2048, 2048], P(('dp', 'expert')), may hold values from -1.5 to 1.5
- w_router: bfloat16 [2048, 16], P(('dp', 'expert')), may hold values from -0.0625 to 0.0625
- attn_gain: bfloat16 [2048], P(('dp', 'expert')), may hold values from 0.099609375 to 1.8984375
- query_gain: bfloat16 [2048], P(('dp', 'expert')), may hold values from 0.099609375 to 1.8984375
- key_gain: bfloat16 [2048], P(('dp', 'expert')), may hold values from 0.099609375 to 1.8984375
- ffn_gain: bfloat16 [2048], P(('dp', 'expert')), may hold values from 0.099609375 to 1.8984375
- w_gate: bfloat16 [16, 2048, 1024], P('expert'), may hold values from -0.125 to 0.125
- w_up: bfloat16 [16, 2048, 1024], P('expert'), may hold values from -0.125 to 0.125
- w_down: bfloat16 [16, 1024, 2048], P('expert'), may hold values from -2 to 2
- cotangent: bfloat16 [16, 1024, 2048], P('dp', 'expert'), may hold values from -6 to 6
Outputs:
- output: bfloat16 [16, 1024, 2048], P('dp', 'expert')
- grad_input: float32 [16, 1024, 2048], P('dp', 'expert')
- grad_query: float32 [2048, 2048], P(('dp', 'expert'))
- grad_key: float32 [2048, 2048], P(('dp', 'expert'))
- grad_value: float32 [2048, 2048], P(('dp', 'expert'))
- grad_outproj: float32 [2048, 2048], P(('dp', 'expert'))
- grad_router: float32 [2048, 16], P(('dp', 'expert'))
- grad_attn_gain: float32 [2048], P(('dp', 'expert'))
- grad_query_gain: float32 [2048], P(('dp', 'expert'))
- grad_key_gain: float32 [2048], P(('dp', 'expert'))
- grad_ffn_gain: float32 [2048], P(('dp', 'expert'))
- grad_gate: float32 [16, 2048, 1024], P('expert', 'dp')
- grad_up: float32 [16, 2048, 1024], P('expert', 'dp')
- grad_down: float32 [16, 1024, 2048], P('expert', None, 'dp')
Inputs may be any that keep to these rules, and one draw needn't show every extreme that they name: `lengths`: in each data group one of its 2 sequences, chosen by the seed, has length 1024. Each token names 8 different experts; within the 512 tokens of one block routes[g,b] no expert is named more than 288 times, a bound that some block reaches.
All inputs are finite; a program needn't handle non-finite values.
Results may differ from a plain program's by a relative error of at most 0.02.
Values may be sent and summed in bfloat16 or wider, within the bound.
A program may use at most 512 MiB of HBM per device.

v0:
```python
from functools import partial
import math

import jax
import jax.numpy as jnp
from jax import lax
from jax.sharding import PartitionSpec as P

HEADS = 16
HEAD_DIM = 128
EXPERTS = 16


epsilon = 1e-05
highest = lax.Precision.HIGHEST


def rms_scale(values, gain_vector):
    factor = lax.rsqrt(jnp.mean(values * values, axis=-1, keepdims=True) + epsilon)
    return values * factor * gain_vector


def rotary(values, positions):
    half_dim = values.shape[-1] // 2
    frequencies = jnp.exp(
        jnp.arange(half_dim, dtype=jnp.float32) * (-2.0 * math.log(10000.0) / values.shape[-1])
    )
    angles = positions.astype(jnp.float32)[:, None] * frequencies[None, :]
    cosine = jnp.cos(angles)[:, None, :]
    sine_part = jnp.sin(angles)[:, None, :]
    first_half = values[..., :half_dim]
    second = values[..., half_dim:]
    return jnp.concatenate(
        [first_half * cosine - second * sine_part, second * cosine + first_half * sine_part],
        axis=-1,
    )


def post_norm(raw_values, gain_vector, places):
    normed_heads = rms_scale(raw_values, gain_vector).reshape(raw_values.shape[0], HEADS, HEAD_DIM)
    return rotary(normed_heads, places).reshape(raw_values.shape)


def softmax_parts(scores):
    row_peak = jnp.max(scores, axis=-1, keepdims=True)
    exponent = jnp.exp(scores - row_peak)
    row_total = jnp.sum(exponent, axis=-1, keepdims=True)
    return (exponent / row_total, row_peak, row_total)


def swiglu(gate_proj, up_proj):
    return gate_proj * jax.nn.sigmoid(gate_proj) * up_proj


def contract_rows(left_side, right_side):
    return lax.dot_general(
        left_side, right_side, (((0,), (0,)), ((), ())), preferred_element_type=jnp.float32
    )


def contract_last(left_side, right_side):
    return lax.dot_general(
        left_side, right_side, (((1,), (1,)), ((), ())), preferred_element_type=jnp.float32
    )


def local(
    tokens,
    lengths,
    routes,
    w_query,
    w_key,
    w_value,
    w_out,
    w_router,
    attn_gain,
    query_gain,
    key_gain,
    ffn_gain,
    w_gate,
    w_up,
    w_down,
    cotangent,
):
    query_full, key_full, value_full, out_full, router_full, attn_g, query_g, key_g, ffn_g = (
        lax.all_gather(w_query, ("dp", "expert"), axis=0, tiled=True),
        lax.all_gather(w_key, ("dp", "expert"), axis=0, tiled=True),
        lax.all_gather(w_value, ("dp", "expert"), axis=0, tiled=True),
        lax.all_gather(w_out, ("dp", "expert"), axis=0, tiled=True),
        lax.all_gather(w_router, ("dp", "expert"), axis=0, tiled=True),
        lax.all_gather(attn_gain, ("dp", "expert"), axis=0, tiled=True),
        lax.all_gather(query_gain, ("dp", "expert"), axis=0, tiled=True),
        lax.all_gather(key_gain, ("dp", "expert"), axis=0, tiled=True),
        lax.all_gather(ffn_gain, ("dp", "expert"), axis=0, tiled=True),
    )
    attn_g = attn_g.astype(jnp.float32)
    query_g = query_g.astype(jnp.float32)
    key_g = key_g.astype(jnp.float32)
    ffn_g = ffn_g.astype(jnp.float32)
    seq_count, span_dev, model_width = tokens.shape
    block_count = lax.axis_size("expert")
    seq_length = span_dev * block_count
    token_count = seq_count * span_dev
    top_count = routes.shape[-1]
    experts = EXPERTS
    capacity = (token_count * top_count * 9 + 8 * experts - 1) // (8 * experts)
    score_scale = 1.0 / math.sqrt(HEAD_DIM)
    places = lax.axis_index("expert") * span_dev + jnp.arange(span_dev, dtype=jnp.int32)
    flat_places = jnp.tile(places, seq_count)
    key_places = jnp.arange(seq_length, dtype=jnp.int32)
    flat_tokens = tokens.astype(jnp.float32).reshape(token_count, model_width)
    normed_f, norm_pull = jax.vjp(rms_scale, flat_tokens, attn_g)
    normed = normed_f.astype(jnp.bfloat16)
    query_raw = jnp.dot(normed, query_full, preferred_element_type=jnp.float32)
    key_raw = jnp.dot(normed, key_full, preferred_element_type=jnp.float32)
    value_raw = jnp.dot(normed, value_full, preferred_element_type=jnp.float32)
    query_f, query_pull = jax.vjp(partial(post_norm, places=flat_places), query_raw, query_g)
    key_f, key_pull = jax.vjp(partial(post_norm, places=flat_places), key_raw, key_g)
    query = query_f.astype(jnp.bfloat16).reshape(seq_count, span_dev, HEADS, HEAD_DIM)
    key_low = key_f.astype(jnp.bfloat16).reshape(seq_count, span_dev, model_width)
    value_low = value_raw.astype(jnp.bfloat16).reshape(seq_count, span_dev, model_width)
    key_all, value_all = (
        lax.all_gather(key_low, "expert", axis=1, tiled=True),
        lax.all_gather(value_low, "expert", axis=1, tiled=True),
    )
    key_all = key_all.reshape(seq_count, seq_length, HEADS, HEAD_DIM)
    value_all = value_all.reshape(seq_count, seq_length, HEADS, HEAD_DIM)
    scores = (
        jnp.einsum("sqhd,skhd->shqk", query, key_all, preferred_element_type=jnp.float32)
        * score_scale
    )
    allowed = (key_places[None, :] <= places[:, None])[None, None] & (
        key_places[None, None, None, :] < lengths[:, None, None, None]
    )
    attn_probs, row_peak, row_total = softmax_parts(jnp.where(allowed, scores, -1e30))
    probs_low = attn_probs.astype(jnp.bfloat16)
    attended = jnp.einsum(
        "shqk,skhd->sqhd", probs_low, value_all, preferred_element_type=jnp.float32
    )
    attended = attended.reshape(token_count, model_width).astype(jnp.bfloat16)
    resid = flat_tokens + jnp.dot(attended, out_full, preferred_element_type=jnp.float32)
    ffn_f, ffn_pull = jax.vjp(rms_scale, resid, ffn_g)
    ffn_in = ffn_f.astype(jnp.bfloat16)
    router = softmax_parts(jnp.dot(ffn_in, router_full, preferred_element_type=jnp.float32))[0]
    choose = routes.reshape(token_count, top_count)
    gate_weight = jnp.take_along_axis(router, choose, axis=1)
    pair_expert = choose.reshape(-1)
    onehot = (pair_expert[:, None] == jnp.arange(experts, dtype=jnp.int32)[None, :]).astype(
        jnp.int32
    )
    before = jnp.cumsum(onehot, axis=0) - onehot
    pair_slot = pair_expert * capacity + jnp.sum(before * onehot, axis=1)
    pair_count = token_count * top_count
    owner_pair = (
        jnp.full((experts * capacity,), pair_count, jnp.int32)
        .at[pair_slot]
        .set(jnp.arange(pair_count, dtype=jnp.int32))
    )
    owner_token = owner_pair // top_count
    padded = jnp.concatenate([ffn_in, jnp.zeros((1, model_width), jnp.bfloat16)], axis=0)
    send_rows = padded[owner_token].reshape(experts, capacity, model_width)
    buffer = lax.all_to_all(send_rows, "expert", split_axis=0, concat_axis=1, tiled=True)
    gate_proj = jnp.einsum("erd,edf->erf", buffer, w_gate, preferred_element_type=jnp.float32)
    up_proj = jnp.einsum("erd,edf->erf", buffer, w_up, preferred_element_type=jnp.float32)
    hidden_f, hidden_pull = jax.vjp(swiglu, gate_proj, up_proj)
    hidden = hidden_f.astype(jnp.bfloat16)
    expert_out = jnp.einsum(
        "erf,efd->erd", hidden, w_down, preferred_element_type=jnp.float32
    ).astype(jnp.bfloat16)
    returned = lax.all_to_all(expert_out, "expert", split_axis=1, concat_axis=0, tiled=True)
    expert_rows = returned.reshape(experts * capacity, model_width)[pair_slot].reshape(
        token_count, top_count, model_width
    )
    mixture = jnp.sum(gate_weight[:, :, None] * expert_rows, axis=1)
    output = (resid + mixture).astype(jnp.bfloat16).reshape(seq_count, span_dev, model_width)
    valid_mask = (places[None, :] < lengths[:, None]).astype(jnp.float32).reshape(token_count)
    out_grad = cotangent.astype(jnp.float32).reshape(token_count, model_width) * valid_mask[:, None]
    gate_grad = jnp.sum(out_grad[:, None, :] * expert_rows, axis=-1)
    pair_grads = (
        (gate_weight[:, :, None] * out_grad[:, None, :])
        .astype(jnp.bfloat16)
        .reshape(pair_count, model_width)
    )
    pair_grads = jnp.concatenate([pair_grads, jnp.zeros((1, model_width), jnp.bfloat16)], axis=0)
    grad_send = pair_grads[owner_pair].reshape(experts, capacity, model_width)
    dexpert = lax.all_to_all(grad_send, "expert", split_axis=0, concat_axis=1, tiled=True)
    dhidden = jnp.einsum("erd,efd->erf", dexpert, w_down, preferred_element_type=jnp.float32)
    grad_down = jnp.einsum("erf,erd->efd", hidden, dexpert, preferred_element_type=jnp.float32)
    dgate_f, dup_f = hidden_pull(dhidden)
    dgate = dgate_f.astype(jnp.bfloat16)
    dup_low = dup_f.astype(jnp.bfloat16)
    grad_gate = jnp.einsum("erd,erf->edf", buffer, dgate, preferred_element_type=jnp.float32)
    grad_up = jnp.einsum("erd,erf->edf", buffer, dup_low, preferred_element_type=jnp.float32)
    dbuffer = (
        jnp.einsum("erf,edf->erd", dgate, w_gate, preferred_element_type=jnp.float32)
        + jnp.einsum("erf,edf->erd", dup_low, w_up, preferred_element_type=jnp.float32)
    ).astype(jnp.bfloat16)
    dreturn = lax.all_to_all(dbuffer, "expert", split_axis=1, concat_axis=0, tiled=True)
    grad_gate, grad_up, grad_down = (
        lax.psum_scatter(
            grad_gate.astype(jnp.bfloat16), "dp", scatter_dimension=1, tiled=True
        ).astype(jnp.float32),
        lax.psum_scatter(
            grad_up.astype(jnp.bfloat16), "dp", scatter_dimension=1, tiled=True
        ).astype(jnp.float32),
        lax.psum_scatter(
            grad_down.astype(jnp.bfloat16), "dp", scatter_dimension=2, tiled=True
        ).astype(jnp.float32),
    )
    dffn = jnp.sum(
        dreturn.reshape(experts * capacity, model_width)[pair_slot].reshape(
            token_count, top_count, model_width
        ),
        axis=1,
        dtype=jnp.float32,
    )
    route_hits = (choose[:, :, None] == jnp.arange(experts, dtype=jnp.int32)[None, None, :]).astype(
        jnp.float32
    )
    drouter = jnp.sum(route_hits * gate_grad[:, :, None], axis=1)
    dlogits = router * (drouter - jnp.sum(router * drouter, axis=-1, keepdims=True))
    grad_router = lax.dot_general(
        ffn_in.astype(jnp.float32), dlogits, (((0,), (0,)), ((), ())), precision=highest
    )
    dffn = dffn + lax.dot_general(
        dlogits, router_full.astype(jnp.float32), (((1,), (1,)), ((), ())), precision=highest
    )
    dresid_norm, grad_ffn_g = ffn_pull(dffn)
    dresid = out_grad + dresid_norm
    dattn = dresid.astype(jnp.bfloat16)
    grad_outproj = contract_rows(attended, dattn)
    dattended = (
        contract_last(dattn, out_full)
        .astype(jnp.bfloat16)
        .reshape(seq_count, span_dev, HEADS, HEAD_DIM)
    )
    dprobs = jnp.einsum("sqhd,skhd->shqk", dattended, value_all, preferred_element_type=jnp.float32)
    row_delta = jnp.sum(attn_probs * dprobs, axis=-1, keepdims=True)
    dscore = (attn_probs * (dprobs - row_delta)).astype(jnp.bfloat16)
    dquery = (
        jnp.einsum("shqk,skhd->sqhd", dscore, key_all, preferred_element_type=jnp.float32)
        * score_scale
    )
    dkey_terms = (
        jnp.einsum("shqk,sqhd->skhd", dscore, query, preferred_element_type=jnp.float32)
        * score_scale
    )
    dvalue_terms = jnp.einsum(
        "shqk,sqhd->skhd", probs_low, dattended, preferred_element_type=jnp.float32
    )
    dkey_own, dvalue_own = (
        lax.psum_scatter(
            dkey_terms.reshape(seq_count, seq_length, model_width).astype(jnp.bfloat16),
            "expert",
            scatter_dimension=1,
            tiled=True,
        ).astype(jnp.float32),
        lax.psum_scatter(
            dvalue_terms.reshape(seq_count, seq_length, model_width).astype(jnp.bfloat16),
            "expert",
            scatter_dimension=1,
            tiled=True,
        ).astype(jnp.float32),
    )
    dquery_raw, grad_query_g = query_pull(dquery.reshape(token_count, model_width))
    dkey_raw, grad_key_g = key_pull(dkey_own.reshape(token_count, model_width))
    dquery_low = dquery_raw.astype(jnp.bfloat16)
    dkey_low = dkey_raw.astype(jnp.bfloat16)
    dvalue_low = dvalue_own.reshape(token_count, model_width).astype(jnp.bfloat16)
    grad_query = contract_rows(normed, dquery_low)
    grad_key = contract_rows(normed, dkey_low)
    grad_value = contract_rows(normed, dvalue_low)
    dnormed = (
        contract_last(dquery_low, query_full)
        + contract_last(dkey_low, key_full)
        + contract_last(dvalue_low, value_full)
    )
    dflat, grad_attn_g = norm_pull(dnormed)
    grad_input = (dresid + dflat).reshape(seq_count, span_dev, model_width)
    (
        grad_query,
        grad_key,
        grad_value,
        grad_outproj,
        grad_router,
        grad_attn_g,
        grad_query_g,
        grad_key_g,
        grad_ffn_g,
    ) = (
        lax.psum_scatter(grad_query, ("dp", "expert"), scatter_dimension=0, tiled=True),
        lax.psum_scatter(grad_key, ("dp", "expert"), scatter_dimension=0, tiled=True),
        lax.psum_scatter(grad_value, ("dp", "expert"), scatter_dimension=0, tiled=True),
        lax.psum_scatter(grad_outproj, ("dp", "expert"), scatter_dimension=0, tiled=True),
        lax.psum_scatter(grad_router, ("dp", "expert"), scatter_dimension=0, tiled=True),
        lax.psum_scatter(grad_attn_g, ("dp", "expert"), scatter_dimension=0, tiled=True),
        lax.psum_scatter(grad_query_g, ("dp", "expert"), scatter_dimension=0, tiled=True),
        lax.psum_scatter(grad_key_g, ("dp", "expert"), scatter_dimension=0, tiled=True),
        lax.psum_scatter(grad_ffn_g, ("dp", "expert"), scatter_dimension=0, tiled=True),
    )
    return (
        output,
        grad_input,
        grad_query,
        grad_key,
        grad_value,
        grad_outproj,
        grad_router,
        grad_attn_g,
        grad_query_g,
        grad_key_g,
        grad_ffn_g,
        grad_gate,
        grad_up,
        grad_down,
    )


def solution(mesh):
    placed = (
        P("dp", "expert", None),
        P("dp"),
        P("dp", "expert", None, None),
        P(("dp", "expert"), None),
        P(("dp", "expert"), None),
        P(("dp", "expert"), None),
        P(("dp", "expert"), None),
        P(("dp", "expert"), None),
        P(("dp", "expert")),
        P(("dp", "expert")),
        P(("dp", "expert")),
        P(("dp", "expert")),
        P("expert", None, None),
        P("expert", None, None),
        P("expert", None, None),
        P("dp", "expert", None),
    )
    return jax.shard_map(
        local,
        mesh=mesh,
        in_specs=placed,
        out_specs=(
            P("dp", "expert", None),
            P("dp", "expert", None),
            P(("dp", "expert"), None),
            P(("dp", "expert"), None),
            P(("dp", "expert"), None),
            P(("dp", "expert"), None),
            P(("dp", "expert"), None),
            P(("dp", "expert")),
            P(("dp", "expert")),
            P(("dp", "expert")),
            P(("dp", "expert")),
            P("expert", "dp", None),
            P("expert", "dp", None),
            P("expert", None, "dp"),
        ),
        check_vma=False,
    )
```

profile of v0, /device:TPU:0, one launch (start us, length us, event | category | flops | bytes accessed | tf_op | source)
XLA Modules:
  0.0 3635.1 jit_solution(5207341034372693823)
XLA Ops:
  16.0 42.5 %all-reduce.15 = (bf16[2048]{0:T(1024)(128)(2,1)S(1)}, bf16[2048]{0:T(1024)(128)(2,1)S(1)}, bf16[2048]{0:T(1024)(128)(2,1)S(1)}, bf16[2048]{0:T(1024)(128)(2,1)S(1)}) all-reduce(bf16[2048]{0:T(1024)(128)(2,1)S(1)} %dynamic-update-slice, bf16[2048]{0:T(1024)(128)(2,1)S(1)} %dynamic-update-slice.1, ...), channel_id=1, replica_groups=mesh['dp'=8,'expert'=4] {'dp','expert'}, use_global_device_ids=true, to_apply=%add.6 | all-reduce | flops 8192 | bytes 32768
  61.0 30.2 all-gather.8.cloned.1.call-done
  102.4 67.7 %all-gather.12.cloned.1.call-done = bf16[2048,2048]{1,0:T(8,128)(2,1)} async-done(((bf16[64,2048]{1,0:T(8,128)(2,1)}), bf16[2048,2048]{1,0:T(8,128)(2,1)}) %all-gather.12.cloned.1.call-update) | async-done | bytes 8388624 | tf_op jit(solution)/shard_map/all_gather | solution.py:86
  182.8 66.3 %all-gather.14.cloned.1.call-done = bf16[2048,2048]{1,0:T(8,128)(2,1)} async-done(((bf16[64,2048]{1,0:T(8,128)(2,1)}), bf16[2048,2048]{1,0:T(8,128)(2,1)}) %all-gather.14.cloned.1.call-update) | async-done | bytes 8388624 | tf_op jit(solution)/shard_map/all_gather | solution.py:87
  322.8 46.1 %all-gather.16.cloned.1.call-done = bf16[2,1024,2048]{1,2,0:T(8,128)(2,1)} async-done(((bf16[2,256,2048]{1,2,0:T(8,128)(2,1)}), bf16[2,1024,2048]{1,2,0:T(8,128)(2,1)}) %all-gather.16.cloned.1.call-update) | async-done | bytes 8388624 | tf_op jit(solution)/shard_map/all_gather | solution.py:123
  408.5 40.5 %all-gather.18.cloned.1.call-done = bf16[2048,2048]{1,0:T(8,128)(2,1)} async-done(((bf16[64,2048]{1,0:T(8,128)(2,1)}), bf16[2048,2048]{1,0:T(8,128)(2,1)}) %all-gather.18.cloned.1.call-update) | async-done | bytes 8388624 | tf_op jit(solution)/shard_map/all_gather | solution.py:89
  485.7 236.9 %all-gather = bf16[32,64,16]{1,2,0:T(8,128)(2,1)S(1)} all-gather(bf16[1,64,16]{1,2,0:T(8,128)(2,1)S(1)} %bitcast.257), channel_id=1, replica_groups=mesh['dp'=8,'expert'=4] {'dp','expert'}, dimensions={0}, use_global_device_ids=true | all-gather | bytes 67584 | tf_op jit(solution)/shard_map/all_gather | solution.py:90
  728.4 33.0 gather_fusion.4
  775.5 43.0 %gather_fusion.2 = bf16[4608,2048]{1,0:T(8,128)(2,1)} fusion(bf16[4097,2048]{1,0:T(8,128)(2,1)} %concatenate.17, s32[5120]{0:T(1024)S(1)} %copy-done.52), kind=kCustom, calls=%fused_computation.2 | custom fusion | bytes 37767168 | tf_op jit(solution)/shard_map/gather | solution.py:185
  843.1 188.5 %all-to-all-done.2 = bf16[16,288,2048]{2,1,0:T(8,128)(2,1)} async-done(((bf16[16,288,2048]{2,1,0:T(8,128)(2,1)}), bf16[16,288,2048]{2,1,0:T(8,128)(2,1)}, u32[]{:S(2)}, u32[]{:S(2)}) %all-to-all-start.2) | async-done | bytes 18874400 | tf_op jit(solution)/shard_map/all_to_all | solution.py:186
  1048.5 29.7 fusion.75
  1078.2 29.9 fusion.74
  1108.1 42.9 %multiply_convert_fusion.1 = (bf16[4,1152,1024]{2,1,0:T(8,128)(2,1)}, bf16[4,1152,1024]{2,1,0:T(8,128)(2,1)}, bf16[4,1152,1024]{2,1,0:T(8,128)(2,1)}) fusion(f32[4,1152,1024]{2,1,0:T(8,128)} %fusion.74, f32[4,1152,1024]{2,1,0:T(8,128)} %fusion.75, bf16[4,1152,2048]{2,1,0:T(8,128)(2,1)} %bitcast.233, bf16[4,1024,2048]{2,1,0:T(8,128)(2,1)} %param.30), kind=kOutput, calls=%fused_computation.26 | convolution fusion | flops 19402850304 | bytes 101711872 | tf_op jit(solution)/shard_map/erd,efd->erf/dot_general | solution.py:187
  1150.9 29.9 convolution_convert_fusion
  1213.1 29.3 fusion.76
  1242.4 32.2 fusion.4
  1299.3 119.3 %all-to-all-done.1 = bf16[4,1152,2048]{2,0,1:T(4,128)(2,1)} async-done(((bf16[4,1152,2048]{2,0,1:T(4,128)(2,1)}), bf16[4,1152,2048]{2,0,1:T(4,128)(2,1)}, u32[]{:S(2)}, u32[]{:S(2)}) %all-to-all-start.1) | async-done | bytes 18874400 | tf_op jit(solution)/shard_map/all_to_all | solution.py:170
  1447.2 40.1 %gather_fusion.1 = bf16[4096,2048]{1,0:T(8,128)(2,1)} fusion(bf16[4608,2048]{1,0:T(8,128)(2,1)} %bitcast.215, s32[4096]{0:T(1024)S(1)} %broadcast_clamp_fusion), kind=kCustom, calls=%fused_computation.1 | custom fusion | bytes 33570816 | tf_op jit(solution)/shard_map/gather | solution.py:171
  1504.6 126.8 %all-to-all-done.3 = bf16[4,1152,2048]{2,0,1:T(4,128)(2,1)} async-done(((bf16[4,1152,2048]{2,0,1:T(4,128)(2,1)}), bf16[4,1152,2048]{2,0,1:T(4,128)(2,1)}, u32[]{:S(2)}, u32[]{:S(2)}) %all-to-all-start.3) | async-done | bytes 18874400 | tf_op jit(solution)/shard_map/all_to_all | solution.py:198
  1652.2 40.5 %gather_fusion.3 = bf16[4096,2048]{1,0:T(8,128)(2,1)} fusion(bf16[4608,2048]{1,0:T(8,128)(2,1)} %bitcast.214, s32[4096]{0:T(1024)S(1)} %broadcast_clamp_fusion), kind=kCustom, calls=%fused_computation.3 | custom fusion | bytes 33570816 | tf_op jit(solution)/shard_map/gather | solution.py:211
  1778.0 28.4 multiply_convert_fusion
  1823.5 35.8 convolution_convert_fusion.1
  1859.4 29.9 convolution_convert_fusion.2
  1889.4 30.1 convolution_convert_fusion.3
  2060.1 40.5 %all-reduce.14 = (f32[2048]{0:T(1024)S(1)}, f32[2048]{0:T(1024)S(1)}, f32[2048]{0:T(1024)S(1)}, f32[2048]{0:T(1024)S(1)}) all-reduce(f32[2048]{0:T(1024)S(1)} %get-tuple-element.22, f32[2048]{0:T(1024)S(1)} %get-tuple-element.20, f32[2048]{0:T(1024)S(1)} %get-tuple-element.18, ...), channel_id=9, replica_groups=mesh['dp'=8,'expert'=4] {'dp','expert'}, use_global_device_ids=true, to_apply=%region_30.31.clone | all-reduce | flops 8192 | bytes 65536
  2109.6 202.1 %reduce-scatter.29.cloned.1.call-done = bf16[4,1024,256]{2,1,0:T(8,128)(2,1)} async-done(((bf16[4,1024,2048]{2,1,0:T(8,128)(2,1)}), bf16[4,1024,256]{2,1,0:T(8,128)(2,1)}) %reduce-scatter.29.cloned.1.call-update) | async-done | bytes 2097168 | tf_op jit(solution)/shard_map/reduce_scatter | solution.py:206
  2315.7 280.9 %reduce-scatter.27.cloned.1.call-done = bf16[4,256,1024]{2,1,0:T(8,128)(2,1)} async-done(((bf16[4,2048,1024]{2,1,0:T(8,128)(2,1)}), bf16[4,256,1024]{2,1,0:T(8,128)(2,1)}) %reduce-scatter.27.cloned.1.call-update) | async-done | bytes 2097168 | tf_op jit(solution)/shard_map/reduce_scatter | solution.py:203
  2600.6 281.1 %reduce-scatter.25.cloned.1.call-done = bf16[4,256,1024]{2,1,0:T(8,128)(2,1)} async-done(((bf16[4,2048,1024]{2,1,0:T(8,128)(2,1)}), bf16[4,256,1024]{2,1,0:T(8,128)(2,1)}) %reduce-scatter.25.cloned.1.call-update) | async-done | bytes 2097168 | tf_op jit(solution)/shard_map/reduce_scatter | solution.py:200
  2885.8 180.7 %reduce-scatter.23.cloned.1.call-done = f32[64,2048]{1,0:T(8,128)} async-done(((f32[2048,2048]{1,0:T(8,128)}), f32[64,2048]{1,0:T(8,128)}) %reduce-scatter.23.cloned.1.call-update) | async-done | bytes 524304 | tf_op jit(solution)/shard_map/reduce_scatter | solution.py:294
  3066.5 187.2 %reduce-scatter.21.cloned.1.call-done = f32[64,2048]{1,0:T(8,128)} async-done(((f32[2048,2048]{1,0:T(8,128)}), f32[64,2048]{1,0:T(8,128)}) %reduce-scatter.21.cloned.1.call-update) | async-done | bytes 524304 | tf_op jit(solution)/shard_map/reduce_scatter | solution.py:293
  3253.8 187.1 %reduce-scatter.17.cloned.1.call-done = f32[64,2048]{1,0:T(8,128)} async-done(((f32[2048,2048]{1,0:T(8,128)}), f32[64,2048]{1,0:T(8,128)}) %reduce-scatter.17.cloned.1.call-update) | async-done | bytes 524304 | tf_op jit(solution)/shard_map/reduce_scatter | solution.py:291
  3440.8 187.3 %reduce-scatter.19.cloned.1.call-done = f32[64,2048]{1,0:T(8,128)} async-done(((f32[2048,2048]{1,0:T(8,128)}), f32[64,2048]{1,0:T(8,128)}) %reduce-scatter.19.cloned.1.call-update) | async-done | bytes 524304 | tf_op jit(solution)/shard_map/reduce_scatter | solution.py:292
  (366 shorter events, 632.9 us)
Async XLA Ops:
  7.2 84.0 %all-gather.8.cloned.1.call-start = ((), (), s32[]{:S(2)}) async-start(), calls=%async_computation.14 | async-start | bytes 8650752 | tf_op jit(solution)/shard_map/all_gather | solution.py:88
  7.9 162.2 %all-gather.12.cloned.1.call-start = ((), (), s32[]{:S(2)}) async-start(), calls=%async_computation.16 | async-start | bytes 8650752 | tf_op jit(solution)/shard_map/all_gather | solution.py:86
  8.7 240.4 %all-gather.14.cloned.1.call-start = ((), (), s32[]{:S(2)}) async-start(), calls=%async_computation.17 | async-start | bytes 8650752 | tf_op jit(solution)/shard_map/all_gather | solution.py:87
  9.4 301.1 %all-gather.10.cloned.1.call-start = ((), (), s32[]{:S(2)}) async-start(), calls=%async_computation.15 | async-start | bytes 10485760 | tf_op jit(solution)/shard_map/all_gather | solution.py:124
  101.0 267.8 %all-gather.16.cloned.1.call-start = ((), (), s32[]{:S(2)}) async-start(), calls=%async_computation.18 | async-start | bytes 10485760 | tf_op jit(solution)/shard_map/all_gather | solution.py:123
  101.3 199.7 %copy-start.78 = (s32[256]{0:T(256)}, s32[256]{0:T(256)S(1)}, u32[]{:S(2)}) copy-start(s32[256]{0:T(256)S(1)} %get-tuple-element.69) | copy-start | bytes 3076
  101.4 155.5 %copy-start.48 = (f32[2048]{0:T(1024)}, f32[2048]{0:T(1024)S(1)}, u32[]{:S(2)}) copy-start(f32[2048]{0:T(1024)S(1)} %convert_element_type.187) | copy-start | bytes 24580
  102.4 157.5 %copy-start.24 = (f32[512,64]{1,0:T(8,128)}, f32[512,64]{1,0:T(8,128)S(1)}, u32[]{:S(2)}) copy-start(f32[512,64]{1,0:T(8,128)S(1)} %get-tuple-element.51) | copy-start | bytes 393220
  102.4 157.5 %copy-start.26 = (f32[512,64]{1,0:T(8,128)}, f32[512,64]{1,0:T(8,128)S(1)}, u32[]{:S(2)}) copy-start(f32[512,64]{1,0:T(8,128)S(1)} %get-tuple-element.52) | copy-start | bytes 393220
  276.7 172.4 %all-gather.18.cloned.1.call-start = ((), (), s32[]{:S(2)}) async-start(), calls=%async_computation.19 | async-start | bytes 8650752 | tf_op jit(solution)/shard_map/all_gather | solution.py:89
  277.7 179.1 %copy-start.46 = (f32[2048]{0:T(1024)}, f32[2048]{0:T(1024)S(1)}, u32[]{:S(2)}) copy-start(f32[2048]{0:T(1024)S(1)} %convert_element_type.193) | copy-start | bytes 24580
  478.0 244.8 %copy-start.42 = (s32[1,1,512,8]{2,3,1,0:T(8,128)S(1)}, s32[1,1,512,8]{2,3,1,0:T(8,128)}, u32[]{:S(2)}) copy-start(s32[1,1,512,8]{2,3,1,0:T(8,128)} %param.18) | copy-start | bytes 49156
  478.1 340.5 %all-to-all-start = ((bf16[16,288,2048]{2,1,0:T(8,128)(2,1)}), bf16[16,288,2048]{2,1,0:T(8,128)(2,1)}, u32[]{:S(2)}, u32[]{:S(2)}) async-start(bf16[16,288,2048]{2,1,0:T(8,128)(2,1)} %bitcast.216), calls=%async_computation | async-start | bytes 37748736 | tf_op jit(solution)/shard_map/all_to_all | solution.py:162
  485.6 241.5 %copy-start.12 = (bf16[512,2048]{1,0:T(8,128)(2,1)S(1)}, bf16[512,2048]{1,0:T(8,128)(2,1)}, u32[]{:S(2)}) copy-start(bf16[512,2048]{1,0:T(8,128)(2,1)} %copy-done.11) | copy-start | bytes 6291460
  485.7 242.1 %copy-start.68 = (f32[1,2,2,128]{3,1,2,0:T(2,128)}, f32[1,2,2,128]{3,1,2,0:T(2,128)S(1)}, u32[]{:S(2)}) copy-start(f32[1,2,2,128]{3,1,2,0:T(2,128)S(1)} %copy.174) | copy-start | bytes 6148
  818.5 213.1 %all-to-all-start.2 = ((bf16[16,288,2048]{2,1,0:T(8,128)(2,1)}), bf16[16,288,2048]{2,1,0:T(8,128)(2,1)}, u32[]{:S(2)}, u32[]{:S(2)}) async-start(bf16[16,288,2048]{2,1,0:T(8,128)(2,1)} %bitcast.217), calls=%async_computation.2 | async-start | bytes 37748736 | tf_op jit(solution)/shard_map/all_to_all | solution.py:186
  1205.5 213.1 %all-to-all-start.1 = ((bf16[4,1152,2048]{2,0,1:T(4,128)(2,1)}), bf16[4,1152,2048]{2,0,1:T(4,128)(2,1)}, u32[]{:S(2)}, u32[]{:S(2)}) async-start(bf16[4,1152,2048]{2,0,1:T(4,128)(2,1)} %copy.141), calls=%async_computation.1 | async-start | bytes 37748736 | tf_op jit(solution)/shard_map/all_to_all | solution.py:170
  1299.2 126.8 %copy-start.21 = (f32[4096]{0:T(1024)S(1)}, f32[4096]{0:T(1024)}, u32[]{:S(2)}) copy-start(f32[4096]{0:T(1024)} %copy-done.20) | copy-start | bytes 49156
  1299.2 127.0 %copy-start.23 = (s32[1,1,512,8]{3,2,1,0:T(8,128)S(1)}, s32[1,1,512,8]{3,2,1,0:T(8,128)}, u32[]{:S(2)}) copy-start(s32[1,1,512,8]{3,2,1,0:T(8,128)} %copy-done.22) | copy-start | bytes 49156
  1418.6 212.9 %all-to-all-start.3 = ((bf16[4,1152,2048]{2,0,1:T(4,128)(2,1)}), bf16[4,1152,2048]{2,0,1:T(4,128)(2,1)}, u32[]{:S(2)}, u32[]{:S(2)}) async-start(bf16[4,1152,2048]{2,0,1:T(4,128)(2,1)} %copy.144), calls=%async_computation.3 | async-start | bytes 37748736 | tf_op jit(solution)/shard_map/all_to_all | solution.py:198
  1425.9 505.8 %reduce-scatter.15.cloned.1.call-start = ((), (), s32[]{:S(2)}) async-start(), calls=%async_computation.21 | async-start | bytes 10485760 | tf_op jit(solution)/shard_map/reduce_scatter | solution.py:258
  1504.6 201.7 %copy-start.37 = (f32[512,16]{0,1:T(8,128)}, f32[512,16]{0,1:T(8,128)S(1)}, u32[]{:S(2)}) copy-start(f32[512,16]{0,1:T(8,128)S(1)} %select_reduce_fusion) | copy-start | bytes 98308
  1504.6 201.6 %copy-start.74 = (f32[512]{0:T(512)}, f32[512]{0:T(512)S(1)}, u32[]{:S(2)}) copy-start(f32[512]{0:T(512)S(1)} %multiply_reduce_fusion.8) | copy-start | bytes 6148
  1748.6 212.2 %reduce-scatter.13.cloned.1.call-start = ((), (), s32[]{:S(2)}) async-start(), calls=%async_computation.20 | async-start | bytes 10485760 | tf_op jit(solution)/shard_map/reduce_scatter | solution.py:252
  1818.6 209.7 %reduce-scatter.31.cloned.1.call-start = ((), (), s32[]{:S(2)}) async-start(), calls=%async_computation.29 | async-start | bytes 1081344
  1823.5 488.3 %reduce-scatter.29.cloned.1.call-start = ((), (), s32[]{:S(2)}) async-start(), calls=%async_computation.28 | async-start | bytes 18874368 | tf_op jit(solution)/shard_map/reduce_scatter | solution.py:206
  1859.3 737.2 %reduce-scatter.27.cloned.1.call-start = ((), (), s32[]{:S(2)}) async-start(), calls=%async_computation.27 | async-start | bytes 18874368 | tf_op jit(solution)/shard_map/reduce_scatter | solution.py:203
  1889.4 992.4 %reduce-scatter.25.cloned.1.call-start = ((), (), s32[]{:S(2)}) async-start(), calls=%async_computation.26 | async-start | bytes 18874368 | tf_op jit(solution)/shard_map/reduce_scatter | solution.py:200
  1919.5 1147.0 %reduce-scatter.23.cloned.1.call-start = ((), (), s32[]{:S(2)}) async-start(), calls=%async_computation.25 | async-start | bytes 17301504 | tf_op jit(solution)/shard_map/reduce_scatter | solution.py:294
  1931.6 1322.1 %reduce-scatter.21.cloned.1.call-start = ((), (), s32[]{:S(2)}) async-start(), calls=%async_computation.24 | async-start | bytes 17301504 | tf_op jit(solution)/shard_map/reduce_scatter | solution.py:293
  1943.2 1497.6 %reduce-scatter.17.cloned.1.call-start = ((), (), s32[]{:S(2)}) async-start(), calls=%async_computation.22 | async-start | bytes 17301504 | tf_op jit(solution)/shard_map/reduce_scatter | solution.py:291
  1988.7 1639.4 %reduce-scatter.19.cloned.1.call-start = ((), (), s32[]{:S(2)}) async-start(), calls=%async_computation.23 | async-start | bytes 17301504 | tf_op jit(solution)/shard_map/reduce_scatter | solution.py:292
  (82 other events, 1019.4 us)
Sparse Core Ops, SparseCore 0:
  10.9 80.2 all-gather.7
  94.0 76.0 all-gather.11
  173.0 76.0 all-gather.13
  251.1 56.8 all-gather.9
  309.4 59.3 all-gather.15
  371.5 77.4 all-gather.17
  1748.8 67.8 reduce-scatter.14
  1819.4 71.7 reduce-scatter.12
  1893.4 134.8 reduce-scatter.30
  2032.4 279.2 reduce-scatter.28
  2315.5 281.0 reduce-scatter.26
  2600.7 281.0 reduce-scatter.24
  2884.6 181.9 reduce-scatter.22
  3069.2 184.4 reduce-scatter.20
  3256.5 184.3 reduce-scatter.16
  3443.6 184.5 reduce-scatter.18
where the time goes:
time: 3640 us
  waiting for transfers between devices  2220 us (61%)
  matrix products  506 us (14%)
  local copies, waits for them, and re-layouts  414 us (11%)
  blocking collectives  320 us (9%)
  other arithmetic  133 us (4%)
    reduce_scatter x1, waiting for transfers between devices, local(): lax.psum_scatter(grad_gate.astype(jnp.bfloat16), 'dp', scatter_dimension=...  281 us
    reduce_scatter x1, waiting for transfers between devices, local(): lax.psum_scatter(grad_up.astype(jnp.bfloat16), 'dp', scatter_dimension=1,...  281 us
    all_gather x1, blocking collectives, local(): lax.all_gather(w_router, ('dp', 'expert'), axis=0, tiled=True)  237 us
    reduce_scatter x1, waiting for transfers between devices, local(): lax.psum_scatter(grad_down.astype(jnp.bfloat16), 'dp', scatter_dimension=...  202 us
    all_to_all x1, waiting for transfers between devices, local(): lax.all_to_all(grad_send, 'expert', split_axis=0, concat_axis=1, tiled=True)  189 us
    reduce_scatter x1, waiting for transfers between devices, local(): lax.psum_scatter(grad_key, ('dp', 'expert'), scatter_dimension=0, tiled=T...  187 us
    reduce_scatter x1, waiting for transfers between devices, local(): lax.psum_scatter(grad_value, ('dp', 'expert'), scatter_dimension=0, tiled...  187 us
    reduce_scatter x1, waiting for transfers between devices, local(): lax.psum_scatter(grad_query, ('dp', 'expert'), scatter_dimension=0, tiled...  187 us
  transfers between devices with their start and end apart: 20, of which 16 were waited for; matrix products, arithmetic and copies ran while one was open for 20% of the time, Pallas kernels for 0%

commit v1 on v0

v1 whole, which is shorter than its diff:
```python
from functools import partial
import math

import jax
import jax.numpy as jnp
from jax import lax
from jax.experimental import pallas as pl
from jax.experimental.pallas import tpu as pltpu
from jax.sharding import Mesh, PartitionSpec as P

HEAD_DIM = 128
EXPERTS = 16
EPS = 1e-05
F32 = jnp.float32
BF = jnp.bfloat16
VMEM_LIMIT = 60 * 1024 * 1024


def dot(a, b, dims=((1,), (0,))):
    return lax.dot_general(a, b, (dims, ((), ())), preferred_element_type=F32)


NT = ((1,), (1,))
TN = ((0,), (0,))


def masked_scores(q, k, i, j, rows, length, scale):
    s = dot(q, k, NT) * scale
    col = j * rows + lax.broadcasted_iota(jnp.int32, s.shape, 1)
    ok = col < length
    if i == j:
        row = i * rows + lax.broadcasted_iota(jnp.int32, s.shape, 0)
        ok = ok & (col <= row)
    return jnp.where(ok, s, -1e30)


def probs_of(q, k_ref, inv, i, rows, length, scale):
    parts = [
        masked_scores(q, k_ref[inv[j]], i, j, rows, length, scale) for j in range(i + 1)
    ]
    peak = parts[0].max(axis=1, keepdims=True)
    for s in parts[1:]:
        peak = jnp.maximum(peak, s.max(axis=1, keepdims=True))
    parts = [jnp.exp(s - peak) for s in parts]
    total = parts[0].sum(axis=1, keepdims=True)
    for e in parts[1:]:
        total = total + e.sum(axis=1, keepdims=True)
    inverse = 1.0 / total
    return [e * inverse for e in parts]


def attend_kernel(inv, lens, q_ref, k_ref, v_ref, o_ref, *, blocks, rows, scale):
    length = lens[pl.program_id(0)]
    for i in range(blocks):
        probs = probs_of(q_ref[inv[i]], k_ref, inv, i, rows, length, scale)
        out = jnp.zeros((rows, HEAD_DIM), F32)
        for j, p in enumerate(probs):
            out = out + dot(p.astype(BF), v_ref[inv[j]])
        o_ref[i] = out.astype(BF)


def attend_back_kernel(
    inv, lens, q_ref, k_ref, v_ref, do_ref, dq_ref, dk_ref, dv_ref, dk_acc, dv_acc, *, blocks, rows, scale
):
    length = lens[pl.program_id(0)]
    dk_acc[...] = jnp.zeros_like(dk_acc)
    dv_acc[...] = jnp.zeros_like(dv_acc)
    for i in range(blocks):
        q = q_ref[inv[i]]
        do = do_ref[i]
        probs = probs_of(q, k_ref, inv, i, rows, length, scale)
        dprobs = [dot(do, v_ref[inv[j]], NT) for j in range(i + 1)]
        delta = jnp.zeros((rows, 1), F32)
        for p, dp in zip(probs, dprobs):
            delta = delta + jnp.sum(p * dp, axis=1, keepdims=True)
        dq = jnp.zeros((rows, HEAD_DIM), F32)
        for j, (p, dp) in enumerate(zip(probs, dprobs)):
            ds = (p * (dp - delta)).astype(BF)
            dq = dq + dot(ds, k_ref[inv[j]])
            dk_acc[j] += dot(ds, q, TN)
            dv_acc[j] += dot(p.astype(BF), do, TN)
        dq_ref[inv[i]] = dq * scale
    for j in range(blocks):
        dk_ref[inv[j]] = dk_acc[j] * scale
        dv_ref[inv[j]] = dv_acc[j].astype(BF)


def attention_call(kernel, inv, lens, ins, out_types, scratch, flops):
    blocks, seqs, rows, width = ins[0].shape
    heads = width // HEAD_DIM
    spec = pl.BlockSpec((blocks, None, rows, HEAD_DIM), lambda s, h, *_: (0, s, 0, h))
    return pl.pallas_call(
        partial(kernel, blocks=blocks, rows=rows, scale=1.0 / math.sqrt(HEAD_DIM)),
        out_shape=[jax.ShapeDtypeStruct(ins[0].shape, t) for t in out_types],
        grid_spec=pltpu.PrefetchScalarGridSpec(
            num_scalar_prefetch=2,
            grid=(seqs, heads),
            in_specs=[spec] * len(ins),
            out_specs=[spec] * len(out_types),
            scratch_shapes=scratch,
        ),
        compiler_params=pltpu.CompilerParams(vmem_limit_bytes=VMEM_LIMIT),
        cost_estimate=pl.CostEstimate(
            flops=flops, bytes_accessed=ins[0].size * 8, transcendentals=blocks * rows * blocks * rows * seqs * heads
        ),
    )(inv, lens, *ins)


def pick_row(table, index):
    which = lax.broadcasted_iota(jnp.int32, table.shape, 0) == index
    return jnp.sum(jnp.where(which, table, 0.0), axis=0, keepdims=True)


def experts_in_kernel(
    base, f00, f01, f10, f11, c00, c01, c10, c11, r0, r1, g0, g1, wg, wu, wd, *rest, cap, aliased
):
    buf, og, hg, dg, du, gg, weight, dots = rest[5 if aliased else 0 :]
    e, f = pl.program_id(0), pl.program_id(1)
    expert = base[1] + e
    half = f00.shape[0]

    def select(b):
        rank = pick_row((r0, r1)[b][...], expert)
        slot = lax.broadcasted_iota(jnp.int32, (cap, rank.shape[1]), 0).astype(F32)
        return slot == rank

    @pl.when(f == 0)
    def _():
        for b in range(2):
            s = select(b)
            sb = s.astype(F32).astype(BF)
            rows = pl.ds(b * cap, cap)
            top, low = ((f00, f01), (f10, f11))[b]
            buf[rows, :] = (dot(sb[:, :half], top[...]) + dot(sb[:, half:], low[...])).astype(BF)
            top, low = ((c00, c01), (c10, c11))[b]
            og[rows, :] = (dot(sb[:, :half], top[...]) + dot(sb[:, half:], low[...])).astype(BF)
            gate = pick_row((g0, g1)[b][...], expert)
            weight[rows, :] = jnp.sum(jnp.where(s, gate, 0.0), axis=1, keepdims=True)
        dots[...] = jnp.zeros_like(dots)

    x, o = buf[...], og[...]
    gate = dot(x, wg[...])
    up = dot(x, wu[...])
    dh = dot(o, wd[...], NT)
    w = weight[...]
    sg = 1.0 / (1.0 + jnp.exp(-gate))
    silu = gate * sg
    hidden = (silu * up).astype(BF).astype(F32)
    dots[...] += jnp.sum(hidden * dh, axis=1, keepdims=True)
    dh = dh * w
    hg[...] = (hidden * w).astype(BF)
    dg[...] = (dh * up * (sg * (1.0 + gate * (1.0 - sg)))).astype(BF)
    du[...] = (dh * silu).astype(BF)

    @pl.when(f == pl.num_programs(1) - 1)
    def _():
        for b in range(2):
            s = select(b)
            gg[b] = jnp.sum(jnp.where(s, dots[pl.ds(b * cap, cap), :], 0.0), axis=0, keepdims=True)


def experts_in(group, groups, base, feats, cots, ranks, gates, wg, wu, wd, cap, local, before):
    tokens = ranks[0].shape[1]
    width, ff = wg.shape[1:]
    tile = 512
    whole = lambda a: pl.BlockSpec(a.shape, lambda e, f, s: (0, 0), pipeline_mode=pl.Buffered(1))
    small = [*feats, *cots, *ranks, *gates]
    rows = 2 * cap
    wide = pl.BlockSpec((None, rows, width), lambda e, f, s: (e, group, 0))
    thin = pl.BlockSpec((None, rows, tile), lambda e, f, s: (e, group, f))
    wide_type = jax.ShapeDtypeStruct((local, groups * rows, width), BF)
    thin_type = jax.ShapeDtypeStruct((local, groups * rows, ff), BF)
    aliased = before is not None
    n = 1 + len(small) + 3
    return pl.pallas_call(
        partial(experts_in_kernel, cap=cap, aliased=aliased),
        out_shape=[wide_type, wide_type, thin_type, thin_type, thin_type, jax.ShapeDtypeStruct((local, 2, 1, tokens), F32)],
        grid_spec=pltpu.PrefetchScalarGridSpec(
            num_scalar_prefetch=1,
            grid=(local, ff // tile),
            in_specs=[whole(a) for a in small]
            + [
                pl.BlockSpec((None, width, tile), lambda e, f, s: (s[0] + e, 0, f)),
                pl.BlockSpec((None, width, tile), lambda e, f, s: (s[0] + e, 0, f)),
                pl.BlockSpec((None, tile, width), lambda e, f, s: (s[0] + e, f, 0)),
            ]
            + [pl.BlockSpec(memory_space=pl.ANY)] * (5 if aliased else 0),
            out_specs=[wide, wide, thin, thin, thin, pl.BlockSpec((None, 2, 1, tokens), lambda e, f, s: (e, 0, 0, 0))],
            scratch_shapes=[pltpu.VMEM((rows, 1), F32), pltpu.VMEM((rows, 1), F32)],
        ),
        input_output_aliases={n + i: i for i in range(5)} if aliased else {},
        compiler_params=pltpu.CompilerParams(vmem_limit_bytes=VMEM_LIMIT),
        cost_estimate=pl.CostEstimate(
            flops=local * rows * width * (6 * ff + 4 * tokens),
            bytes_accessed=local * (3 * width * ff + rows * (2 * width + 3 * ff)) * 2 + 8 * tokens * width,
            transcendentals=local * rows * ff,
        ),
    )(base, *small, wg, wu, wd, *(before if aliased else ()))


def experts_out_kernel(base, hg, dg, du, r0, r1, wg, wu, wd, m0, m1, d0, d1, *accs, cap):
    e = pl.program_id(1)
    expert = base[1] + e
    out = dot(hg[e], wd[...]).astype(BF)
    back = (dot(dg[e], wg[...], NT) + dot(du[e], wu[...], NT)).astype(BF)
    for b, (rank, mix, dff) in enumerate(((r0, m0, d0), (r1, m1, d1))):
        table = rank[...]
        which = lax.broadcasted_iota(jnp.int32, table.shape, 1) == expert
        column = jnp.sum(jnp.where(which, table, 0.0), axis=1, keepdims=True)
        slot = lax.broadcasted_iota(jnp.int32, (table.shape[0], cap), 1).astype(F32)
        s = (slot == column).astype(F32).astype(BF)
        rows = slice(b * cap, (b + 1) * cap)
        for acc, value, final in ((accs[2 * b], out, mix), (accs[2 * b + 1], back, dff)):
            term = dot(s, value[rows])

            @pl.when(e == 0)
            def _():
                acc[...] = term

            @pl.when(e > 0)
            def _():
                acc[...] += term

            @pl.when(e == pl.num_programs(1) - 1)
            def _():
                final[...] = acc[...].astype(BF)


def experts_out(group, base, hg, dg, du, ranks, wg, wu, wd, cap, local):
    tokens = ranks[0].shape[0]
    width, ff = wg.shape[1:]
    tile = 512
    rows = 2 * cap
    thin = pl.BlockSpec((local, rows, ff), lambda d, e, s: (0, group, 0))
    whole = pl.BlockSpec((tokens, EXPERTS), lambda d, e, s: (0, 0))
    final = pl.BlockSpec((tokens, tile), lambda d, e, s: (0, d))
    return pl.pallas_call(
        partial(experts_out_kernel, cap=cap),
        out_shape=[jax.ShapeDtypeStruct((tokens, width), BF)] * 4,
        grid_spec=pltpu.PrefetchScalarGridSpec(
            num_scalar_prefetch=1,
            grid=(width // tile, local),
            in_specs=[
                thin,
                thin,
                thin,
                whole,
                whole,
                pl.BlockSpec((None, tile, ff), lambda d, e, s: (s[0] + e, d, 0)),
                pl.BlockSpec((None, tile, ff), lambda d, e, s: (s[0] + e, d, 0)),
                pl.BlockSpec((None, ff, tile), lambda d, e, s: (s[0] + e, 0, d)),
            ],
            out_specs=[final] * 4,
            scratch_shapes=[pltpu.VMEM((tokens, tile), F32)] * 4,
        ),
        compiler_params=pltpu.CompilerParams(vmem_limit_bytes=VMEM_LIMIT),
        cost_estimate=pl.CostEstimate(
            flops=local * rows * width * (6 * ff + 4 * tokens),
            bytes_accessed=local * (3 * width * ff + rows * 3 * ff) * 2 + 8 * tokens * width,
            transcendentals=0,
        ),
    )(base, hg, dg, du, *ranks, wg, wu, wd)


def shift(value, axis, by):
    n = lax.axis_size(axis)
    return lax.ppermute(value, axis, [(i, (i + by) % n) for i in range(n)])


def add_low(*terms):
    total = terms[0].astype(F32)
    for t in terms[1:]:
        total = total + t.astype(F32)
    return total.astype(BF)


def rms_parts(values):
    return values * lax.rsqrt(jnp.mean(values * values, axis=-1, keepdims=True) + EPS)


def local(
    nx,
    tokens,
    lengths,
    routes,
    w_query,
    w_key,
    w_value,
    w_out,
    w_router,
    attn_gain,
    query_gain,
    key_gain,
    ffn_gain,
    w_gate,
    w_up,
    w_down,
    cotangent,
):
    ALL, GROUP = ("r", "y", "x", "c"), ("x", "c")
    r, y, x, c = (lax.axis_index(a) for a in ALL)
    nr = lax.axis_size("r")
    me = 2 * x + c
    ng = 2 * nx
    seqs, span, width = tokens.shape
    token_count = seqs * span
    top_count = routes.shape[-1]
    cap = (token_count * top_count * 9 + 8 * EXPERTS - 1) // (8 * EXPERTS)
    cols = width // ng
    length = span * ng
    places = [(dx, dc) for dx in range(nx) for dc in range(2)]
    owner = jnp.stack([2 * ((x - dx) % nx) + (c - dc) % 2 for dx, dc in places]).astype(jnp.int32)
    inverse = jnp.stack(
        [2 * ((x - j // 2) % nx) + (c - j % 2) % 2 for j in range(ng)]
    ).astype(jnp.int32)

    w3 = jnp.stack([w_query, w_key, w_value], axis=1).reshape(-1, 3, ng, cols)
    w3 = w3.transpose(2, 0, 1, 3).reshape(ng, -1, 3 * cols)
    w3 = lax.all_to_all(w3, GROUP, split_axis=0, concat_axis=0, tiled=True)
    w3 = lax.all_gather(w3.reshape(-1, 3 * cols), ("r", "y"), axis=0, tiled=True)
    extras = jnp.concatenate(
        [w_router, attn_gain[:, None], query_gain[:, None], key_gain[:, None], ffn_gain[:, None]], axis=1
    )
    extras = lax.all_gather(extras, ALL, axis=0, tiled=True)
    out_full = lax.all_gather(w_out, ALL, axis=0, tiled=True)
    router_full = extras[:, :EXPERTS]
    attn_g, query_g, key_g, ffn_g = (extras[:, EXPERTS + i].astype(F32) for i in range(4))
    query_g = lax.dynamic_slice(query_g, (me * cols,), (cols,))
    key_g = lax.dynamic_slice(key_g, (me * cols,), (cols,))

    choose = routes.reshape(token_count, top_count)
    chosen = jnp.sum(
        (choose[:, :, None] == jnp.arange(EXPERTS, dtype=jnp.int32)).astype(F32), axis=1
    )
    tri = (
        lax.broadcasted_iota(jnp.int32, (token_count, token_count), 0)
        > lax.broadcasted_iota(jnp.int32, (token_count, token_count), 1)
    ).astype(BF)
    rank = jnp.where(chosen > 0, dot(tri, chosen.astype(BF)), -1.0)

    def gather_group(value):
        pieces = []
        for dx in range(nx):
            far = shift(value, "x", dx) if dx else value
            pieces += [far, shift(far, "c", 1)]
        return pieces

    own_places = me * span + jnp.arange(span, dtype=jnp.int32)
    valid = (own_places[None, :] < lengths[:, None]).reshape(token_count)
    own_cot = jnp.where(valid[:, None], cotangent.reshape(token_count, width), jnp.zeros((), BF))
    own_tokens = tokens.astype(F32).reshape(token_count, width)

    all_tokens = jnp.stack(gather_group(tokens)).reshape(ng * token_count, width).astype(F32)
    normed_n = rms_parts(all_tokens)
    normed = (normed_n * attn_g).astype(BF)

    def sum_group(stats):
        stats = stats.reshape(2, ng, token_count)
        stats = jnp.concatenate([lax.dynamic_slice_in_dim(stats, inverse[j], 1, 1) for j in range(ng)], 1)
        stats = lax.psum(stats, GROUP)
        stats = jnp.concatenate([lax.dynamic_slice_in_dim(stats, owner[p], 1, 1) for p in range(ng)], 1)
        return stats.reshape(2, ng * token_count)

    raw = dot(normed, w3)
    query_raw, key_raw = raw[:, :cols], raw[:, cols : 2 * cols]
    value = raw[:, 2 * cols :].astype(BF)
    squares = jnp.stack([jnp.sum(query_raw * query_raw, -1), jnp.sum(key_raw * key_raw, -1)])
    squares = sum_group(squares)
    factor = lax.rsqrt(squares / width + EPS)

    half = HEAD_DIM // 2
    frequencies = jnp.exp(jnp.arange(half, dtype=F32) * (-2.0 * math.log(10000.0) / HEAD_DIM))
    spot = owner[:, None] * span + jnp.arange(span, dtype=jnp.int32)[None, :]
    angles = spot.astype(F32)[:, :, None] * frequencies
    cosine, sine = jnp.cos(angles), jnp.sin(angles)
    cosine = jnp.concatenate([cosine, cosine], -1)[:, None, :, None, :]
    sine = jnp.concatenate([-sine, sine], -1)[:, None, :, None, :]

    def turn(v, sign):
        v = v.reshape(ng, seqs, span, -1, HEAD_DIM)
        swapped = jnp.concatenate([v[..., half:], v[..., :half]], -1)
        return (v * cosine + sign * swapped * sine).reshape(ng * token_count, cols)

    blocked = (ng, seqs, span, cols)
    query_n = query_raw * factor[0][:, None]
    key_n = key_raw * factor[1][:, None]
    query = turn(query_n * query_g, 1.0).astype(BF).reshape(blocked)
    key = turn(key_n * key_g, 1.0).astype(BF).reshape(blocked)
    value = value.reshape(blocked)
    pair_flops = 2 * length * length * seqs * cols * 5 // 8
    (attended,) = attention_call(
        attend_kernel, inverse, lengths, [query, key, value], [BF], [], 2 * pair_flops
    )
    attended = lax.all_to_all(attended, GROUP, split_axis=0, concat_axis=0, tiled=True)
    attended = attended.reshape(ng, token_count, cols).transpose(1, 0, 2).reshape(token_count, width)
    resid = own_tokens + dot(attended, out_full)
    ffn_scale = lax.rsqrt(jnp.mean(resid * resid, axis=-1, keepdims=True) + EPS)
    ffn_n = resid * ffn_scale
    ffn_in = (ffn_n * ffn_g).astype(BF)
    logits = dot(ffn_in, router_full)
    router = jnp.exp(logits - jnp.max(logits, axis=-1, keepdims=True))
    router = router / jnp.sum(router, axis=-1, keepdims=True)

    spots = [(dy, dx) for dy in range(2) for dx in range(nx)]

    def gather_pair(value):
        out = {(0, 0): value}
        for dx in range(1, nx):
            out[0, dx] = shift(value, "x", dx)
        for dx in range(nx):
            out[1, dx] = shift(out[0, dx], "y", 1)
        return {(dy, dx, dc): shift(v, "c", 1) if dc else v for (dy, dx), v in out.items() for dc in range(2)}

    def gather_pair_late(value):
        out = {(0, 0): value, (1, 0): shift(value, "y", 1)}
        for dx in range(1, nx):
            out[0, dx] = shift(value, "x", dx)
            out[1, dx] = shift(out[1, 0], "x", dx)
        return {(dy, dx, dc): shift(v, "c", 1) if dc else v for (dy, dx), v in out.items() for dc in range(2)}

    def gather_halves(value):
        h = token_count // 2
        return gather_pair(value[:h]), gather_pair_late(value[h:])

    cots = gather_halves(own_cot)
    ranks = gather_pair(rank)
    ranks_t = gather_pair(rank.T)
    gates_t = gather_pair(router.T)
    feats = gather_halves(ffn_in)

    local_experts = w_gate.shape[0]
    mine = local_experts // 2
    base = jnp.stack([y * mine, me * local_experts + y * mine]).astype(jnp.int32)
    before, gate_terms = None, {}
    for g, (dy, dx) in enumerate(spots):
        both = lambda halves: [halves[h][dy, dx, dc] for dc in range(2) for h in range(2)]
        pair = lambda table: [table[dy, dx, dc] for dc in range(2)]
        *before, gg = experts_in(
            g, len(spots), base, both(feats), both(cots), pair(ranks_t), pair(gates_t), w_gate, w_up, w_down, cap, mine, before
        )
        gate_terms[dy, dx] = gg
    buf, og, hg, dg, du = before

    def weight_grad(left, right):
        full = lax.dot_general(
            left, right, (((1,), (1,)), ((0,), (0,))), preferred_element_type=F32
        ).astype(BF)
        return lax.psum_scatter(full, "r", scatter_dimension=1, tiled=True)

    def finish_grad(part):
        rows = part.shape[1] // 2
        keep = lax.dynamic_slice_in_dim(part, y * rows, rows, 1)
        give = shift(lax.dynamic_slice_in_dim(part, (1 - y) * rows, rows, 1), "y", 1)
        first = jnp.where(y == 0, keep, give)
        second = jnp.where(y == 0, give, keep)
        return jnp.concatenate([first, second], axis=0).astype(F32)

    grad_down = finish_grad(weight_grad(og, hg)).transpose(0, 2, 1)
    grad_gate = finish_grad(weight_grad(buf, dg))
    grad_up = finish_grad(weight_grad(buf, du))

    mixes, backs = {}, {}
    for g, (dy, dx) in reversed(list(enumerate(spots))):
        m0, m1, d0, d1 = experts_out(
            g, base, hg, dg, du, [ranks[dy, dx, dc] for dc in range(2)], w_gate, w_up, w_down, cap, mine
        )
        mixes[dy, dx] = (m0, m1)
        backs[dy, dx] = (d0, d1)

    def send_back(parts):
        acc = {k: add_low(p0, shift(p1, "c", 1)) for k, (p0, p1) in parts.items()}
        h = token_count // 2
        top = {k: v[:h] for k, v in acc.items()}
        low = {k: v[h:] for k, v in acc.items()}
        far = add_low(top[1, 0], *[shift(top[1, dx], "x", -dx) for dx in range(1, nx)])
        top = [top[0, 0], shift(far, "y", 1)] + [shift(top[0, dx], "x", -dx) for dx in range(1, nx)]
        near = [low[0, 0], shift(low[1, 0], "y", 1)]
        for dx in range(1, nx):
            near.append(shift(add_low(low[0, dx], shift(low[1, dx], "y", 1)), "x", -dx))
        total = lambda terms: sum(t.astype(F32) for t in terms)
        return jnp.concatenate([total(top), total(near)], axis=0)

    dffn = send_back(backs)
    mixture = send_back(mixes)
    output = (resid + mixture).astype(BF).reshape(seqs, span, width)

    terms = jnp.stack([gate_terms[k] for k in spots])
    terms = terms.reshape(2, nx, mine, 2, token_count)
    order = []
    for k in range(2 * ng):
        ty, tx, tc = k // ng, (k % ng) // 2, k % 2
        piece = lax.dynamic_slice(
            terms, ((y - ty) % 2, (x - tx) % nx, 0, (c - tc) % 2, 0), (1, 1, mine, 1, token_count)
        )
        order.append(piece.reshape(mine, token_count))
    terms = lax.all_to_all(jnp.stack(order), ("y", "x", "c"), split_axis=0, concat_axis=0, tiled=True)
    drouter = terms.reshape(2, ng, mine, token_count).transpose(1, 0, 2, 3).reshape(EXPERTS, token_count).T

    dlogits = router * (drouter - jnp.sum(router * drouter, axis=-1, keepdims=True))
    highest = lax.Precision.HIGHEST
    grad_router = lax.dot_general(ffn_in.astype(F32), dlogits, (((0,), (0,)), ((), ())), precision=highest)
    dffn = dffn + lax.dot_general(
        dlogits, router_full.astype(F32), (((1,), (1,)), ((), ())), precision=highest
    )
    grad_ffn_g = jnp.sum(dffn * ffn_n, axis=0)
    gd = dffn * ffn_g
    dresid = own_cot.astype(F32) + ffn_scale * (gd - ffn_n * jnp.mean(gd * ffn_n, axis=-1, keepdims=True))

    dattn = dresid.astype(BF)
    grad_out = dot(attended, dattn, TN).astype(BF)
    dattended = dot(dattn, out_full, NT).astype(BF)
    dattended = dattended.reshape(token_count, ng, cols).transpose(1, 0, 2).reshape(blocked)
    dattended = lax.all_to_all(dattended, GROUP, split_axis=0, concat_axis=0, tiled=True)
    dquery, dkey, dvalue = attention_call(
        attend_back_kernel,
        inverse,
        lengths,
        [query, key, value, dattended],
        [F32, F32, BF],
        [pltpu.VMEM((ng, span, HEAD_DIM), F32)] * 2,
        5 * pair_flops,
    )
    dquery = turn(dquery.reshape(-1, cols), -1.0)
    dkey = turn(dkey.reshape(-1, cols), -1.0)
    means = jnp.stack(
        [jnp.sum(dquery * query_g * query_n, -1), jnp.sum(dkey * key_g * key_n, -1)]
    )
    means = sum_group(means) / width
    dquery_raw = factor[0][:, None] * (dquery * query_g - query_n * means[0][:, None])
    dkey_raw = factor[1][:, None] * (dkey * key_g - key_n * means[1][:, None])
    grad_query_g = jnp.sum(dquery * query_n, axis=0)
    grad_key_g = jnp.sum(dkey * key_n, axis=0)
    draw = jnp.concatenate(
        [dquery_raw.astype(BF), dkey_raw.astype(BF), dvalue.reshape(-1, cols)], axis=1
    )
    grad_three = dot(normed, draw, TN).astype(BF)
    dnormed = dot(draw, w3, NT)
    grad_attn_g = jnp.sum(dnormed * normed_n, axis=0)
    dnormed = dnormed.astype(BF).reshape(nx, 2, token_count, width)
    dnormed = [add_low(dnormed[dx, 0], shift(dnormed[dx, 1], "c", 1)) for dx in range(nx)]
    dnormed = sum(
        (shift(dnormed[dx], "x", -dx) if dx else dnormed[0]).astype(F32) for dx in range(nx)
    )
    own_scale = lax.rsqrt(jnp.mean(own_tokens * own_tokens, axis=-1, keepdims=True) + EPS)
    own_n = own_tokens * own_scale
    gd = dnormed * attn_g
    grad_input = dresid + own_scale * (gd - own_n * jnp.mean(gd * own_n, axis=-1, keepdims=True))
    grad_input = grad_input.reshape(seqs, span, width)

    def swap_y(part):
        keep = lax.dynamic_index_in_dim(part, y, 1, keepdims=False)
        give = lax.dynamic_index_in_dim(part, 1 - y, 1, keepdims=False)
        return add_low(keep, shift(give, "y", 1))

    g3 = swap_y(grad_three.reshape(nr, 2, -1, 3 * cols))
    g3 = lax.psum_scatter(g3, "r", scatter_dimension=0, tiled=True)
    g3 = lax.all_to_all(g3.reshape(ng, -1, 3 * cols), GROUP, split_axis=0, concat_axis=0, tiled=True)
    rows = g3.shape[1]
    g3 = g3.reshape(ng, rows, 3, cols).transpose(2, 1, 0, 3).reshape(3, rows, width).astype(F32)

    go = grad_out.reshape(nr * 2, nx, 2, rows, width)
    keep = lax.dynamic_index_in_dim(go, c, 2, keepdims=False)
    give = lax.dynamic_index_in_dim(go, 1 - c, 2, keepdims=False)
    go = add_low(keep, shift(give, "c", 1))
    go = add_low(
        *[
            shift(lax.dynamic_index_in_dim(go, (x + dx) % nx, 1, keepdims=False), "x", dx)
            if dx
            else lax.dynamic_index_in_dim(go, x, 1, keepdims=False)
            for dx in range(nx)
        ]
    )
    go = swap_y(go.reshape(nr, 2, rows, width))
    go = lax.psum_scatter(go, "r", scatter_dimension=0, tiled=True).reshape(rows, width).astype(F32)

    spread = lambda v: lax.dynamic_update_slice(jnp.zeros((width,), F32), v, (me * cols,))
    sums = jnp.concatenate(
        [
            grad_router,
            grad_attn_g[:, None],
            spread(grad_query_g)[:, None],
            spread(grad_key_g)[:, None],
            grad_ffn_g[:, None],
        ],
        axis=1,
    )
    sums = lax.psum_scatter(sums, ALL, scatter_dimension=0, tiled=True)
    return (
        output,
        grad_input,
        g3[0],
        g3[1],
        g3[2],
        go,
        sums[:, :EXPERTS],
        sums[:, EXPERTS],
        sums[:, EXPERTS + 1],
        sums[:, EXPERTS + 2],
        sums[:, EXPERTS + 3],
        grad_gate,
        grad_up,
        grad_down,
    )


def solution(mesh):
    ndp, nex = mesh.shape["dp"], mesh.shape["expert"]
    nx = nex // 2
    fine = Mesh(mesh.devices.reshape(ndp // 2, 2, nx, 2), ("r", "y", "x", "c"))
    dp, ex = ("r", "y"), ("x", "c")
    both = dp + ex
    placed = (
        P(dp, ex, None),
        P(dp),
        P(dp, ex, None, None),
        P(both, None),
        P(both, None),
        P(both, None),
        P(both, None),
        P(both, None),
        P(both),
        P(both),
        P(both),
        P(both),
        P(ex, None, None),
        P(ex, None, None),
        P(ex, None, None),
        P(dp, ex, None),
    )
    return jax.shard_map(
        partial(local, nx),
        mesh=fine,
        in_specs=placed,
        out_specs=(
            P(dp, ex, None),
            P(dp, ex, None),
            P(both, None),
            P(both, None),
            P(both, None),
            P(both, None),
            P(both, None),
            P(both),
            P(both),
            P(both),
            P(both),
            P(ex, dp, None),
            P(ex, dp, None),
            P(ex, None, dp),
        ),
        check_vma=False,
    )
```

time: 3640 us -> 1830 us (0.50)
  waiting for transfers between devices: 2220 us -> 831 us
  matrix products: 506 us -> 167 us
  Pallas kernels: 0 us -> 339 us
  local copies, waits for them, and re-layouts: 414 us -> 147 us
  blocking collectives: 320 us -> 120 us
  starting transfers between devices: 30.9 us -> 70 us
    reduce_scatter x9 -> x5, waiting for transfers between devices: 1510 us -> 337 us  [the longest x3 311 us: weight_grad(): return lax.psum_scatter(full, 'r', scatter_dimension=1, tiled=True)]
    ppermute x0 -> x82, waiting for transfers between devices: none -> 468 us  [shift(): return lax.ppermute(value, axis, [(i, (i + by) % n) for i in range(n)])]
    all_to_all x4, waiting for transfers between devices: 435 us -> 24.8 us  [the longest x1 24.8 us: local(): lax.all_to_all(dattended, GROUP, split_axis=0, concat_axis=0, tiled=True)]
    pallas_call x0 -> x10, Pallas kernels: none -> 339 us  [the longest x4 156 us: experts_out(): pl.pallas_call(partial(experts_out_kernel, cap=cap), out_shape=[jax.Shape...]
    dot_general x28 -> x13, matrix products: 483 us -> 167 us  [the longest x8 82.1 us: dot(): return lax.dot_general(a, b, (dims, ((), ())), preferred_element_type=F32)]
    all_gather x6 -> x2, waiting for transfers between devices: 251 us -> 0.02 us  [the longest x1 0.02 us: local(): out_full = lax.all_gather(w_out, ALL, axis=0, tiled=True)]
    gather x8 -> x0, local copies, waits for them, and re-layouts: 175 us -> none  [the longest x1 43 us: local(): grad_send = pair_grads[owner_pair].reshape(experts, capacity, model_width)]
    all_gather x1, blocking collectives: 237 us -> 82.8 us  [local(): extras = lax.all_gather(extras, ALL, axis=0, tiled=True)]
  transfers between devices with their start and end apart: 20 -> 94, of which waited for: 16 -> 35; matrix products, arithmetic and copies ran while one was open for 20% -> 18% of each run, Pallas kernels for 0% -> 17%
where the time goes in v1:
time: 1830 us; the launch traced here: 1820 us
  waiting for transfers between devices  831 us (45%)
  Pallas kernels  339 us (19%)
  matrix products  167 us (9%)
  local copies, waits for them, and re-layouts  147 us (8%)
  other arithmetic  132 us (7%)
  blocking collectives  120 us (7%)
  starting transfers between devices  70 us (4%)
    ppermute x82, waiting for transfers between devices, shift(): return lax.ppermute(value, axis, [(i, (i + by) % n) for i in range(n)])  468 us
    reduce_scatter x3, waiting for transfers between devices, weight_grad(): return lax.psum_scatter(full, 'r', scatter_dimension=1, tiled=True)  311 us
    pallas_call x4, Pallas kernels, experts_out(): pl.pallas_call(partial(experts_out_kernel, cap=cap), out_shape=[jax.Shape...  156 us
    pallas_call x4, Pallas kernels, experts_in(): pl.pallas_call(partial(experts_in_kernel, cap=cap, aliased=aliased), out_...  128 us
    all_gather x1, blocking collectives, local(): extras = lax.all_gather(extras, ALL, axis=0, tiled=True)  82.8 us
    dot_general x8, matrix products, dot(): return lax.dot_general(a, b, (dims, ((), ())), preferred_element_type=F32)  82.1 us
    dot_general x3, matrix products, weight_grad(): lax.dot_general(left, right, (((1,), (1,)), ((0,), (0,))), preferred_elem...  80.9 us
    pallas_call x2, Pallas kernels, attention_call(): pl.pallas_call(partial(kernel, blocks=blocks, rows=rows, scale=1.0 / math...  54.5 us
  transfers between devices with their start and end apart: 94, of which 35 were waited for; matrix products, arithmetic and copies ran while one was open for 18% of the time, Pallas kernels for 17%

profile of v1, /device:TPU:0, one launch (start us, length us, event | category | flops | bytes accessed | tf_op | source)
XLA Modules:
  0.0 1822.6 jit_solution(14491802862398043622)
XLA Ops:
  36.1 82.8 %all-gather = bf16[32,64,20]{1,2,0:T(8,128)(2,1)S(1)} all-gather(bf16[1,64,20]{1,2,0:T(8,128)(2,1)S(1)} %bitcast.330), channel_id=1, replica_groups=mesh['r'=4,'y'=2,'x'=2,'c'=2] {'r','y','x','c'}, dimensions={0}, use_global_device_ids=true | all-gather | bytes 84480 | tf_op jit(solution)/shard_map/all_gather | solution.py:324
  136.9 17.4 fusion.56
  216.6 20.3 %shard_map.263 = bf16[4,2,256,512]{3,2,1,0:T(8,128)(2,1)} custom-call(s32[4]{0:T(128)} %get-tuple-element.199.inv, s32[2]{0:T(128)} %lens.3, bf16[4,2,256,512]{3,2,1,0:T(8,128)(2,1)} %bitcast.285, bf16[4,2,256,512]{3,2,1,0:T(8,128)(2,1)} %bitcast.283, bf16[4,2,256,512]{3,2,1,0:T(8,128)(2,1)} %bitcast.290), custom_call_target="tpu_custom_call" | custom-call | flops 2684354560 | bytes 8388608 | tf_op jit(solution)/shard_map/pallas_call | solution.py:92
  249.6 46.1 %collective-permute-done.15 = f32[16,512]{0,1:T(8,128)S(1)} collective-permute-done((f32[16,512]{0,1:T(8,128)S(1)}, f32[16,512]{0,1:T(8,128)S(1)}, u32[]{:S(2)}, u32[]{:S(2)}) %collective-permute-start.15) | collective-permute-done | bytes 32800 | tf_op jit(solution)/shard_map/ppermute | solution.py:267
  341.6 22.5 %collective-permute-done.24.c00 = bf16[256,2048]{1,0:T(8,128)(2,1)} collective-permute-done((bf16[256,2048]{1,0:T(8,128)(2,1)}, bf16[256,2048]{1,0:T(8,128)(2,1)}, u32[]{:S(2)}, u32[]{:S(2)}) %collective-permute-start.24) | collective-permute-done | bytes 1048608 | tf_op jit(solution)/shard_map/ppermute | solution.py:267
  393.7 42.3 %collective-permute-done.18.g0 = f32[16,512]{1,0:T(8,128)S(1)} collective-permute-done((f32[16,512]{1,0:T(8,128)S(1)}, f32[16,512]{1,0:T(8,128)S(1)}, u32[]{:S(2)}, u32[]{:S(2)}) %collective-permute-start.18) | collective-permute-done | bytes 32800 | tf_op jit(solution)/shard_map/ppermute | solution.py:267
  455.5 32.1 %shard_map.264 = (bf16[2,2304,2048]{2,1,0:T(8,128)(2,1)}, bf16[2,2304,2048]{2,1,0:T(8,128)(2,1)}, bf16[2,2304,1024]{2,1,0:T(8,128)(2,1)}, bf16[2,2304,1024]{2,1,...) custom-call(s32[2]{0:T(128)} %pad_add_fusion.1.base, ...), custom_call_target="tpu_custom_call" | custom-call | flops 19327352832 | bytes 50069504 | tf_op jit(solution)/shard_map/pallas_call | solution.py:175
  503.6 31.9 %shard_map.265 = (bf16[2,2304,2048]{2,1,0:T(8,128)(2,1)}, bf16[2,2304,2048]{2,1,0:T(8,128)(2,1)}, bf16[2,2304,1024]{2,1,0:T(8,128)(2,1)}, bf16[2,2304,1024]{2,1,...) custom-call(s32[2]{0:T(128)} %pad_add_fusion.1.base, ...), custom_call_target="tpu_custom_call", output_to_operand_aliasing={{0}: (16, {}), {1}: (17, {}), {2}: (18, {}), {3}: (19, {}),... | custom-call | flops 19327352832 | bytes 50069504 | tf_op jit(solution)/shard_map/pallas_call | solution.py:175
  536.9 32.2 %shard_map.266 = (bf16[2,2304,2048]{2,1,0:T(8,128)(2,1)}, bf16[2,2304,2048]{2,1,0:T(8,128)(2,1)}, bf16[2,2304,1024]{2,1,0:T(8,128)(2,1)}, bf16[2,2304,1024]{2,1,...) custom-call(s32[2]{0:T(128)} %pad_add_fusion.1.base, ...), custom_call_target="tpu_custom_call", output_to_operand_aliasing={{0}: (16, {}), {1}: (17, {}), {2}: (18, {}), {3}: (19, {}),... | custom-call | flops 19327352832 | bytes 50069504 | tf_op jit(solution)/shard_map/pallas_call | solution.py:175
  570.3 32.1 %shard_map.267 = (bf16[2,2304,2048]{2,1,0:T(8,128)(2,1)}, bf16[2,2304,2048]{2,1,0:T(8,128)(2,1)}, bf16[2,2304,1024]{2,1,0:T(8,128)(2,1)}, bf16[2,2304,1024]{2,1,...) custom-call(s32[2]{0:T(128)} %pad_add_fusion.1.base, ...), custom_call_target="tpu_custom_call", output_to_operand_aliasing={{0}: (16, {}), {1}: (17, {}), {2}: (18, {}), {3}: (19, {}),... | custom-call | flops 19327352832 | bytes 50069504 | tf_op jit(solution)/shard_map/pallas_call | solution.py:175
  612.5 38.9 %shard_map.270 = (bf16[512,2048]{1,0:T(8,128)(2,1)}, bf16[512,2048]{1,0:T(8,128)(2,1)}, bf16[512,2048]{1,0:T(8,128)(2,1)}, bf16[512,2048]{1,0:T(8,128)(2,1)}) custom-call(s32[2]{0:T(128)} %pad_add_fusion.1.base, bf16[2,2304,1024]{2,1,0:T(8,128)(2,1)} %get-tuple-element.72.hg, bf16[2,2304,1024]{2,1,0:T(8,128)(2,1)} %get-tuple-element.73.dg, ...), custom_call_target="tpu_custom_call" | custom-call | flops 19327352832 | bytes 40632320 | tf_op jit(solution)/shard_map/pallas_call | solution.py:237
  652.5 38.9 %shard_map.269 = (bf16[512,2048]{1,0:T(8,128)(2,1)}, bf16[512,2048]{1,0:T(8,128)(2,1)}, bf16[512,2048]{1,0:T(8,128)(2,1)}, bf16[512,2048]{1,0:T(8,128)(2,1)}) custom-call(s32[2]{0:T(128)} %pad_add_fusion.1.base, bf16[2,2304,1024]{2,1,0:T(8,128)(2,1)} %get-tuple-element.72.hg, bf16[2,2304,1024]{2,1,0:T(8,128)(2,1)} %get-tuple-element.73.dg, ...), custom_call_target="tpu_custom_call" | custom-call | flops 19327352832 | bytes 40632320 | tf_op jit(solution)/shard_map/pallas_call | solution.py:237
  692.3 38.9 %shard_map.271 = (bf16[512,2048]{1,0:T(8,128)(2,1)}, bf16[512,2048]{1,0:T(8,128)(2,1)}, bf16[512,2048]{1,0:T(8,128)(2,1)}, bf16[512,2048]{1,0:T(8,128)(2,1)}) custom-call(s32[2]{0:T(128)} %pad_add_fusion.1.base, bf16[2,2304,1024]{2,1,0:T(8,128)(2,1)} %get-tuple-element.72.hg, bf16[2,2304,1024]{2,1,0:T(8,128)(2,1)} %get-tuple-element.73.dg, ...), custom_call_target="tpu_custom_call" | custom-call | flops 19327352832 | bytes 40632320 | tf_op jit(solution)/shard_map/pallas_call | solution.py:237
  732.4 39.2 %shard_map.268 = (bf16[512,2048]{1,0:T(8,128)(2,1)}, bf16[512,2048]{1,0:T(8,128)(2,1)}, bf16[512,2048]{1,0:T(8,128)(2,1)}, bf16[512,2048]{1,0:T(8,128)(2,1)}) custom-call(s32[2]{0:T(128)} %pad_add_fusion.1.base, bf16[2,2304,1024]{2,1,0:T(8,128)(2,1)} %get-tuple-element.72.hg, bf16[2,2304,1024]{2,1,0:T(8,128)(2,1)} %get-tuple-element.73.dg, ...), custom_call_target="tpu_custom_call" | custom-call | flops 19327352832 | bytes 40632320 | tf_op jit(solution)/shard_map/pallas_call | solution.py:237
  797.6 35.9 %collective-permute-done.70 = bf16[256,2048]{1,0:T(8,128)(2,1)S(1)} collective-permute-done((bf16[256,2048]{1,0:T(8,128)(2,1)S(1)}, bf16[256,2048]{1,0:T(8,128)(2,1)S(1)}, u32[]{:S(2)}, u32[]{:S(2)}) %collective-permute-start.70) | collective-permute-done | bytes 1048608 | tf_op jit(solution)/shard_map/ppermute | solution.py:267
  861.2 20.8 %collective-permute-done.71 = bf16[256,2048]{1,0:T(8,128)(2,1)S(1)} collective-permute-done((bf16[256,2048]{1,0:T(8,128)(2,1)S(1)}, bf16[256,2048]{1,0:T(8,128)(2,1)S(1)}, u32[]{:S(2)}, u32[]{:S(2)}) %collective-permute-start.71) | collective-permute-done | bytes 1048608 | tf_op jit(solution)/shard_map/ppermute | solution.py:267
  904.5 20.9 %collective-permute-done.61 = bf16[256,2048]{1,0:T(8,128)(2,1)S(1)} collective-permute-done((bf16[256,2048]{1,0:T(8,128)(2,1)S(1)}, bf16[256,2048]{1,0:T(8,128)(2,1)S(1)}, u32[]{:S(2)}, u32[]{:S(2)}) %collective-permute-start.61) | collective-permute-done | bytes 1048608 | tf_op jit(solution)/shard_map/ppermute | solution.py:267
  946.6 24.8 %all-to-all-done.3.do_ref = bf16[4,2,256,512]{3,2,1,0:T(8,128)(2,1)} async-done(((bf16[4,2,256,512]{3,2,1,0:T(8,128)(2,1)}), bf16[4,2,256,512]{3,2,1,0:T(8,128)(2,1)}, u32[]{:S(2)}, u32[]{:S(2)}) %all-to-all-start.3) | async-done | bytes 2097184 | tf_op jit(solution)/shard_map/all_to_all | solution.py:513
  971.4 34.2 %shard_map.272 = (f32[4,2,256,512]{3,2,1,0:T(8,128)}, f32[4,2,256,512]{3,2,1,0:T(8,128)}, bf16[4,2,256,512]{3,2,1,0:T(8,128)(2,1)}) custom-call(s32[4]{0:T(128)} %get-tuple-element.199.inv, s32[2]{0:T(128)} %lens.3, bf16[4,2,256,512]{3,2,1,0:T(8,128)(2,1)} %bitcast.286, bf16[4,2,256,512]{3,2,1,0:T(8,128)(2,1)} %bitcast.284, ...), custom_call_target="tpu_custom_call" | custom-call | flops 6710886400 | bytes 8388608 | tf_op jit(solution)/shard_map/pallas_call | solution.py:92
  1075.4 17.7 convolution_convert_fusion.1
  1099.2 20.9 %multiply_reduce_fusion = (f32[2048]{0:T(1024)S(1)}, bf16[2048,2048]{1,0:T(8,128)(2,1)}) fusion(f32[2048]{0:T(1024)S(1)} %bitcast.320, bf16[1,2,256,2048]{3,2,1,0:T(8,128)(2,1)} %bitcast.8, bf16[1,2,256,2048]{3,2,1,0:T(8,128)(2,1)} %bitcast.7, bf16[1,2,256,2048]{3,2,1,0:T(8,128)(2,1)} %bitcast.6, bf16[1,2,256,2048]{3,2,1,0:T(8,128)(2,1)S(1)} %bitcast.263, ...), kind=kOutput, calls=%fused_computation.1 | convolution fusion | flops 12937328640 | bytes 29376512 | tf_op jit(solution)/shard_map/dot_general | solution.py:20
  1121.6 47.2 %collective-permute-done.75 = bf16[4,256,1536]{2,1,0:T(8,128)(2,1)} collective-permute-done((bf16[4,256,1536]{2,1,0:T(8,128)(2,1)}, bf16[4,256,1536]{2,1,0:T(8,128)(2,1)}, u32[]{:S(2)}, u32[]{:S(2)}) %collective-permute-start.75) | collective-permute-done | bytes 3145760 | tf_op jit(solution)/shard_map/ppermute | solution.py:267
  1174.3 27.2 %convolution_convert_fusion.2 = bf16[2,2048,1024]{2,1,0:T(8,128)(2,1)} fusion(bf16[2,2304,2048]{2,1,0:T(8,128)(2,1)} %get-tuple-element.99, bf16[2,2304,1024]{2,1,0:T(8,128)(2,1)} %get-tuple-element.72.hg), kind=kOutput, calls=%fused_computation.12 | convolution fusion | flops 19331547136 | bytes 36700160 | tf_op jit(solution)/shard_map/dot_general | solution.py:445
  1201.6 26.8 %convolution_convert_fusion.3 = bf16[2,2048,1024]{2,1,0:T(8,128)(2,1)} fusion(bf16[2,2304,2048]{2,1,0:T(8,128)(2,1)} %get-tuple-element.98, bf16[2,2304,1024]{2,1,0:T(8,128)(2,1)} %get-tuple-element.74.du), kind=kOutput, calls=%fused_computation.13 | convolution fusion | flops 19331547136 | bytes 36700160 | tf_op jit(solution)/shard_map/dot_general | solution.py:445
  1259.5 46.4 %collective-permute-done.77 = bf16[8,64,2048]{2,1,0:T(8,128)(2,1)S(1)} collective-permute-done((bf16[8,64,2048]{2,1,0:T(8,128)(2,1)}, bf16[8,64,2048]{2,1,0:T(8,128)(2,1)S(1)}, u32[]{:S(2)}, u32[]{:S(2)}) %collective-permute-start.77) | collective-permute-done | bytes 2097184 | tf_op jit(solution)/shard_map/ppermute | solution.py:267
  1310.2 22.8 %collective-permute-done.78 = bf16[4,64,2048]{2,1,0:T(8,128)(2,1)S(1)} collective-permute-done((bf16[4,64,2048]{2,1,0:T(8,128)(2,1)S(1)}, bf16[4,64,2048]{2,1,0:T(8,128)(2,1)S(1)}, u32[]{:S(2)}, u32[]{:S(2)}) %collective-permute-start.78) | collective-permute-done | bytes 1048608 | tf_op jit(solution)/shard_map/ppermute | solution.py:267
  1334.6 26.9 %convolution_convert_fusion.4 = bf16[2,2048,1024]{2,1,0:T(8,128)(2,1)} fusion(bf16[2,2304,2048]{2,1,0:T(8,128)(2,1)} %get-tuple-element.98, bf16[2,2304,1024]{2,1,0:T(8,128)(2,1)} %get-tuple-element.73.dg), kind=kOutput, calls=%fused_computation.14 | convolution fusion | flops 19331547136 | bytes 36700160 | tf_op jit(solution)/shard_map/dot_general | solution.py:445
  1382.5 41.3 %collective-permute-done.74 = bf16[512,2048]{1,0:T(8,128)(2,1)} collective-permute-done((bf16[512,2048]{1,0:T(8,128)(2,1)}, bf16[512,2048]{1,0:T(8,128)(2,1)}, u32[]{:S(2)}, u32[]{:S(2)}) %collective-permute-start.74) | collective-permute-done | bytes 2097184 | tf_op jit(solution)/shard_map/ppermute | solution.py:267
  1437.6 24.5 %reduce-scatter.17.cloned.1.call-done = bf16[2,512,1024]{2,1,0:T(8,128)(2,1)} async-done(((bf16[2,2048,1024]{2,1,0:T(8,128)(2,1)}), bf16[2,512,1024]{2,1,0:T(8,128)(2,1)}) %reduce-scatter.17.cloned.1.call-update) | async-done | bytes 2097168 | tf_op jit(solution)/shard_map/reduce_scatter | solution.py:448
  1465.8 143.8 %reduce-scatter.15.cloned.1.call-done = bf16[2,512,1024]{2,1,0:T(8,128)(2,1)} async-done(((bf16[2,2048,1024]{2,1,0:T(8,128)(2,1)}), bf16[2,512,1024]{2,1,0:T(8,128)(2,1)}) %reduce-scatter.15.cloned.1.call-update) | async-done | bytes 2097168 | tf_op jit(solution)/shard_map/reduce_scatter | solution.py:448
  1613.4 26.5 %reduce-scatter.11.cloned.1.call-done = bf16[1,64,2048]{2,1,0:T(8,128)(2,1)} async-done(((bf16[4,64,2048]{2,1,0:T(8,128)(2,1)}), bf16[1,64,2048]{2,1,0:T(8,128)(2,1)}) %reduce-scatter.11.cloned.1.call-update) | async-done | bytes 262160 | tf_op jit(solution)/shard_map/reduce_scatter | solution.py:574
  1643.1 142.4 %reduce-scatter.13.cloned.1.call-done = bf16[2,512,1024]{2,1,0:T(8,128)(2,1)} async-done(((bf16[2,2048,1024]{2,1,0:T(8,128)(2,1)}), bf16[2,512,1024]{2,1,0:T(8,128)(2,1)}) %reduce-scatter.13.cloned.1.call-update) | async-done | bytes 2097168 | tf_op jit(solution)/shard_map/reduce_scatter | solution.py:448
  (555 shorter events, 539.9 us)
Async XLA Ops:
  7.2 129.8 %all-gather.4.cloned.1.call-start = ((), (), s32[]{:S(2)}) async-start(), calls=%async_computation.11 | async-start | bytes 7077888 | tf_op jit(solution)/shard_map/all_gather | solution.py:320
  35.0 282.3 %all-gather.6.cloned.1.call-start = ((), (), s32[]{:S(2)}) async-start(), calls=%async_computation.12 | async-start | bytes 8650752 | tf_op jit(solution)/shard_map/all_gather | solution.py:325
  35.8 83.4 %collective-permute-start.1 = (bf16[2,256,2048]{2,1,0:T(8,128)(2,1)S(1)}, bf16[2,256,2048]{2,1,0:T(8,128)(2,1)}, u32[]{:S(2)}, u32[]{:S(2)}) collective-permute-start(bf16[2,256,2048]{2,1,0:T(8,128)(2,1)S(1)} %copy-done.1), channel_id=1, source_target_pairs={{0,2},{2,0},{1,3},{3,1},{4,6},{6,4},{5,7},{7,5},{8,10},{10,8},{9,1... | collective-permute-start | bytes 6291464 | tf_op jit(solution)/shard_map/ppermute | solution.py:267
  35.9 89.4 %collective-permute-start = (bf16[2,256,2048]{2,1,0:T(8,128)(2,1)S(1)}, bf16[2,256,2048]{2,1,0:T(8,128)(2,1)}, u32[]{:S(2)}, u32[]{:S(2)}) collective-permute-start(bf16[2,256,2048]{2,1,0:T(8,128)(2,1)S(1)} %copy-done.1), channel_id=1, source_target_pairs={{0,1},{1,0},{2,3},{3,2},{4,5},{5,4},{6,7},{7,6},{8,9},{9,8},{10,11... | collective-permute-start | bytes 6291464 | tf_op jit(solution)/shard_map/ppermute | solution.py:267
  236.9 73.4 %all-to-all-start.1 = ((bf16[4,2,256,512]{3,2,1,0:T(8,128)(2,1)}), bf16[4,2,256,512]{3,2,1,0:T(8,128)(2,1)}, u32[]{:S(2)}, u32[]{:S(2)}) async-start(bf16[4,2,256,512]{3,2,1,0:T(8,128)(2,1)} %shard_map.263), calls=%async_computation.1 | async-start | bytes 4194304 | tf_op jit(solution)/shard_map/all_to_all | solution.py:394
  244.6 70.8 %collective-permute-start.41 = (bf16[256,2048]{1,0:T(8,128)(2,1)}, bf16[256,2048]{1,0:T(8,128)(2,1)}, u32[]{:S(2)}, u32[]{:S(2)}) collective-permute-start(bf16[256,2048]{1,0:T(8,128)(2,1)} %get-tuple-element.240.c00), channel_id=1, source_target_pairs={{0,1},{1,0},{2,3},{3,2},{4,5},{5,4},{6,7},{7,6},{8,9},{9,8},{10,11... | collective-permute-start | bytes 3145736 | tf_op jit(solution)/shard_map/ppermute | solution.py:267
  245.1 72.2 %collective-permute-start.9 = (bf16[256,2048]{1,0:T(8,128)(2,1)}, bf16[256,2048]{1,0:T(8,128)(2,1)S(1)}, u32[]{:S(2)}, u32[]{:S(2)}) collective-permute-start(bf16[256,2048]{1,0:T(8,128)(2,1)} %get-tuple-element.240.c00), channel_id=1, source_target_pairs={{0,2},{2,0},{1,3},{3,1},{4,6},{6,4},{5,7},{7,5},{8,10},{10,8},{9,1... | collective-permute-start | bytes 3145736 | tf_op jit(solution)/shard_map/ppermute | solution.py:267
  325.5 59.8 %collective-permute-start.10 = (bf16[256,2048]{1,0:T(8,128)(2,1)S(1)}, bf16[256,2048]{1,0:T(8,128)(2,1)S(1)}, u32[]{:S(2)}, u32[]{:S(2)}) collective-permute-start(bf16[256,2048]{1,0:T(8,128)(2,1)S(1)} %collective-permute-done.9.c00), channel_id=1, source_target_pairs={{0,4},{4,0},{1,5},{5,1},{2,6},{6,2},{3,7},{7,3},{8,12},{12,8},{9,1... | collective-permute-start | bytes 3145736 | tf_op jit(solution)/shard_map/ppermute | solution.py:267
  367.8 85.2 %collective-permute-start.39 = (bf16[256,2048]{1,0:T(8,128)(2,1)}, bf16[256,2048]{1,0:T(8,128)(2,1)}, u32[]{:S(2)}, u32[]{:S(2)}) collective-permute-start(bf16[256,2048]{1,0:T(8,128)(2,1)} %get-tuple-element.242.f00), channel_id=1, source_target_pairs={{0,1},{1,0},{2,3},{3,2},{4,5},{5,4},{6,7},{7,6},{8,9},{9,8},{10,11... | collective-permute-start | bytes 3145736 | tf_op jit(solution)/shard_map/ppermute | solution.py:267
  368.1 86.8 %collective-permute-start.40 = (bf16[256,2048]{1,0:T(8,128)(2,1)}, bf16[256,2048]{1,0:T(8,128)(2,1)}, u32[]{:S(2)}, u32[]{:S(2)}) collective-permute-start(bf16[256,2048]{1,0:T(8,128)(2,1)} %get-tuple-element.241.f01), channel_id=1, source_target_pairs={{0,1},{1,0},{2,3},{3,2},{4,5},{5,4},{6,7},{7,6},{8,9},{9,8},{10,11... | collective-permute-start | bytes 3145736 | tf_op jit(solution)/shard_map/ppermute | solution.py:267
  368.4 86.5 %collective-permute-start.3 = (bf16[256,2048]{1,0:T(8,128)(2,1)}, bf16[256,2048]{1,0:T(8,128)(2,1)}, u32[]{:S(2)}, u32[]{:S(2)}) collective-permute-start(bf16[256,2048]{1,0:T(8,128)(2,1)} %get-tuple-element.242.f00), channel_id=1, source_target_pairs={{0,2},{2,0},{1,3},{3,1},{4,6},{6,4},{5,7},{7,5},{8,10},{10,8},{9,1... | collective-permute-start | bytes 3145736 | tf_op jit(solution)/shard_map/ppermute | solution.py:267
  385.3 70.1 %collective-permute-start.31 = (bf16[256,2048]{1,0:T(8,128)(2,1)}, bf16[256,2048]{1,0:T(8,128)(2,1)S(1)}, u32[]{:S(2)}, u32[]{:S(2)}) collective-permute-start(bf16[256,2048]{1,0:T(8,128)(2,1)} %get-tuple-element.241.f01), channel_id=1, source_target_pairs={{0,2},{2,0},{1,3},{3,1},{4,6},{6,4},{5,7},{7,5},{8,10},{10,8},{9,1... | collective-permute-start | bytes 3145736 | tf_op jit(solution)/shard_map/ppermute | solution.py:267
  569.1 162.6 %collective-permute-start.45 = (f32[512,16]{1,0:T(8,128)S(1)}, f32[512,16]{1,0:T(8,128)S(1)}, u32[]{:S(2)}, u32[]{:S(2)}) collective-permute-start(f32[512,16]{1,0:T(8,128)S(1)} %convolution_select_fusion.r0), channel_id=1, source_target_pairs={{0,1},{1,0},{2,3},{3,2},{4,5},{5,4},{6,7},{7,6},{8,9},{9,8},{10,11... | collective-permute-start | bytes 98312 | tf_op jit(solution)/shard_map/ppermute | solution.py:267
  569.4 122.1 %collective-permute-start.56 = (f32[512,16]{1,0:T(8,128)}, f32[512,16]{1,0:T(8,128)S(1)}, u32[]{:S(2)}, u32[]{:S(2)}) collective-permute-start(f32[512,16]{1,0:T(8,128)} %collective-permute-done.50.r0), channel_id=1, source_target_pairs={{0,1},{1,0},{2,3},{3,2},{4,5},{5,4},{6,7},{7,6},{8,9},{9,8},{10,11... | collective-permute-start | bytes 98312 | tf_op jit(solution)/shard_map/ppermute | solution.py:267
  569.7 82.1 %collective-permute-start.48 = (f32[512,16]{1,0:T(8,128)}, f32[512,16]{1,0:T(8,128)S(1)}, u32[]{:S(2)}, u32[]{:S(2)}) collective-permute-start(f32[512,16]{1,0:T(8,128)} %collective-permute-done.47.r0), channel_id=1, source_target_pairs={{0,1},{1,0},{2,3},{3,2},{4,5},{5,4},{6,7},{7,6},{8,9},{9,8},{10,11... | collective-permute-start | bytes 98312 | tf_op jit(solution)/shard_map/ppermute | solution.py:267
  608.0 164.2 %all-to-all-start.2 = ((f32[8,2,512]{2,1,0:T(2,128)}), f32[8,2,512]{2,1,0:T(2,128)S(1)}, u32[]{:S(2)}, u32[]{:S(2)}) async-start(f32[8,2,512]{2,1,0:T(2,128)} %constant_dynamic-update-slice_fusion.2), calls=%async_computation.2 | async-start | bytes 65536 | tf_op jit(solution)/shard_map/all_to_all | solution.py:496
  651.4 127.4 %collective-permute-start.53 = (bf16[512,2048]{1,0:T(8,128)(2,1)}, bf16[512,2048]{1,0:T(8,128)(2,1)}, u32[]{:S(2)}, u32[]{:S(2)}) collective-permute-start(bf16[512,2048]{1,0:T(8,128)(2,1)} %get-tuple-element.80), channel_id=1, source_target_pairs={{0,1},{1,0},{2,3},{3,2},{4,5},{5,4},{6,7},{7,6},{8,9},{9,8},{10,11... | collective-permute-start | bytes 6291464 | tf_op jit(solution)/shard_map/ppermute | solution.py:267
  691.5 80.8 %collective-permute-start.49 = (bf16[512,2048]{1,0:T(8,128)(2,1)}, bf16[512,2048]{1,0:T(8,128)(2,1)}, u32[]{:S(2)}, u32[]{:S(2)}) collective-permute-start(bf16[512,2048]{1,0:T(8,128)(2,1)} %get-tuple-element.78), channel_id=1, source_target_pairs={{0,1},{1,0},{2,3},{3,2},{4,5},{5,4},{6,7},{7,6},{8,9},{9,8},{10,11... | collective-permute-start | bytes 6291464 | tf_op jit(solution)/shard_map/ppermute | solution.py:267
  785.0 52.6 %collective-permute-start.60 = (bf16[256,2048]{1,0:T(8,128)(2,1)S(1)}, bf16[256,2048]{1,0:T(8,128)(2,1)S(1)}, u32[]{:S(2)}, u32[]{:S(2)}) collective-permute-start(bf16[256,2048]{1,0:T(8,128)(2,1)S(1)} %get-tuple-element.238), channel_id=1, source_target_pairs={{0,4},{4,0},{1,5},{5,1},{2,6},{6,2},{3,7},{7,3},{8,12},{12,8},{9,1... | collective-permute-start | bytes 3145736 | tf_op jit(solution)/shard_map/ppermute | solution.py:267
  795.0 60.9 %collective-permute-start.69 = (bf16[256,2048]{1,0:T(8,128)(2,1)S(1)}, bf16[256,2048]{1,0:T(8,128)(2,1)S(1)}, u32[]{:S(2)}, u32[]{:S(2)}) collective-permute-start(bf16[256,2048]{1,0:T(8,128)(2,1)S(1)} %slice.249), channel_id=1, source_target_pairs={{0,4},{4,0},{1,5},{5,1},{2,6},{6,2},{3,7},{7,3},{8,12},{12,8},{9,1... | collective-permute-start | bytes 3145736 | tf_op jit(solution)/shard_map/ppermute | solution.py:267
  838.6 62.2 %collective-permute-start.59 = (bf16[256,2048]{1,0:T(8,128)(2,1)S(1)}, bf16[256,2048]{1,0:T(8,128)(2,1)S(1)}, u32[]{:S(2)}, u32[]{:S(2)}) collective-permute-start(bf16[256,2048]{1,0:T(8,128)(2,1)S(1)} %slice.241), channel_id=1, source_target_pairs={{0,4},{4,0},{1,5},{5,1},{2,6},{6,2},{3,7},{7,3},{8,12},{12,8},{9,1... | collective-permute-start | bytes 3145736 | tf_op jit(solution)/shard_map/ppermute | solution.py:267
  859.5 65.9 %collective-permute-start.61 = (bf16[256,2048]{1,0:T(8,128)(2,1)S(1)}, bf16[256,2048]{1,0:T(8,128)(2,1)S(1)}, u32[]{:S(2)}, u32[]{:S(2)}) collective-permute-start(bf16[256,2048]{1,0:T(8,128)(2,1)S(1)} %add_convert_fusion.10), channel_id=1, source_target_pairs={{0,2},{2,0},{1,3},{3,1},{4,6},{6,4},{5,7},{7,5},{8,10},{10,8},{9,1... | collective-permute-start | bytes 3145736 | tf_op jit(solution)/shard_map/ppermute | solution.py:267
  945.6 432.1 %reduce-scatter.19.cloned.1.call-start = ((), (), s32[]{:S(2)}) async-start(), calls=%async_computation.18 | async-start | bytes 1081344
  1097.8 71.1 %collective-permute-start.75 = (bf16[4,256,1536]{2,1,0:T(8,128)(2,1)}, bf16[4,256,1536]{2,1,0:T(8,128)(2,1)}, u32[]{:S(2)}, u32[]{:S(2)}) collective-permute-start(bf16[4,256,1536]{2,1,0:T(8,128)(2,1)} %dynamic-slice_bitcast_fusion), channel_id=1, source_target_pairs={{0,4},{4,0},{1,5},{5,1},{2,6},{6,2},{3,7},{7,3},{8,12},{12,8},{9,1... | collective-permute-start | bytes 9437192 | tf_op jit(solution)/shard_map/ppermute | solution.py:267
  1121.6 312.3 %reduce-scatter.9.cloned.1.call-start = ((), (), s32[]{:S(2)}) async-start(), calls=%async_computation.13 | async-start | bytes 3932160 | tf_op jit(solution)/shard_map/reduce_scatter | solution.py:556
  1174.3 287.8 %reduce-scatter.17.cloned.1.call-start = ((), (), s32[]{:S(2)}) async-start(), calls=%async_computation.17 | async-start | bytes 10485760 | tf_op jit(solution)/shard_map/reduce_scatter | solution.py:448
  1201.6 408.1 %reduce-scatter.15.cloned.1.call-start = ((), (), s32[]{:S(2)}) async-start(), calls=%async_computation.16 | async-start | bytes 10485760 | tf_op jit(solution)/shard_map/reduce_scatter | solution.py:448
  1228.4 411.5 %reduce-scatter.11.cloned.1.call-start = ((), (), s32[]{:S(2)}) async-start(), calls=%async_computation.14 | async-start | bytes 1310720 | tf_op jit(solution)/shard_map/reduce_scatter | solution.py:574
  1334.4 451.1 %reduce-scatter.13.cloned.1.call-start = ((), (), s32[]{:S(2)}) async-start(), calls=%async_computation.15 | async-start | bytes 10485760 | tf_op jit(solution)/shard_map/reduce_scatter | solution.py:448
  1433.8 207.9 %all-to-all-start.4 = ((bf16[4,64,1536]{2,1,0:T(8,128)(2,1)}), bf16[4,64,1536]{2,1,0:T(8,128)(2,1)S(1)}, u32[]{:S(2)}, u32[]{:S(2)}) async-start(bf16[4,64,1536]{2,1,0:T(8,128)(2,1)} %bitcast.301), calls=%async_computation.5 | async-start | bytes 1572864 | tf_op jit(solution)/shard_map/all_to_all | solution.py:557
  1464.4 329.9 %collective-permute-start.81 = (bf16[2,256,1024]{2,1,0:T(8,128)(2,1)}, bf16[2,256,1024]{2,1,0:T(8,128)(2,1)}, u32[]{:S(2)}, u32[]{:S(2)}) collective-permute-start(bf16[2,256,1024]{2,1,0:T(8,128)(2,1)} %constant_dynamic-slice_fusion), channel_id=1, source_target_pairs={{0,4},{4,0},{1,5},{5,1},{2,6},{6,2},{3,7},{7,3},{8,12},{12,8},{9,1... | collective-permute-start | bytes 3145736 | tf_op jit(solution)/shard_map/ppermute | solution.py:267
  1611.9 192.0 %collective-permute-start.80 = (bf16[2,256,1024]{2,1,0:T(8,128)(2,1)}, bf16[2,256,1024]{2,1,0:T(8,128)(2,1)}, u32[]{:S(2)}, u32[]{:S(2)}) collective-permute-start(bf16[2,256,1024]{2,1,0:T(8,128)(2,1)} %constant_dynamic-slice_fusion.1), channel_id=1, source_target_pairs={{0,4},{4,0},{1,5},{5,1},{2,6},{6,2},{3,7},{7,3},{8,12},{12,8},{9,1... | collective-permute-start | bytes 3145736 | tf_op jit(solution)/shard_map/ppermute | solution.py:267
  (159 other events, 4765.1 us)
Sparse Core Ops, SparseCore 0:
  35.1 101.1 all-gather.3
  139.2 75.5 all-gather.5
  1121.7 133.6 reduce-scatter.18
  1257.7 57.5 reduce-scatter.8
  1317.5 144.5 reduce-scatter.16
  1464.4 145.1 reduce-scatter.14
  1612.1 27.8 reduce-scatter.10
  1642.3 143.1 reduce-scatter.12

commit v2 on v1

v2 whole, which is shorter than its diff:
```python
from functools import partial
import math

import jax
import jax.numpy as jnp
from jax import lax
from jax.experimental import pallas as pl
from jax.experimental.pallas import tpu as pltpu
from jax.sharding import Mesh, PartitionSpec as P

HEAD_DIM = 128
EXPERTS = 16
EPS = 1e-05
F32 = jnp.float32
BF = jnp.bfloat16
VMEM_LIMIT = 60 * 1024 * 1024


def dot(a, b, dims=((1,), (0,))):
    return lax.dot_general(a, b, (dims, ((), ())), preferred_element_type=F32)


NT = ((1,), (1,))
TN = ((0,), (0,))


def masked_scores(q, k, i, j, rows, length, scale):
    s = dot(q, k, NT) * scale
    col = j * rows + lax.broadcasted_iota(jnp.int32, s.shape, 1)
    ok = col < length
    if i == j:
        row = i * rows + lax.broadcasted_iota(jnp.int32, s.shape, 0)
        ok = ok & (col <= row)
    return jnp.where(ok, s, -1e30)


def probs_of(q, key, i, rows, length, scale):
    parts = [masked_scores(q, key[j], i, j, rows, length, scale) for j in range(i + 1)]
    peak = parts[0].max(axis=1, keepdims=True)
    for s in parts[1:]:
        peak = jnp.maximum(peak, s.max(axis=1, keepdims=True))
    parts = [jnp.exp(s - peak) for s in parts]
    total = parts[0].sum(axis=1, keepdims=True)
    for e in parts[1:]:
        total = total + e.sum(axis=1, keepdims=True)
    inverse = 1.0 / total
    return [e * inverse for e in parts]


def turned(v, cosine, sine):
    return v * cosine + pltpu.roll(v, HEAD_DIM // 2, 1) * sine


def normed_turned(raw, factor, gain, cosine, sine):
    return turned(raw * factor * gain, cosine, sine).astype(BF)


def attend_kernel(inv, lens, q_ref, k_ref, v_ref, fac_ref, qg_ref, kg_ref, cos_ref, sin_ref, o_ref, key, *, first, blocks, rows, scale):
    length = lens[first + pl.program_id(0)]
    for i in range(blocks):
        at = inv[i]
        fac, cosine, sine = fac_ref[at], cos_ref[at], sin_ref[at]
        q = normed_turned(q_ref[at], fac[:, 0:1], qg_ref[...], cosine, sine)
        key[i] = normed_turned(k_ref[at], fac[:, 1:2], kg_ref[...], cosine, sine)
        probs = probs_of(q, key, i, rows, length, scale)
        out = jnp.zeros((rows, HEAD_DIM), F32)
        for j, p in enumerate(probs):
            out = out + dot(p.astype(BF), v_ref[inv[j]].astype(BF))
        o_ref[i] = out.astype(BF)


def attend_back_kernel(
    inv, lens, q_ref, k_ref, v_ref, fac_ref, qg_ref, kg_ref, cos_ref, sin_ref, do_ref,
    dq_ref, dk_ref, dv_ref, stat_ref, gain_ref, key, dk_acc, dv_acc, *, first, blocks, rows, scale
):
    length = lens[first + pl.program_id(0)]
    head = pl.program_id(1)
    dk_acc[...] = jnp.zeros_like(dk_acc)
    dv_acc[...] = jnp.zeros_like(dv_acc)

    @pl.when(head == 0)
    def _():
        stat_ref[...] = jnp.zeros_like(stat_ref)

    def unturn(at, grad, raw_ref, which, gain, out_ref):
        grad = turned(grad * scale, cos_ref[at], -sin_ref[at])
        out_ref[at] = grad
        weighted = grad * (raw_ref[at] * fac_ref[at][:, which : which + 1])
        stat_ref[at, :, which : which + 1] += jnp.sum(weighted * gain, axis=1, keepdims=True)
        return jnp.sum(weighted, axis=0, keepdims=True)

    qg, kg = qg_ref[...], kg_ref[...]
    dqg = jnp.zeros((1, HEAD_DIM), F32)
    dkg = jnp.zeros((1, HEAD_DIM), F32)
    for i in range(blocks):
        at = inv[i]
        fac, cosine, sine = fac_ref[at], cos_ref[at], sin_ref[at]
        q = normed_turned(q_ref[at], fac[:, 0:1], qg, cosine, sine)
        key[i] = normed_turned(k_ref[at], fac[:, 1:2], kg, cosine, sine)
        do = do_ref[i]
        probs = probs_of(q, key, i, rows, length, scale)
        dprobs = [dot(do, v_ref[inv[j]].astype(BF), NT) for j in range(i + 1)]
        delta = jnp.zeros((rows, 1), F32)
        for p, dp in zip(probs, dprobs):
            delta = delta + jnp.sum(p * dp, axis=1, keepdims=True)
        dq = jnp.zeros((rows, HEAD_DIM), F32)
        for j, (p, dp) in enumerate(zip(probs, dprobs)):
            ds = (p * (dp - delta)).astype(BF)
            dq = dq + dot(ds, key[j])
            dk_acc[j] += dot(ds, q, TN)
            dv_acc[j] += dot(p.astype(BF), do, TN)
        dqg = dqg + unturn(at, dq, q_ref, 0, qg, dq_ref)
    for j in range(blocks):
        at = inv[j]
        dkg = dkg + unturn(at, dk_acc[j], k_ref, 1, kg, dk_ref)
        dv_ref[at] = dv_acc[j].astype(BF)
    gain_ref[0:1, :] = dqg
    gain_ref[1:2, :] = dkg


def attention_call(lens, raw, factor, query_g, key_g, cosine, sine, first, seqs, inverse, grad=None):
    blocks, _, rows, width = raw.shape
    heads = width // (3 * HEAD_DIM)
    part = lambda k: pl.BlockSpec((blocks, None, rows, HEAD_DIM), lambda s, h, *_: (0, first + s, 0, k * heads + h))
    out = pl.BlockSpec((blocks, None, rows, HEAD_DIM), lambda s, h, *_: (0, s, 0, h))
    fac = pl.BlockSpec((blocks, None, rows, 2), lambda s, h, *_: (0, first + s, 0, 0))
    gain = pl.BlockSpec((1, HEAD_DIM), lambda s, h, *_: (0, h))
    turn = pl.BlockSpec((blocks, rows, HEAD_DIM), lambda s, h, *_: (0, 0, 0))
    ins = [raw, raw, raw, factor, query_g, key_g, cosine, sine]
    in_specs = [part(0), part(1), part(2), fac, gain, gain, turn, turn]
    one = (blocks, seqs, rows, width // 3)
    shape = jax.ShapeDtypeStruct
    scratch = [pltpu.VMEM((blocks, rows, HEAD_DIM), BF)]
    flops = 2 * 2 * (blocks * rows) ** 2 * seqs * width // 3 * 5 // 8
    if grad is None:
        kernel, outs, out_specs = attend_kernel, [shape(one, BF)], [out]
    else:
        ins, in_specs = ins + [grad], in_specs + [out]
        kernel = attend_back_kernel
        outs = [shape(one, F32), shape(one, F32), shape(one, BF)]
        outs += [shape((blocks, seqs, rows, 2), F32), shape((seqs, 2, width // 3), F32)]
        out_specs = [out] * 3 + [fac, pl.BlockSpec((None, 2, HEAD_DIM), lambda s, h, *_: (s, 0, h))]
        scratch += [pltpu.VMEM((blocks, rows, HEAD_DIM), F32)] * 2
        flops = flops * 5 // 2
    return pl.pallas_call(
        partial(kernel, first=first, blocks=blocks, rows=rows, scale=1.0 / math.sqrt(HEAD_DIM)),
        out_shape=outs,
        grid_spec=pltpu.PrefetchScalarGridSpec(
            num_scalar_prefetch=2, grid=(seqs, heads), in_specs=in_specs, out_specs=out_specs, scratch_shapes=scratch
        ),
        compiler_params=pltpu.CompilerParams(vmem_limit_bytes=VMEM_LIMIT),
        cost_estimate=pl.CostEstimate(
            flops=flops, bytes_accessed=raw.size * 6, transcendentals=(blocks * rows) ** 2 * seqs * heads * 5 // 8
        ),
    )(inverse, lens, *ins)


def pick_row(table, index):
    which = lax.broadcasted_iota(jnp.int32, table.shape, 0) == index
    return jnp.sum(jnp.where(which, table, 0.0), axis=0, keepdims=True)


def selection(rank_table, expert, cap):
    rank = pick_row(rank_table, expert)
    return lax.broadcasted_iota(jnp.int32, (cap, rank.shape[1]), 0).astype(F32) == rank


def dispatch(out, b, s, top, low, cap):
    half = top.shape[0]
    s = s.astype(F32).astype(BF)
    out[pl.ds(b * cap, cap), :] = (dot(s[:, :half], top[...]) + dot(s[:, half:], low[...])).astype(BF)


def experts_grad_kernel(base, c00, c01, c10, c11, r0, r1, wd, *rest, cap):
    og, dh = rest[-2:]
    expert = base[1] + pl.program_id(0)

    @pl.when(pl.program_id(1) == 0)
    def _():
        for b, (r, top, low) in enumerate(((r0, c00, c01), (r1, c10, c11))):
            dispatch(og, b, selection(r[...], expert, cap), top, low, cap)

    dh[...] = dot(og[...], wd[...], NT)


def experts_in_kernel(base, f00, f01, f10, f11, r0, r1, g0, g1, dhu, wg, wu, *rest, cap):
    buf, hg, dg, du, gg, weight, dots = rest[-7:]
    f = pl.program_id(1)
    expert = base[1] + pl.program_id(0)

    @pl.when(f == 0)
    def _():
        for b, (r, g, top, low) in enumerate(((r0, g0, f00, f01), (r1, g1, f10, f11))):
            s = selection(r[...], expert, cap)
            dispatch(buf, b, s, top, low, cap)
            gate = pick_row(g[...], expert)
            weight[pl.ds(b * cap, cap), :] = jnp.sum(jnp.where(s, gate, 0.0), axis=1, keepdims=True)
        dots[...] = jnp.zeros_like(dots)

    x = buf[...]
    gate = dot(x, wg[...])
    up = dot(x, wu[...])
    dh = dhu[...]
    w = weight[...]
    sg = 1.0 / (1.0 + jnp.exp(-gate))
    silu = gate * sg
    hidden = (silu * up).astype(BF).astype(F32)
    dots[...] += jnp.sum(hidden * dh, axis=1, keepdims=True)
    dh = dh * w
    hg[...] = (hidden * w).astype(BF)
    dg[...] = (dh * up * (sg * (1.0 + gate * (1.0 - sg)))).astype(BF)
    du[...] = (dh * silu).astype(BF)

    @pl.when(f == pl.num_programs(1) - 1)
    def _():
        for b, r in enumerate((r0, r1)):
            s = selection(r[...], expert, cap)
            gg[b] = jnp.sum(jnp.where(s, dots[pl.ds(b * cap, cap), :], 0.0), axis=0, keepdims=True)


def experts_call(kernel, group, groups, base, small, wide_ins, weights, wide_outs, gates, cap, local, before, flops):
    tile = 512
    width = weights[-1].shape[1] if gates else weights[-1].shape[2]
    ff = weights[-1].shape[2] if gates else weights[-1].shape[1]
    rows = 2 * cap
    tokens = small[0].shape[0] * 2
    whole = lambda a: pl.BlockSpec(a.shape, lambda e, f, s: (0, 0), pipeline_mode=pl.Buffered(1))
    wide = pl.BlockSpec((None, rows, width), lambda e, f, s: (e, group, 0))
    thin = pl.BlockSpec((None, rows, tile), lambda e, f, s: (e, group, f))
    if gates:
        heavy = pl.BlockSpec((None, width, tile), lambda e, f, s: (s[0] + e, 0, f))
    else:
        heavy = pl.BlockSpec((None, tile, width), lambda e, f, s: (s[0] + e, f, 0))
    shape = jax.ShapeDtypeStruct
    outs = [shape((local, groups * rows, width if w else ff), t) for w, t in wide_outs]
    out_specs = [wide if w else thin for w, _ in wide_outs]
    scratch = []
    if gates:
        outs.append(shape((local, 2, 1, tokens), F32))
        out_specs.append(pl.BlockSpec((None, 2, 1, tokens), lambda e, f, s: (e, 0, 0, 0)))
        scratch = [pltpu.VMEM((rows, 1), F32)] * 2
    before = [] if before is None else before
    n = 1 + len(small) + len(wide_ins) + len(weights)
    return pl.pallas_call(
        partial(kernel, cap=cap),
        out_shape=outs,
        grid_spec=pltpu.PrefetchScalarGridSpec(
            num_scalar_prefetch=1,
            grid=(local, ff // tile),
            in_specs=[whole(a) for a in small]
            + [thin] * len(wide_ins)
            + [heavy] * len(weights)
            + [pl.BlockSpec(memory_space=pl.ANY)] * len(before),
            out_specs=out_specs,
            scratch_shapes=scratch,
        ),
        input_output_aliases={n + i: i for i in range(len(before))},
        compiler_params=pltpu.CompilerParams(vmem_limit_bytes=VMEM_LIMIT),
        cost_estimate=pl.CostEstimate(
            flops=flops,
            bytes_accessed=local * (len(weights) * width * ff * 2 + rows * (2 * width + 10 * ff)) + 4 * tokens * width,
            transcendentals=local * rows * ff if gates else 0,
        ),
    )(base, *small, *wide_ins, *weights, *before)


def experts_grad(group, groups, base, cots, ranks, wd, cap, local, before):
    flops = local * 2 * cap * wd.shape[2] * (2 * wd.shape[1] + 4 * cots[0].shape[0])
    return experts_call(
        experts_grad_kernel, group, groups, base, [*cots, *ranks], [], [wd], [(True, BF), (False, F32)],
        False, cap, local, before, flops,
    )


def experts_in(group, groups, base, feats, ranks, gates, dhu, wg, wu, cap, local, before):
    flops = local * 2 * cap * wg.shape[1] * (4 * wg.shape[2] + 4 * feats[0].shape[0])
    return experts_call(
        experts_in_kernel, group, groups, base, [*feats, *ranks, *gates], [dhu], [wg, wu],
        [(True, BF), (False, BF), (False, BF), (False, BF)], True, cap, local, before, flops,
    )


def experts_out_kernel(base, *refs, cap, forward):
    if forward:
        hg, r0, r1, wd, t0, t1 = refs
        parts = [dot(hg[e], wd[e]).astype(BF) for e in range(hg.shape[0])]
    else:
        dg, du, r0, r1, wg, wu, t0, t1 = refs
        parts = [(dot(dg[e], wg[e], NT) + dot(du[e], wu[e], NT)).astype(BF) for e in range(dg.shape[0])]
    for b, (rank, final) in enumerate(((r0, t0), (r1, t1))):
        table = rank[...]
        total = None
        for e, part in enumerate(parts):
            which = lax.broadcasted_iota(jnp.int32, table.shape, 1) == base[1] + e
            column = jnp.sum(jnp.where(which, table, 0.0), axis=1, keepdims=True)
            slot = lax.broadcasted_iota(jnp.int32, (table.shape[0], cap), 1).astype(F32)
            pick = (slot == column).astype(F32).astype(BF)
            term = dot(pick, part[b * cap : (b + 1) * cap])
            total = term if total is None else total + term
        final[...] = total.astype(BF)


def experts_out(group, base, rows_in, ranks, weights, cap, local, forward):
    tokens = ranks[0].shape[0]
    width, ff = weights[0].shape[1:]
    if forward:
        ff, width = width, ff
    tile = 512
    rows = 2 * cap
    thin = pl.BlockSpec((local, rows, ff), lambda d, s: (0, group, 0))
    whole = pl.BlockSpec((tokens, EXPERTS), lambda d, s: (0, 0))
    final = pl.BlockSpec((tokens, tile), lambda d, s: (0, d))
    if forward:
        heavy = pl.BlockSpec((local, ff, tile), lambda d, s: (s[2], 0, d))
    else:
        heavy = pl.BlockSpec((local, tile, ff), lambda d, s: (s[2], d, 0))
    n = len(weights)
    return pl.pallas_call(
        partial(experts_out_kernel, cap=cap, forward=forward),
        out_shape=[jax.ShapeDtypeStruct((tokens, width), BF)] * 2,
        grid_spec=pltpu.PrefetchScalarGridSpec(
            num_scalar_prefetch=1,
            grid=(width // tile,),
            in_specs=[thin] * n + [whole] * 2 + [heavy] * n,
            out_specs=[final] * 2,
        ),
        compiler_params=pltpu.CompilerParams(vmem_limit_bytes=VMEM_LIMIT),
        cost_estimate=pl.CostEstimate(
            flops=local * rows * width * (2 * n * ff + 2 * tokens),
            bytes_accessed=local * n * (width * ff + rows * ff) * 2 + 4 * tokens * width,
            transcendentals=0,
        ),
    )(base, *rows_in, *ranks, *weights)


def shift(value, axis, by):
    n = lax.axis_size(axis)
    return lax.ppermute(value, axis, [(i, (i + by) % n) for i in range(n)])


def gather_small(value, axis):
    n, index, rows = lax.axis_size(axis), lax.axis_index(axis), value.shape[0]
    out = jnp.zeros((n * rows, *value.shape[1:]), value.dtype)
    for by in range(n):
        piece = shift(value, axis, by) if by else value
        out = lax.dynamic_update_slice_in_dim(out, piece, (index - by) % n * rows, 0)
    return out


def scatter_small(value, axis):
    n, index = lax.axis_size(axis), lax.axis_index(axis)
    value = value.reshape(n, -1, *value.shape[1:])
    part = lambda i: lax.dynamic_index_in_dim(value, i % n, 0, keepdims=False)
    total = part(index)
    for by in range(1, n):
        total = total + shift(part(index + by), axis, by)
    return total


def tie(*values):
    return lax.optimization_barrier(values)


def add_low(*terms):
    total = terms[0].astype(F32)
    for t in terms[1:]:
        total = total + t.astype(F32)
    return total.astype(BF)


def rms_parts(values):
    return values * lax.rsqrt(jnp.mean(values * values, axis=-1, keepdims=True) + EPS)


def local(
    nx,
    tokens,
    lengths,
    routes,
    w_query,
    w_key,
    w_value,
    w_out,
    w_router,
    attn_gain,
    query_gain,
    key_gain,
    ffn_gain,
    w_gate,
    w_up,
    w_down,
    cotangent,
):
    ALL, GROUP = ("r", "y", "x", "c"), ("x", "c")
    r, y, x, c = (lax.axis_index(a) for a in ALL)
    nr = lax.axis_size("r")
    me = 2 * x + c
    ng = 2 * nx
    seqs, span, width = tokens.shape
    token_count = seqs * span
    top_count = routes.shape[-1]
    cap = (token_count * top_count * 9 + 8 * EXPERTS - 1) // (8 * EXPERTS)
    cols = width // ng
    length = span * ng
    places = [(dx, dc) for dx in range(nx) for dc in range(2)]
    owner = jnp.stack([2 * ((x - dx) % nx) + (c - dc) % 2 for dx, dc in places]).astype(jnp.int32)
    inverse = jnp.stack(
        [2 * ((x - j // 2) % nx) + (c - j % 2) % 2 for j in range(ng)]
    ).astype(jnp.int32)

    w3 = jnp.stack([w_query, w_key, w_value], axis=1).reshape(-1, 3, ng, cols)
    w3 = w3.transpose(2, 0, 1, 3).reshape(ng, -1, 3 * cols)
    w3 = lax.all_to_all(w3, GROUP, split_axis=0, concat_axis=0, tiled=True)
    w3 = lax.all_gather(w3.reshape(-1, 3 * cols), ("r", "y"), axis=0, tiled=True)
    extras = jnp.concatenate(
        [w_router, attn_gain[:, None], query_gain[:, None], key_gain[:, None], ffn_gain[:, None]], axis=1
    )
    for axis in reversed(ALL):
        extras = gather_small(extras, axis)
    out_full = lax.all_gather(w_out, ALL, axis=0, tiled=True)
    router_full = extras[:, :EXPERTS]
    attn_g, query_g, key_g, ffn_g = (extras[:, EXPERTS + i].astype(F32) for i in range(4))
    query_g = lax.dynamic_slice(query_g, (me * cols,), (cols,))
    key_g = lax.dynamic_slice(key_g, (me * cols,), (cols,))

    choose = routes.reshape(token_count, top_count)
    chosen = jnp.sum(
        (choose[:, :, None] == jnp.arange(EXPERTS, dtype=jnp.int32)).astype(F32), axis=1
    )
    tri = (
        lax.broadcasted_iota(jnp.int32, (token_count, token_count), 0)
        > lax.broadcasted_iota(jnp.int32, (token_count, token_count), 1)
    ).astype(BF)
    rank = jnp.where(chosen > 0, dot(tri, chosen.astype(BF)), -1.0)

    def gather_group(value):
        pieces = []
        for dx in range(nx):
            far = shift(value, "x", dx) if dx else value
            pieces += [far, shift(far, "c", 1)]
        return pieces

    own_places = me * span + jnp.arange(span, dtype=jnp.int32)
    valid = (own_places[None, :] < lengths[:, None]).reshape(token_count)
    own_cot = jnp.where(valid[:, None], cotangent.reshape(token_count, width), jnp.zeros((), BF))
    own_tokens = tokens.astype(F32).reshape(token_count, width)

    all_tokens = jnp.stack(gather_group(tokens)).reshape(ng * token_count, width).astype(F32)
    h = token_count // 2
    cot_halves = [own_cot[:h], own_cot[h:]]
    near = [{dx: shift(v, "x", dx) if dx else v for dx in range(nx)} for v in cot_halves]
    normed_n = rms_parts(all_tokens)
    normed = (normed_n * attn_g).astype(BF)

    spots = [(dy, dx) for dy in range(2) for dx in range(nx)]

    def gather_pair(value):
        out = {(0, 0): value}
        for dx in range(1, nx):
            out[0, dx] = shift(value, "x", dx)
        for dx in range(nx):
            out[1, dx] = shift(out[0, dx], "y", 1)
        return {(dy, dx, dc): shift(v, "c", 1) if dc else v for (dy, dx), v in out.items() for dc in range(2)}

    def with_core(pieces):
        return pieces | {(dy, dx, 1): shift(v, "c", 1) for (dy, dx, _), v in pieces.items()}

    ranks_t = gather_pair(rank.T)
    ranks = {k: v.T for k, v in ranks_t.items()}
    w3, normed, ranks_t = lax.optimization_barrier((w3, normed, ranks_t))

    local_experts = w_gate.shape[0]
    mine = local_experts // 2
    base = jnp.stack([y * mine, me * local_experts + y * mine, y]).astype(jnp.int32)
    both = lambda halves, dy, dx: [halves[h][dy, dx, dc] for dc in range(2) for h in range(2)]
    pair = lambda table, dy, dx: [table[dy, dx, dc] for dc in range(2)]

    def cot_group(g, base, before):
        dy, dx = spots[g]
        return experts_grad(
            g, len(spots), base, both(cots, dy, dx), pair(ranks_t, dy, dx), w_down, cap, mine, before
        )

    def sum_group(stats):
        stats = stats.reshape(2, ng, token_count)
        stats = jnp.concatenate([lax.dynamic_slice_in_dim(stats, inverse[j], 1, 1) for j in range(ng)], 1)
        stats = lax.psum(stats, GROUP)
        stats = jnp.concatenate([lax.dynamic_slice_in_dim(stats, owner[p], 1, 1) for p in range(ng)], 1)
        return stats.reshape(2, ng * token_count)

    starts = [n[0] for n in near]
    raw = dot(normed, w3)
    squares = jnp.stack(
        [jnp.sum(raw[:, i * cols : (i + 1) * cols] ** 2, -1) for i in range(2)]
    )
    cots = [{(0, dx, 0): v for dx, v in n.items()} for n in near]
    for i in range(2):
        cots[i][1, 0, 0] = shift(starts[i], "y", 1)
    squares = sum_group(squares)
    factor = lax.rsqrt(squares / width + EPS).T

    half = HEAD_DIM // 2
    frequencies = jnp.exp(jnp.arange(half, dtype=F32) * (-2.0 * math.log(10000.0) / HEAD_DIM))
    spot = owner[:, None] * span + jnp.arange(span, dtype=jnp.int32)[None, :]
    angles = spot.astype(F32)[:, :, None] * frequencies
    cosine, sine = jnp.cos(angles), jnp.sin(angles)
    cosine = jnp.concatenate([cosine, cosine], -1)
    sine = jnp.concatenate([-sine, sine], -1)
    attention = partial(
        attention_call,
        lengths,
        raw.reshape(ng, seqs, span, -1),
        factor.reshape(ng, seqs, span, 2),
        query_g[None],
        key_g[None],
        cosine,
        sine,
    )
    for dx in range(1, nx):
        cots[0][1, dx, 0] = shift(near[0][dx], "y", 1)
        cots[1][1, dx, 0] = shift(cots[1][1, 0, 0], "x", dx)
    in_turn = [inverse, inverse]
    cots = [with_core(p) for p in cots]
    mixed = [attention(i, 1, inverse=in_turn[i])[0].reshape(ng, span, cols) for i in range(seqs)]
    mixed = [lax.all_to_all(a, GROUP, split_axis=0, concat_axis=0, tiled=True) for a in mixed]
    cot_terms = cot_group(0, base, None)
    parts = []
    for i in range(seqs):
        a = mixed[i].transpose(1, 0, 2).reshape(span, width)
        u = tokens[i].astype(F32) + dot(a, out_full)
        q = lax.rsqrt(jnp.mean(u * u, axis=-1, keepdims=True) + EPS)
        f = (u * q * ffn_g).astype(BF)
        logits = dot(f, router_full)
        weights = jnp.exp(logits - jnp.max(logits, axis=-1, keepdims=True))
        parts.append((a, u, q, f, weights / jnp.sum(weights, axis=-1, keepdims=True)))
    attended, resid, ffn_scale, ffn_in, router = (jnp.concatenate(p, axis=0) for p in zip(*parts))
    ffn_n = resid * ffn_scale

    feats = [{(0, 0, 0): p[3]} for p in parts]
    for i in range(2):
        for dx in range(1, nx):
            feats[i][0, dx, 0] = shift(feats[i][0, 0, 0], "x", dx)
        feats[i][1, 0, 0] = shift(feats[i][0, 0, 0], "y", 1)
        if i == 0:
            row = [feats[0][k] for k in feats[0]]
            row, feats[1][0, 0, 0] = tie(row, feats[1][0, 0, 0])
            feats[0] = dict(zip(feats[0], row))
    base_at, feats[1][0, 0, 0] = tie(base, feats[1][0, 0, 0])
    for g in range(1, len(spots)):
        if g == len(spots) - 1:
            row = [feats[1][k] for k in feats[1]]
            base_at, row, cot_terms = tie(base_at, row, cot_terms)
            feats[1] = dict(zip(feats[1], row))
        cot_terms = cot_group(g, base_at, cot_terms)
    for dx in range(1, nx):
        feats[0][1, dx, 0] = shift(feats[0][0, dx, 0], "y", 1)
        feats[1][1, dx, 0] = shift(feats[1][1, 0, 0], "x", dx)
    gates_t = gather_pair(router.T)

    before, gate_terms = None, {}
    base_at, cot_terms = tie(base, cot_terms)
    feats = [with_core(p) for p in feats]
    og, dhu = cot_terms
    for g, (dy, dx) in enumerate(spots):
        if g == 1:
            row = [[p[k] for k in p] for p in feats]
            base_at, row, before = tie(base_at, row, before)
            feats = [dict(zip(p, v)) for p, v in zip(feats, row)]
        *before, gg = experts_in(
            g, len(spots), base_at, both(feats, dy, dx), pair(ranks_t, dy, dx), pair(gates_t, dy, dx), dhu, w_gate, w_up,
            cap, mine, before,
        )
        gate_terms[dy, dx] = gg
    buf, hg, dg, du = before

    def weight_grad(left, right):
        return lax.dot_general(
            left, right, (((1,), (1,)), ((0,), (0,))), preferred_element_type=F32
        ).astype(BF)

    def finish_part(part):
        rows = part.shape[1] // 2
        keep = lax.dynamic_slice_in_dim(part, y * rows, rows, 1)
        give = shift(lax.dynamic_slice_in_dim(part, (1 - y) * rows, rows, 1), "y", 1)
        return keep, give

    def finish_grad(keep, give):
        first = jnp.where(y == 0, keep, give)
        second = jnp.where(y == 0, give, keep)
        return jnp.concatenate([first, second], axis=0).astype(F32)

    def over_r(value, dim):
        return lax.psum_scatter(value, "r", scatter_dimension=dim, tiled=True)

    first_full, at = tie(weight_grad(og, hg), base)
    scattered = [over_r(first_full, 1)]

    order = list(reversed(list(enumerate(spots))))
    both_ranks = lambda spot: [ranks[*spot, dc] for dc in range(2)]
    top = lambda v: v[:h]
    low = lambda v: v[h:]

    def core_sum(pair):
        return add_low(pair[0], shift(pair[1], "c", 1))

    def first_hops(acc):
        over_x = [shift(top(acc[1, dx]), "x", -dx) for dx in range(1, nx)]
        over_y = [shift(low(acc[1, dx]), "y", 1) for dx in range(1, nx)]
        return over_x, over_y

    def direct(acc):
        return [shift(top(acc[0, dx]), "x", -dx) for dx in range(1, nx)], shift(low(acc[1, 0]), "y", 1)

    def last_hops(acc, hops):
        far = shift(add_low(top(acc[1, 0]), *hops[0]), "y", 1)
        near = [shift(add_low(low(acc[0, dx]), hops[1][dx - 1]), "x", -dx) for dx in range(1, nx)]
        return far, near

    def arrived(acc, straight, last):
        total = lambda terms: sum(t.astype(F32) for t in terms)
        halves = total([top(acc[0, 0]), last[0], *straight[0]]), total([low(acc[0, 0]), straight[1], *last[1]])
        return jnp.concatenate(halves, axis=0)

    back = {}
    for i, (g, spot) in enumerate(order):
        if i >= 2:
            before_last = order[i - 2][1]
            at, back[before_last] = tie(at, back[before_last])
        terms = experts_out(g, at, [dg, du], both_ranks(spot), [w_gate, w_up], cap, mine, False)
        at, terms = tie(at, terms)
        back[spot] = core_sum(terms)
    dg, at = tie(dg, at)
    hops = first_hops(back)
    full = weight_grad(buf, dg)
    full, du, hops = tie(full, du, hops)
    straight = direct(back)
    at, straight, full, scattered[0] = tie(base, straight, full, scattered[0])
    scattered.append(over_r(full, 1))
    mix = {}

    def mix_group(i, at):
        g, spot = order[i]
        mix[spot] = experts_out(g, at, [hg], both_ranks(spot), [w_down], cap, mine, True)
        at, mix[spot] = tie(at, mix[spot])
        return at

    last = last_hops(back, hops)
    for i in range(len(order)):
        if i == len(order) // 2:
            at, last = tie(at, last)
        at = mix_group(i, at)
    dffn = arrived(back, straight, last)

    def swap_y(part):
        keep = lax.dynamic_index_in_dim(part, y, 1, keepdims=False)
        give = lax.dynamic_index_in_dim(part, 1 - y, 1, keepdims=False)
        return keep, shift(give, "y", 1)

    terms = jnp.stack([gate_terms[k] for k in spots])
    terms = terms.reshape(2, nx, mine, 2, token_count)
    pieces = []
    for k in range(2 * ng):
        ty, tx, tc = k // ng, (k % ng) // 2, k % 2
        piece = lax.dynamic_slice(
            terms, ((y - ty) % 2, (x - tx) % nx, 0, (c - tc) % 2, 0), (1, 1, mine, 1, token_count)
        )
        pieces.append(piece.reshape(mine, token_count))
    terms = lax.all_to_all(jnp.stack(pieces), ("y", "x", "c"), split_axis=0, concat_axis=0, tiled=True)
    drouter = terms.reshape(2, ng, mine, token_count).transpose(1, 0, 2, 3).reshape(EXPERTS, token_count).T

    dlogits = router * (drouter - jnp.sum(router * drouter, axis=-1, keepdims=True))
    highest = lax.Precision.HIGHEST
    grad_router = lax.dot_general(ffn_in.astype(F32), dlogits, (((0,), (0,)), ((), ())), precision=highest)
    dffn = dffn + lax.dot_general(
        dlogits, router_full.astype(F32), (((1,), (1,)), ((), ())), precision=highest
    )
    grad_ffn_g = jnp.sum(dffn * ffn_n, axis=0)
    gd = dffn * ffn_g
    dresid = own_cot.astype(F32) + ffn_scale * (gd - ffn_n * jnp.mean(gd * ffn_n, axis=-1, keepdims=True))

    dattn, mix = tie(dresid.astype(BF), mix)
    mix = {k: core_sum(v) for k, v in mix.items()}
    dattended = dot(dattn, out_full, NT).astype(BF)
    dattended = dattended.reshape(token_count, ng, cols).transpose(1, 0, 2).reshape(ng, seqs, span, cols)
    du, dattended = tie(du, dattended)
    dattended = lax.all_to_all(dattended, GROUP, split_axis=0, concat_axis=0, tiled=True)
    full = weight_grad(buf, du)
    grad_out = dot(attended, dattn, TN).astype(BF)
    wrows = w_out.shape[0]
    go = grad_out.reshape(nr * 2, nx, 2, wrows, width)
    keep = lax.dynamic_index_in_dim(go, c, 2, keepdims=False)
    give = lax.dynamic_index_in_dim(go, 1 - c, 2, keepdims=False)
    go = add_low(keep, shift(give, "c", 1))
    parted = [finish_part(scattered[0])]
    hops, straight = first_hops(mix), direct(mix)
    dattended, go, full, scattered[1], hops, straight = tie(dattended, go, full, scattered[1], hops, straight)
    last = last_hops(mix, hops)
    scattered.append(over_r(full, 1))
    dquery, dkey, dvalue, means, gain_grads = attention(0, seqs, inverse, dattended)

    go = add_low(
        *[
            shift(lax.dynamic_index_in_dim(go, (x + dx) % nx, 1, keepdims=False), "x", dx)
            if dx
            else lax.dynamic_index_in_dim(go, x, 1, keepdims=False)
            for dx in range(nx)
        ]
    )
    parted.append(finish_part(scattered[1]))
    dvalue, means, go, parted, last = tie(dvalue.reshape(-1, cols), means, go, parted, last)
    output = (resid + arrived(mix, straight, last)).astype(BF).reshape(seqs, span, width)
    g_value, means = tie(dot(normed, dvalue, TN).astype(BF), means)
    thirds = [swap_y(g_value.reshape(nr, 2, -1, cols))]
    means = sum_group(means.reshape(-1, 2).T).T / width
    gain_grads = gain_grads.sum(axis=0)
    grad_query_g, grad_key_g = gain_grads[0], gain_grads[1]

    def raw_grad(grad, i, gain):
        n = raw[:, i * cols : (i + 1) * cols] * factor[:, i : i + 1]
        return (factor[:, i : i + 1] * (grad.reshape(-1, cols) * gain - n * means[:, i : i + 1])).astype(BF)

    draws = [raw_grad(dquery, 0, query_g), raw_grad(dkey, 1, key_g), dvalue]
    g_pair = dot(normed, jnp.concatenate(draws[:2], axis=1), TN).astype(BF)
    g_pair, thirds[0], go = tie(g_pair, thirds[0], go)
    thirds.append(swap_y(g_pair.reshape(nr, 2, -1, 2 * cols)))
    draw = jnp.concatenate(draws, axis=1)
    dnormed = dot(draw, w3, NT)
    grad_attn_g = jnp.sum(dnormed * normed_n, axis=0)
    thirds[0] = add_low(*thirds[0])
    dnormed, thirds[1], go = tie(dnormed.astype(BF), thirds[1], go)
    go = add_low(*swap_y(go.reshape(nr, 2, wrows, width)))
    thirds[1], grad_attn_g = tie(add_low(*thirds[1]), grad_attn_g)
    dnormed = dnormed.reshape(nx, 2, token_count, width)
    dnormed = [add_low(dnormed[dx, 0], shift(dnormed[dx, 1], "c", 1)) for dx in range(nx)]
    dnormed = sum(
        (shift(dnormed[dx], "x", -dx) if dx else dnormed[0]).astype(F32) for dx in range(nx)
    )
    own_scale = lax.rsqrt(jnp.mean(own_tokens * own_tokens, axis=-1, keepdims=True) + EPS)
    own_n = own_tokens * own_scale
    gd = dnormed * attn_g
    grad_input = dresid + own_scale * (gd - own_n * jnp.mean(gd * own_n, axis=-1, keepdims=True))
    grad_input = grad_input.reshape(seqs, span, width)

    spread = lambda v: lax.dynamic_update_slice(jnp.zeros((width,), F32), v, (me * cols,))
    sums = jnp.concatenate(
        [
            grad_router,
            grad_attn_g[:, None],
            spread(grad_query_g)[:, None],
            spread(grad_key_g)[:, None],
            grad_ffn_g[:, None],
        ],
        axis=1,
    )
    for axis in ALL:
        sums = scatter_small(sums, axis)
    thirds[0], scattered[2] = tie(thirds[0], scattered[2])
    parted.append(finish_part(scattered[2]))
    g_value = over_r(thirds[0], 0)
    g_value, thirds[1] = tie(g_value, thirds[1])
    g_pair = over_r(thirds[1], 0)
    g_pair, go = tie(g_pair, go)
    go = over_r(go, 0)
    g_pair = g_pair.reshape(ng, wrows, 2, cols)
    g_value = g_value.reshape(ng, wrows, 1, cols)
    go = go.reshape(wrows, width).astype(F32)
    g3 = jnp.concatenate([g_pair, g_value], axis=2).transpose(2, 0, 1, 3)
    g3 = lax.all_to_all(g3, GROUP, split_axis=1, concat_axis=1, tiled=True)
    g3 = g3.transpose(0, 2, 1, 3).reshape(3, wrows, width).astype(F32)
    grad_down, grad_gate, grad_up = (finish_grad(*p) for p in parted)
    grad_down = grad_down.transpose(0, 2, 1)

    return (
        output,
        grad_input,
        g3[0],
        g3[1],
        g3[2],
        go,
        sums[:, :EXPERTS],
        sums[:, EXPERTS],
        sums[:, EXPERTS + 1],
        sums[:, EXPERTS + 2],
        sums[:, EXPERTS + 3],
        grad_gate,
        grad_up,
        grad_down,
    )


def solution(mesh):
    ndp, nex = mesh.shape["dp"], mesh.shape["expert"]
    nx = nex // 2
    fine = Mesh(mesh.devices.reshape(ndp // 2, 2, nx, 2), ("r", "y", "x", "c"))
    dp, ex = ("r", "y"), ("x", "c")
    both = dp + ex
    placed = (
        P(dp, ex, None),
        P(dp),
        P(dp, ex, None, None),
        P(both, None),
        P(both, None),
        P(both, None),
        P(both, None),
        P(both, None),
        P(both),
        P(both),
        P(both),
        P(both),
        P(ex, None, None),
        P(ex, None, None),
        P(ex, None, None),
        P(dp, ex, None),
    )
    return jax.shard_map(
        partial(local, nx),
        mesh=fine,
        in_specs=placed,
        out_specs=(
            P(dp, ex, None),
            P(dp, ex, None),
            P(both, None),
            P(both, None),
            P(both, None),
            P(both, None),
            P(both, None),
            P(both),
            P(both),
            P(both),
            P(both),
            P(ex, dp, None),
            P(ex, dp, None),
            P(ex, None, dp),
        ),
        check_vma=False,
    )
```

time: 1830 us -> 1190 us (0.65)
  waiting for transfers between devices: 831 us -> 265 us
  blocking collectives: 120 us -> 40.1 us
  local copies, waits for them, and re-layouts: 147 us -> 94.3 us
  Pallas kernels: 339 us -> 375 us
  starting transfers between devices: 70 us -> 92.5 us
    reduce_scatter x5 -> x6, waiting for transfers between devices: 337 us -> 9.7 us  [over_r(): return lax.psum_scatter(value, 'r', scatter_dimension=dim, tiled=True)]
    ppermute x82 -> x88, waiting for transfers between devices: 468 us -> 237 us  [shift(): return lax.ppermute(value, axis, [(i, (i + by) % n) for i in range(n)])]
    all_gather x1 -> x0, blocking collectives: 82.8 us -> none  [local(): extras = lax.all_gather(extras, ALL, axis=0, tiled=True)]
    pallas_call x10 -> x19, Pallas kernels: 339 us -> 375 us  [the longest x8 149 us: experts_call(): pl.pallas_call(partial(kernel, cap=cap), out_shape=outs, grid_spec=pltpu....]
    slice x14 -> x10, local copies, waits for them, and re-layouts: 40.1 us -> 9.48 us  [the longest x4 5.27 us: local(): low = lambda v: v[h:]]
    mul x4 -> x0, other arithmetic: 25.2 us -> none  [the longest x3 19.2 us: turn(): return (v * cosine + sign * swapped * sine).reshape(ng * token_count, cols)]
    all_to_all x1, waiting for transfers between devices: 24.8 us -> 0.01 us  [local(): lax.all_to_all(dattended, GROUP, split_axis=0, concat_axis=0, tiled=True)]
    convert_element_type x17 -> x18, other arithmetic: 33.9 us -> 58.1 us  [add_low(): return total.astype(BF)]
  transfers between devices with their start and end apart: 94 -> 101, of which waited for: 35 -> 25; matrix products, arithmetic and copies ran while one was open for 18% -> 29% of each run, Pallas kernels for 17% -> 30%
where the time goes in v2:
time: 1190 us
  Pallas kernels  375 us (32%)
  waiting for transfers between devices  265 us (22%)
  matrix products  164 us (14%)
  other arithmetic  138 us (12%)
  local copies, waits for them, and re-layouts  94.3 us (8%)
  starting transfers between devices  92.5 us (8%)
  blocking collectives  40.1 us (3%)
  between operations  17 us (1%)
    ppermute x88, waiting for transfers between devices, shift(): return lax.ppermute(value, axis, [(i, (i + by) % n) for i in range(n)])  237 us
    pallas_call x8, Pallas kernels, experts_call(): pl.pallas_call(partial(kernel, cap=cap), out_shape=outs, grid_spec=pltpu....  149 us
    pallas_call x8, Pallas kernels, experts_out(): pl.pallas_call(partial(experts_out_kernel, cap=cap, forward=forward), out...  139 us
    pallas_call x3, Pallas kernels, attention_call(): pl.pallas_call(partial(kernel, first=first, blocks=blocks, rows=rows, sca...  86.4 us
    dot_general x11, matrix products, dot(): return lax.dot_general(a, b, (dims, ((), ())), preferred_element_type=F32)  79.9 us
    dot_general x3, matrix products, weight_grad(): lax.dot_general(left, right, (((1,), (1,)), ((0,), (0,))), preferred_elem...  78.4 us
    ppermute x88, starting transfers between devices, shift(): return lax.ppermute(value, axis, [(i, (i + by) % n) for i in range(n)])  71 us
    convert_element_type x18, other arithmetic, add_low(): return total.astype(BF)  58.1 us
  transfers between devices with their start and end apart: 101, of which 25 were waited for; matrix products, arithmetic and copies ran while one was open for 29% of the time, Pallas kernels for 30%

profile of v2, /device:TPU:0, one launch (start us, length us, event | category | flops | bytes accessed | tf_op | source)
XLA Modules:
  0.0 1185.3 jit_solution(6538873668562658039)
XLA Ops:
  18.5 16.5 %all_to_all.30 = bf16[4,64,1536]{2,1,0:T(8,128)(2,1)} all-to-all(bf16[4,64,1536]{2,1,0:T(8,128)(2,1)} %reshape.380), channel_id=1, replica_groups=mesh['r'=4,'y'=2,'x'=2,'c'=2] {'x','c'}, dimensions={0} | all-to-all | bytes 1572864 | tf_op jit(solution)/shard_map/all_to_all | solution.py:413
  41.6 42.9 %collective-permute-done.1 = bf16[2,256,2048]{2,1,0:T(8,128)(2,1)} collective-permute-done((bf16[2,256,2048]{2,1,0:T(8,128)(2,1)S(1)}, bf16[2,256,2048]{2,1,0:T(8,128)(2,1)}, u32[]{:S(2)}, u32[]{:S(2)}) %collective-permute-start.1) | collective-permute-done | bytes 2097184 | tf_op jit(solution)/shard_map/ppermute | solution.py:338
  135.7 17.4 %fusion.71 = f32[2048,1536]{1,0:T(8,128)S(1)} fusion(bf16[2048,2048]{1,0:T(8,128)(2,1)} %multiply_convert_fusion, bf16[2048,1536]{1,0:T(8,128)(2,1)} %all-gather.3.cloned.1.call-done), kind=kOutput, calls=%fused_computation.268 | convolution fusion | flops 12884901888 | bytes 27262976 | tf_op jit(solution)/shard_map/dot_general | solution.py:20
  172.3 15.6 %shard_map.263 = bf16[4,1,256,512]{3,2,1,0:T(8,128)(2,1)} custom-call(s32[4]{0:T(128)} %get-tuple-element.473.inv, s32[2]{0:T(128)} %lens.5, f32[4,2,256,1536]{3,2,1,0:T(8,128)} %bitcast.299, f32[4,2,256,1536]{3,2,1,0:T(8,128)} %bitcast.300, f32[4,2,256,1536]{3,2,1,0:T(8,128)} %bitcast.301, f32[4,2,256,2]{3,2,1,0:T(8,128)} %bitcast.315, f32[1,512]{1,0:T(1,128)} %bitcast.373, ...), custom_call_target="tpu_custom_call" | custom-call | flops 1342177280 | bytes 18874368 | tf_op jit(solution)/shard_map/pallas_call | solution.py:145
  191.6 15.5 %shard_map.264 = bf16[4,1,256,512]{3,2,1,0:T(8,128)(2,1)} custom-call(s32[4]{0:T(128)} %get-tuple-element.473.inv, s32[2]{0:T(128)} %lens.5, f32[4,2,256,1536]{3,2,1,0:T(8,128)} %bitcast.302, f32[4,2,256,1536]{3,2,1,0:T(8,128)} %bitcast.303, f32[4,2,256,1536]{3,2,1,0:T(8,128)} %bitcast.304, f32[4,2,256,2]{3,2,1,0:T(8,128)} %bitcast.316, f32[1,512]{1,0:T(1,128)} %bitcast.374, ...), custom_call_target="tpu_custom_call" | custom-call | flops 1342177280 | bytes 18874368 | tf_op jit(solution)/shard_map/pallas_call | solution.py:145
  257.7 20.0 %collective-permute-done.25.c01 = bf16[256,2048]{1,0:T(8,128)(2,1)} collective-permute-done((bf16[256,2048]{1,0:T(8,128)(2,1)}, bf16[256,2048]{1,0:T(8,128)(2,1)}, u32[]{:S(2)}, u32[]{:S(2)}) %collective-permute-start.25) | collective-permute-done | bytes 1048608 | tf_op jit(solution)/shard_map/ppermute | solution.py:338
  283.1 14.1 %shard_map.265 = (bf16[2,2304,2048]{2,1,0:T(8,128)(2,1)}, f32[2,2304,1024]{2,1,0:T(8,128)}) custom-call(s32[3]{0:T(128)} %pad_add_fusion.1.base, bf16[256,2048]{1,0:T(8,128)(2,1)} %get-tuple-element.505.c00, bf16[256,2048]{1,0:T(8,128)(2,1)} %get-tuple-element.504.c01, bf16[256,2048]{1,0:T(8,128)(2,1)} %collective-permute-done.28.c10, ...), custom_call_target="tpu_custom_call" | custom-call | flops 7247757312 | bytes 29097984 | tf_op jit(solution)/shard_map/pallas_call | solution.py:244
  332.0 14.1 %shard_map.266 = (bf16[2,2304,2048]{2,1,0:T(8,128)(2,1)}, f32[2,2304,1024]{2,1,0:T(8,128)}) custom-call(s32[3]{0:T(128)} %pad_add_fusion.1.base, bf16[256,2048]{1,0:T(8,128)(2,1)} %collective-permute-done.24.c00, bf16[256,2048]{1,0:T(8,128)(2,1)} %collective-permute-done.25.c01, ...), custom_call_target="tpu_custom_call", output_to_operand_aliasing={{0}: (8, {}), {1}: (9, {})} | custom-call | flops 7247757312 | bytes 29097984 | tf_op jit(solution)/shard_map/pallas_call | solution.py:244
  353.6 14.4 %shard_map.267 = (bf16[2,2304,2048]{2,1,0:T(8,128)(2,1)}, f32[2,2304,1024]{2,1,0:T(8,128)}) custom-call(s32[3]{0:T(128)} %pad_add_fusion.1.base, bf16[256,2048]{1,0:T(8,128)(2,1)} %collective-permute-done.20.c00, bf16[256,2048]{1,0:T(8,128)(2,1)} %collective-permute-done.21.c01, ...), custom_call_target="tpu_custom_call", output_to_operand_aliasing={{0}: (8, {}), {1}: (9, {})} | custom-call | flops 7247757312 | bytes 29097984 | tf_op jit(solution)/shard_map/pallas_call | solution.py:244
  373.4 14.1 %shard_map.268 = (bf16[2,2304,2048]{2,1,0:T(8,128)(2,1)}, f32[2,2304,1024]{2,1,0:T(8,128)}) custom-call(s32[3]{0:T(128)} %pad_add_fusion.1.base, bf16[256,2048]{1,0:T(8,128)(2,1)} %collective-permute-done.30.c00, bf16[256,2048]{1,0:T(8,128)(2,1)} %collective-permute-done.31.c01, ...), custom_call_target="tpu_custom_call", output_to_operand_aliasing={{0}: (8, {}), {1}: (9, {})} | custom-call | flops 7247757312 | bytes 29097984 | tf_op jit(solution)/shard_map/pallas_call | solution.py:244
  395.0 23.0 %shard_map.269 = (bf16[2,2304,2048]{2,1,0:T(8,128)(2,1)}, bf16[2,2304,1024]{2,1,0:T(8,128)(2,1)}, bf16[2,2304,1024]{2,1,0:T(8,128)(2,1)}, bf16[2,2304,1024]{2,1,0:T(8,128)(2,1)}, f32[2,2,1,512]{3,2,1,0:T(1,128)}) custom-call(s32[3]{0:T(128)} %pad_add_fusion.1.base, bf16[256,2048]{1,0:T(8,128)(2,1)} %copy-done.11, bf16[256,2048]{1,0:T(8,128)(2,1)} %copy-done.9, ...), custom_call_target="tpu_custom_call" | custom-call | flops 12079595520 | bytes 37486592 | tf_op jit(solution)/shard_map/pallas_call | solution.py:244
  419.5 23.4 %shard_map.270 = (bf16[2,2304,2048]{2,1,0:T(8,128)(2,1)}, bf16[2,2304,1024]{2,1,0:T(8,128)(2,1)}, bf16[2,2304,1024]{2,1,0:T(8,128)(2,1)}, bf16[2,2304,1024]{2,1,0:T(8,128)(2,1)}, f32[2,2,1,512]{3,2,1,0:T(1,128)}) custom-call(s32[3]{0:T(128)} %pad_add_fusion.1.base, ...), custom_call_target="tpu_custom_call", output_to_operand_aliasing={{0}: (12, {}), {1}: (13, {}), {2}: (14, {}), {3}: (15, {})} | custom-call | flops 12079595520 | bytes 37486592 | tf_op jit(solution)/shard_map/pallas_call | solution.py:244
  443.5 23.1 %shard_map.271 = (bf16[2,2304,2048]{2,1,0:T(8,128)(2,1)}, bf16[2,2304,1024]{2,1,0:T(8,128)(2,1)}, bf16[2,2304,1024]{2,1,0:T(8,128)(2,1)}, bf16[2,2304,1024]{2,1,0:T(8,128)(2,1)}, f32[2,2,1,512]{3,2,1,0:T(1,128)}) custom-call(s32[3]{0:T(128)} %pad_add_fusion.1.base, ...), custom_call_target="tpu_custom_call", output_to_operand_aliasing={{0}: (12, {}), {1}: (13, {}), {2}: (14, {}), {3}: (15, {})} | custom-call | flops 12079595520 | bytes 37486592 | tf_op jit(solution)/shard_map/pallas_call | solution.py:244
  467.3 23.0 %shard_map.272 = (bf16[2,2304,2048]{2,1,0:T(8,128)(2,1)}, bf16[2,2304,1024]{2,1,0:T(8,128)(2,1)}, bf16[2,2304,1024]{2,1,0:T(8,128)(2,1)}, bf16[2,2304,1024]{2,1,0:T(8,128)(2,1)}, f32[2,2,1,512]{3,2,1,0:T(1,128)}) custom-call(s32[3]{0:T(128)} %pad_add_fusion.1.base, ...), custom_call_target="tpu_custom_call", output_to_operand_aliasing={{0}: (12, {}), {1}: (13, {}), {2}: (14, {}), {3}: (15, {})} | custom-call | flops 12079595520 | bytes 37486592 | tf_op jit(solution)/shard_map/pallas_call | solution.py:244
  490.2 26.8 %convolution_convert_fusion.3 = bf16[2,2048,1024]{2,1,0:T(8,128)(2,1)} fusion(bf16[2,2304,2048]{2,1,0:T(8,128)(2,1)} %get-tuple-element.215, bf16[2,2304,1024]{2,1,0:T(8,128)(2,1)} %get-tuple-element.253.refs_0_), kind=kOutput, calls=%fused_computation.16 | convolution fusion | flops 19331547136 | bytes 36700160 | tf_op jit(solution)/shard_map/dot_general | solution.py:577
  517.2 20.6 %shard_map.273 = (bf16[512,2048]{1,0:T(8,128)(2,1)}, bf16[512,2048]{1,0:T(8,128)(2,1)}) custom-call(s32[3]{0:T(128)} %pad_add_fusion.1.base, bf16[2,2304,1024]{2,1,0:T(8,128)(2,1)} %get-tuple-element.255.refs_0_, bf16[2,2304,1024]{2,1,0:T(8,128)(2,1)} %get-tuple-element.319.refs_1_, f32[512,16]{1,0:T(8,128)} %bitcast.351, ...), custom_call_target="tpu_custom_call" | custom-call | flops 12079595520 | bytes 25690112 | tf_op jit(solution)/shard_map/pallas_call | solution.py:318
  538.2 20.5 %shard_map.274 = (bf16[512,2048]{1,0:T(8,128)(2,1)}, bf16[512,2048]{1,0:T(8,128)(2,1)}) custom-call(s32[3]{0:T(128)} %pad_add_fusion.1.base, bf16[2,2304,1024]{2,1,0:T(8,128)(2,1)} %get-tuple-element.255.refs_0_, bf16[2,2304,1024]{2,1,0:T(8,128)(2,1)} %get-tuple-element.319.refs_1_, f32[512,16]{1,0:T(8,128)} %bitcast.347, f32[512,16]{1,0:T(8,128)} %bitcast.355, ...), custom_call_target="tpu_custom_call" | custom-call | flops 12079595520 | bytes 25690112 | tf_op jit(solution)/shard_map/pallas_call | solution.py:318
  558.7 26.9 %convolution_convert_fusion.2 = bf16[2,2048,1024]{2,1,0:T(8,128)(2,1)} fusion(bf16[2,2304,2048]{2,1,0:T(8,128)(2,1)} %get-tuple-element.279, bf16[2,2304,1024]{2,1,0:T(8,128)(2,1)} %get-tuple-element.255.refs_0_), kind=kOutput, calls=%fused_computation.15 | convolution fusion | flops 19331547136 | bytes 36700160 | tf_op jit(solution)/shard_map/dot_general | solution.py:577
  588.8 20.7 %shard_map.275 = (bf16[512,2048]{1,0:T(8,128)(2,1)}, bf16[512,2048]{1,0:T(8,128)(2,1)}) custom-call(s32[3]{0:T(128)} %pad_add_fusion.1.base, bf16[2,2304,1024]{2,1,0:T(8,128)(2,1)} %get-tuple-element.255.refs_0_, bf16[2,2304,1024]{2,1,0:T(8,128)(2,1)} %get-tuple-element.319.refs_1_, f32[512,16]{1,0:T(8,128)} %bitcast.345, f32[512,16]{1,0:T(8,128)} %bitcast.353, ...), custom_call_target="tpu_custom_call" | custom-call | flops 12079595520 | bytes 25690112 | tf_op jit(solution)/shard_map/pallas_call | solution.py:318
  624.8 20.5 %shard_map.276 = (bf16[512,2048]{1,0:T(8,128)(2,1)}, bf16[512,2048]{1,0:T(8,128)(2,1)}) custom-call(s32[3]{0:T(128)} %pad_add_fusion.1.base, bf16[2,2304,1024]{2,1,0:T(8,128)(2,1)} %get-tuple-element.255.refs_0_, bf16[2,2304,1024]{2,1,0:T(8,128)(2,1)} %get-tuple-element.319.refs_1_, f32[512,16]{1,0:T(8,128)} %copy-done.47, f32[512,16]{1,0:T(8,128)} %bitcast.349, ...), custom_call_target="tpu_custom_call" | custom-call | flops 12079595520 | bytes 25690112 | tf_op jit(solution)/shard_map/pallas_call | solution.py:318
  647.2 15.9 %collective-permute-done.56 = bf16[256,2048]{1,0:T(8,128)(2,1)S(1)} collective-permute-done((bf16[256,2048]{1,0:T(8,128)(2,1)}, bf16[256,2048]{1,0:T(8,128)(2,1)S(1)}, u32[]{:S(2)}, u32[]{:S(2)}) %collective-permute-start.56) | collective-permute-done | bytes 1048608 | tf_op jit(solution)/shard_map/ppermute | solution.py:338
  681.8 14.2 %shard_map.277 = (bf16[512,2048]{1,0:T(8,128)(2,1)}, bf16[512,2048]{1,0:T(8,128)(2,1)}) custom-call(s32[3]{0:T(128)} %pad_add_fusion.1.base, bf16[2,2304,1024]{2,1,0:T(8,128)(2,1)} %get-tuple-element.253.refs_0_, f32[512,16]{1,0:T(8,128)} %bitcast.352, f32[512,16]{1,0:T(8,128)} %bitcast.41.refs_3_.refs_2_, bf16[4,1024,2048]{2,1,0:T(8,128)(2,1)} %refs_3_.7), custom_call_target="tpu_custom_call" | custom-call | flops 7247757312 | bytes 14942208 | tf_op jit(solution)/shard_map/pallas_call | solution.py:318
  695.9 14.2 %shard_map.278 = (bf16[512,2048]{1,0:T(8,128)(2,1)}, bf16[512,2048]{1,0:T(8,128)(2,1)}) custom-call(s32[3]{0:T(128)} %pad_add_fusion.1.base, bf16[2,2304,1024]{2,1,0:T(8,128)(2,1)} %get-tuple-element.253.refs_0_, f32[512,16]{1,0:T(8,128)} %bitcast.348, f32[512,16]{1,0:T(8,128)} %bitcast.356, bf16[4,1024,2048]{2,1,0:T(8,128)(2,1)} %refs_3_.7), custom_call_target="tpu_custom_call" | custom-call | flops 7247757312 | bytes 14942208 | tf_op jit(solution)/shard_map/pallas_call | solution.py:318
  710.1 14.2 %shard_map.279 = (bf16[512,2048]{1,0:T(8,128)(2,1)}, bf16[512,2048]{1,0:T(8,128)(2,1)}) custom-call(s32[3]{0:T(128)} %pad_add_fusion.1.base, bf16[2,2304,1024]{2,1,0:T(8,128)(2,1)} %get-tuple-element.253.refs_0_, f32[512,16]{1,0:T(8,128)} %bitcast.346, f32[512,16]{1,0:T(8,128)} %bitcast.354, bf16[4,1024,2048]{2,1,0:T(8,128)(2,1)} %refs_3_.7), custom_call_target="tpu_custom_call" | custom-call | flops 7247757312 | bytes 14942208 | tf_op jit(solution)/shard_map/pallas_call | solution.py:318
  724.3 14.6 %shard_map.280 = (bf16[512,2048]{1,0:T(8,128)(2,1)}, bf16[512,2048]{1,0:T(8,128)(2,1)}) custom-call(s32[3]{0:T(128)} %pad_add_fusion.1.base, bf16[2,2304,1024]{2,1,0:T(8,128)(2,1)} %get-tuple-element.253.refs_0_, f32[512,16]{1,0:T(8,128)} %copy-done.47, f32[512,16]{1,0:T(8,128)} %bitcast.350, bf16[4,1024,2048]{2,1,0:T(8,128)(2,1)} %refs_3_.7), custom_call_target="tpu_custom_call" | custom-call | flops 7247757312 | bytes 14942208 | tf_op jit(solution)/shard_map/pallas_call | solution.py:318
  787.5 24.8 %convolution_convert_fusion.1 = bf16[2,2048,1024]{2,1,0:T(8,128)(2,1)} fusion(bf16[2,2304,2048]{2,1,0:T(8,128)(2,1)} %get-tuple-element.279, bf16[2,2304,1024]{2,1,0:T(8,128)(2,1)S(1)} %bitcast.309), kind=kOutput, calls=%fused_computation.14 | convolution fusion | flops 19331547136 | bytes 36700160 | tf_op jit(solution)/shard_map/dot_general | solution.py:577
  820.6 22.0 %collective-permute-done.64 = bf16[256,2048]{1,0:T(8,128)(2,1)} collective-permute-done((bf16[256,2048]{1,0:T(8,128)(2,1)}, bf16[256,2048]{1,0:T(8,128)(2,1)}, u32[]{:S(2)}, u32[]{:S(2)}) %collective-permute-start.64) | collective-permute-done | bytes 1048608 | tf_op jit(solution)/shard_map/ppermute | solution.py:338
  868.1 55.2 %shard_map.281 = (f32[4,2,256,512]{3,2,1,0:T(8,128)}, f32[4,2,256,512]{3,2,1,0:T(8,128)}, bf16[4,2,256,512]{3,2,1,0:T(8,128)(2,1)}, f32[4,2,256,2]{3,2,1,0:T(8,128)}, f32[2,2,512]{2,1,0:T(2,128)}) custom-call(s32[4]{0:T(128)} %get-tuple-element.473.inv, s32[2]{0:T(128)} %lens.5, f32[4,2,256,1536]{3,2,1,0:T(8,128)} %bitcast.305, ...), custom_call_target="tpu_custom_call" | custom-call | flops 6710886400 | bytes 18874368 | tf_op jit(solution)/shard_map/pallas_call | solution.py:145
  964.7 13.1 %fusion.21 = bf16[2048,1024]{1,0:T(8,128)(2,1)S(1)} fusion(bf16[2048,2048]{1,0:T(8,128)(2,1)} %multiply_convert_fusion, bf16[2048,512]{1,0:T(8,128)(2,1)S(1)} %get-tuple-element.477, bf16[2048,512]{1,0:T(8,128)(2,1)S(1)} %get-tuple-element.476), kind=kOutput, calls=%fused_computation.61 | convolution fusion | flops 8600420352 | bytes 16777216 | tf_op jit(solution)/shard_map/dot_general | solution.py:20
  987.6 20.9 %multiply_reduce_fusion = (f32[2048]{0:T(1024)S(1)}, bf16[2048,2048]{1,0:T(8,128)(2,1)}) fusion(f32[2048]{0:T(1024)S(1)} %bitcast.385, bf16[1,2,256,2048]{3,2,1,0:T(8,128)(2,1)} %bitcast.10, bf16[1,2,256,2048]{3,2,1,0:T(8,128)(2,1)} %bitcast.9, bf16[1,2,256,2048]{3,2,1,0:T(8,128)(2,1)} %bitcast.8, bf16[1,2,256,2048]{3,2,1,0:T(8,128)(2,1)S(1)} %bitcast.312, ...), kind=kOutput, calls=%fused_computation.1 | convolution fusion | flops 12937328640 | bytes 29376512 | tf_op jit(solution)/shard_map/dot_general | solution.py:20
  1011.1 20.9 %collective-permute-done.76 = bf16[4,256,1024]{2,1,0:T(8,128)(2,1)} collective-permute-done((bf16[4,256,1024]{2,1,0:T(8,128)(2,1)}, bf16[4,256,1024]{2,1,0:T(8,128)(2,1)}, u32[]{:S(2)}, u32[]{:S(2)}) %collective-permute-start.76) | collective-permute-done | bytes 2097184 | tf_op jit(solution)/shard_map/ppermute | solution.py:338
  1083.2 40.2 %collective-permute-done.85 = f32[128,20]{0,1:T(8,128)S(1)} collective-permute-done((f32[128,20]{0,1:T(8,128)S(1)}, f32[128,20]{0,1:T(8,128)S(1)}, u32[]{:S(2)}, u32[]{:S(2)}) %collective-permute-start.85) | collective-permute-done | bytes 10272 | tf_op jit(solution)/shard_map/ppermute | solution.py:338
  (634 shorter events, 485.2 us)
Async XLA Ops:
  7.2 128.5 %all-gather.3.cloned.1.call-start = ((), (), s32[]{:S(2)}) async-start(), calls=%async_computation.12 | async-start | bytes 7077888 | tf_op jit(solution)/shard_map/all_gather | solution.py:414
  35.0 200.4 %all-gather.5.cloned.1.call-start = ((), (), s32[]{:S(2)}) async-start(), calls=%async_computation.13 | async-start | bytes 8650752 | tf_op jit(solution)/shard_map/all_gather | solution.py:420
  35.8 48.7 %collective-permute-start.1 = (bf16[2,256,2048]{2,1,0:T(8,128)(2,1)S(1)}, bf16[2,256,2048]{2,1,0:T(8,128)(2,1)}, u32[]{:S(2)}, u32[]{:S(2)}) collective-permute-start(bf16[2,256,2048]{2,1,0:T(8,128)(2,1)S(1)} %copy-done.1), channel_id=1, source_target_pairs={{0,2},{2,0},{1,3},{3,1},{4,6},{6,4},{5,7},{7,5},{8,10},{10,8},{9,1... | collective-permute-start | bytes 6291464 | tf_op jit(solution)/shard_map/ppermute | solution.py:338
  35.9 85.8 %collective-permute-start = (bf16[2,256,2048]{2,1,0:T(8,128)(2,1)S(1)}, bf16[2,256,2048]{2,1,0:T(8,128)(2,1)}, u32[]{:S(2)}, u32[]{:S(2)}) collective-permute-start(bf16[2,256,2048]{2,1,0:T(8,128)(2,1)S(1)} %copy-done.1), channel_id=1, source_target_pairs={{0,1},{1,0},{2,3},{3,2},{4,5},{5,4},{6,7},{7,6},{8,9},{9,8},{10,11... | collective-permute-start | bytes 6291464 | tf_op jit(solution)/shard_map/ppermute | solution.py:338
  36.5 76.4 %collective-permute-start.10 = (f32[16,512]{0,1:T(8,128)S(1)}, f32[16,512]{0,1:T(8,128)S(1)}, u32[]{:S(2)}, u32[]{:S(2)}) collective-permute-start(f32[16,512]{0,1:T(8,128)S(1)} %bitcast.341), channel_id=1, source_target_pairs={{0,2},{2,0},{1,3},{3,1},{4,6},{6,4},{5,7},{7,5},{8,10},{10,8},{9,1... | collective-permute-start | bytes 98312 | tf_op jit(solution)/shard_map/ppermute | solution.py:338
  38.5 78.1 %collective-permute-start.12 = (f32[16,512]{0,1:T(8,128)S(1)}, f32[16,512]{0,1:T(8,128)S(1)}, u32[]{:S(2)}, u32[]{:S(2)}) collective-permute-start(f32[16,512]{0,1:T(8,128)S(1)} %bitcast.342), channel_id=1, source_target_pairs={{0,4},{4,0},{1,5},{5,1},{2,6},{6,2},{3,7},{7,3},{8,12},{12,8},{9,1... | collective-permute-start | bytes 98312 | tf_op jit(solution)/shard_map/ppermute | solution.py:338
  40.9 47.3 %collective-permute-start.3 = (bf16[64,20]{0,1:T(8,128)(2,1)S(1)}, bf16[64,20]{0,1:T(8,128)(2,1)S(1)}, u32[]{:S(2)}, u32[]{:S(2)}) collective-permute-start(bf16[64,20]{0,1:T(8,128)(2,1)S(1)} %concatenate.80), channel_id=1, source_target_pairs={{0,1},{1,0},{2,3},{3,2},{4,5},{5,4},{6,7},{7,6},{8,9},{9,8},{10,11... | collective-permute-start | bytes 7688 | tf_op jit(solution)/shard_map/ppermute | solution.py:338
  218.2 444.9 %reduce-scatter.7.cloned.1.call-start = ((), (), s32[]{:S(2)}) async-start(), calls=%async_computation.14 | async-start | bytes 10485760 | tf_op jit(solution)/shard_map/reduce_scatter | solution.py:593
  224.1 53.6 %collective-permute-start.25 = (bf16[256,2048]{1,0:T(8,128)(2,1)}, bf16[256,2048]{1,0:T(8,128)(2,1)}, u32[]{:S(2)}, u32[]{:S(2)}) collective-permute-start(bf16[256,2048]{1,0:T(8,128)(2,1)} %get-tuple-element.504.c01), channel_id=1, source_target_pairs={{0,2},{2,0},{1,3},{3,1},{4,6},{6,4},{5,7},{7,5},{8,10},{10,8},{9,1... | collective-permute-start | bytes 3145736 | tf_op jit(solution)/shard_map/ppermute | solution.py:338
  224.5 53.5 %collective-permute-start.21 = (bf16[256,2048]{1,0:T(8,128)(2,1)}, bf16[256,2048]{1,0:T(8,128)(2,1)}, u32[]{:S(2)}, u32[]{:S(2)}) collective-permute-start(bf16[256,2048]{1,0:T(8,128)(2,1)} %get-tuple-element.504.c01), channel_id=1, source_target_pairs={{0,4},{4,0},{1,5},{5,1},{2,6},{6,2},{3,7},{7,3},{8,12},{12,8},{9,1... | collective-permute-start | bytes 3145736 | tf_op jit(solution)/shard_map/ppermute | solution.py:338
  256.2 46.7 %collective-permute-start.30 = (bf16[256,2048]{1,0:T(8,128)(2,1)}, bf16[256,2048]{1,0:T(8,128)(2,1)}, u32[]{:S(2)}, u32[]{:S(2)}) collective-permute-start(bf16[256,2048]{1,0:T(8,128)(2,1)} %collective-permute-done.24.c00), channel_id=1, source_target_pairs={{0,4},{4,0},{1,5},{5,1},{2,6},{6,2},{3,7},{7,3},{8,12},{12,8},{9,1... | collective-permute-start | bytes 3145736 | tf_op jit(solution)/shard_map/ppermute | solution.py:338
  418.6 48.0 %collective-permute-start.47 = (f32[16,512]{1,0:T(8,128)S(1)}, f32[16,512]{1,0:T(8,128)S(1)}, u32[]{:S(2)}, u32[]{:S(2)}) collective-permute-start(f32[16,512]{1,0:T(8,128)S(1)} %collective-permute-done.46.g0), channel_id=1, source_target_pairs={{0,1},{1,0},{2,3},{3,2},{4,5},{5,4},{6,7},{7,6},{8,9},{9,8},{10,11... | collective-permute-start | bytes 98312 | tf_op jit(solution)/shard_map/ppermute | solution.py:338
  517.1 325.5 %reduce-scatter.9.cloned.1.call-start = ((), (), s32[]{:S(2)}) async-start(), calls=%async_computation.15 | async-start | bytes 10485760 | tf_op jit(solution)/shard_map/reduce_scatter | solution.py:593
  537.7 47.9 %collective-permute-start.51 = (bf16[512,2048]{1,0:T(8,128)(2,1)}, bf16[512,2048]{1,0:T(8,128)(2,1)}, u32[]{:S(2)}, u32[]{:S(2)}) collective-permute-start(bf16[512,2048]{1,0:T(8,128)(2,1)} %get-tuple-element.264), channel_id=1, source_target_pairs={{0,1},{1,0},{2,3},{3,2},{4,5},{5,4},{6,7},{7,6},{8,9},{9,8},{10,11... | collective-permute-start | bytes 6291464 | tf_op jit(solution)/shard_map/ppermute | solution.py:338
  558.6 58.5 %collective-permute-start.52 = (bf16[512,2048]{1,0:T(8,128)(2,1)}, bf16[512,2048]{1,0:T(8,128)(2,1)}, u32[]{:S(2)}, u32[]{:S(2)}) collective-permute-start(bf16[512,2048]{1,0:T(8,128)(2,1)} %get-tuple-element.270), channel_id=1, source_target_pairs={{0,1},{1,0},{2,3},{3,2},{4,5},{5,4},{6,7},{7,6},{8,9},{9,8},{10,11... | collective-permute-start | bytes 6291464 | tf_op jit(solution)/shard_map/ppermute | solution.py:338
  766.8 45.5 %collective-permute-start.62 = (bf16[8,2,64,2048]{3,2,0,1:T(8,128)(2,1)}, bf16[8,2,64,2048]{3,2,0,1:T(8,128)(2,1)}, u32[]{:S(2)}, u32[]{:S(2)}) collective-permute-start(bf16[8,2,64,2048]{3,2,0,1:T(8,128)(2,1)} %bitcast.291), channel_id=1, source_target_pairs={{0,1},{1,0},{2,3},{3,2},{4,5},{5,4},{6,7},{7,6},{8,9},{9,8},{10,11... | collective-permute-start | bytes 12582920 | tf_op jit(solution)/shard_map/ppermute | solution.py:338
  767.3 52.8 %all-to-all-start.4 = ((bf16[4,2,256,512]{3,2,1,0:T(8,128)(2,1)}), bf16[4,2,256,512]{3,2,1,0:T(8,128)(2,1)}, u32[]{:S(2)}, u32[]{:S(2)}) async-start(bf16[4,2,256,512]{3,2,1,0:T(8,128)(2,1)} %bitcast.55), calls=%async_computation.5 | async-start | bytes 4194304 | tf_op jit(solution)/shard_map/all_to_all | solution.py:686
  771.9 260.1 %reduce-scatter.11.cloned.1.call-start = ((), (), s32[]{:S(2)}) async-start(), calls=%async_computation.16 | async-start | bytes 10485760 | tf_op jit(solution)/shard_map/reduce_scatter | solution.py:593
  787.1 55.5 %collective-permute-start.64 = (bf16[256,2048]{1,0:T(8,128)(2,1)}, bf16[256,2048]{1,0:T(8,128)(2,1)}, u32[]{:S(2)}, u32[]{:S(2)}) collective-permute-start(bf16[256,2048]{1,0:T(8,128)(2,1)} %get-tuple-element.499), channel_id=1, source_target_pairs={{0,2},{2,0},{1,3},{3,1},{4,6},{6,4},{5,7},{7,5},{8,10},{10,8},{9,1... | collective-permute-start | bytes 3145736 | tf_op jit(solution)/shard_map/ppermute | solution.py:338
  787.2 55.3 %collective-permute-start.65 = (bf16[256,2048]{1,0:T(8,128)(2,1)}, bf16[256,2048]{1,0:T(8,128)(2,1)}, u32[]{:S(2)}, u32[]{:S(2)}) collective-permute-start(bf16[256,2048]{1,0:T(8,128)(2,1)} %get-tuple-element.498), channel_id=1, source_target_pairs={{0,4},{4,0},{1,5},{5,1},{2,6},{6,2},{3,7},{7,3},{8,12},{12,8},{9,1... | collective-permute-start | bytes 3145736 | tf_op jit(solution)/shard_map/ppermute | solution.py:338
  842.6 220.7 %reduce-scatter.13.cloned.1.call-start = ((), (), s32[]{:S(2)}) async-start(), calls=%async_computation.17 | async-start | bytes 1310720 | tf_op jit(solution)/shard_map/reduce_scatter | solution.py:593
  849.5 81.1 %collective-permute-start.71 = (bf16[2,256,1024]{2,1,0:T(8,128)(2,1)}, bf16[2,256,1024]{2,1,0:T(8,128)(2,1)}, u32[]{:S(2)}, u32[]{:S(2)}) collective-permute-start(bf16[2,256,1024]{2,1,0:T(8,128)(2,1)} %get-tuple-element.496), channel_id=1, source_target_pairs={{0,4},{4,0},{1,5},{5,1},{2,6},{6,2},{3,7},{7,3},{8,12},{12,8},{9,1... | collective-permute-start | bytes 3145736 | tf_op jit(solution)/shard_map/ppermute | solution.py:338
  857.3 68.7 %collective-permute-start.70 = (bf16[8,64,2048]{2,1,0:T(8,128)(2,1)}, bf16[8,64,2048]{2,1,0:T(8,128)(2,1)}, u32[]{:S(2)}, u32[]{:S(2)}) collective-permute-start(bf16[8,64,2048]{2,1,0:T(8,128)(2,1)} %dynamic-slice_bitcast_fusion.2), channel_id=1, source_target_pairs={{0,2},{2,0},{1,3},{3,1},{4,6},{6,4},{5,7},{7,5},{8,10},{10,8},{9,1... | collective-permute-start | bytes 6291464 | tf_op jit(solution)/shard_map/ppermute | solution.py:338
  860.5 70.1 %collective-permute-start.74 = (bf16[256,2048]{1,0:T(8,128)(2,1)}, bf16[256,2048]{1,0:T(8,128)(2,1)}, u32[]{:S(2)}, u32[]{:S(2)}) collective-permute-start(bf16[256,2048]{1,0:T(8,128)(2,1)} %add_convert_fusion.10), channel_id=1, source_target_pairs={{0,2},{2,0},{1,3},{3,1},{4,6},{6,4},{5,7},{7,5},{8,10},{10,8},{9,1... | collective-permute-start | bytes 3145736 | tf_op jit(solution)/shard_map/ppermute | solution.py:338
  864.5 66.1 %collective-permute-start.73 = (bf16[256,2048]{1,0:T(8,128)(2,1)}, bf16[256,2048]{1,0:T(8,128)(2,1)}, u32[]{:S(2)}, u32[]{:S(2)}) collective-permute-start(bf16[256,2048]{1,0:T(8,128)(2,1)} %add_convert_fusion.11), channel_id=1, source_target_pairs={{0,4},{4,0},{1,5},{5,1},{2,6},{6,2},{3,7},{7,3},{8,12},{12,8},{9,1... | collective-permute-start | bytes 3145736 | tf_op jit(solution)/shard_map/ppermute | solution.py:338
  866.4 64.2 %collective-permute-start.72 = (bf16[2,256,1024]{2,1,0:T(8,128)(2,1)}, bf16[2,256,1024]{2,1,0:T(8,128)(2,1)}, u32[]{:S(2)}, u32[]{:S(2)}) collective-permute-start(bf16[2,256,1024]{2,1,0:T(8,128)(2,1)} %get-tuple-element.494), channel_id=1, source_target_pairs={{0,4},{4,0},{1,5},{5,1},{2,6},{6,2},{3,7},{7,3},{8,12},{12,8},{9,1... | collective-permute-start | bytes 3145736 | tf_op jit(solution)/shard_map/ppermute | solution.py:338
  986.1 45.9 %collective-permute-start.76 = (bf16[4,256,1024]{2,1,0:T(8,128)(2,1)}, bf16[4,256,1024]{2,1,0:T(8,128)(2,1)}, u32[]{:S(2)}, u32[]{:S(2)}) collective-permute-start(bf16[4,256,1024]{2,1,0:T(8,128)(2,1)} %get-tuple-element.482), channel_id=1, source_target_pairs={{0,4},{4,0},{1,5},{5,1},{2,6},{6,2},{3,7},{7,3},{8,12},{12,8},{9,1... | collective-permute-start | bytes 6291464 | tf_op jit(solution)/shard_map/ppermute | solution.py:338
  1032.0 111.2 %reduce-scatter.15.cloned.1.call-start = ((), (), s32[]{:S(2)}) async-start(), calls=%async_computation.18 | async-start | bytes 2621440 | tf_op jit(solution)/shard_map/reduce_scatter | solution.py:593
  1063.3 113.0 %reduce-scatter.17.cloned.1.call-start = ((), (), s32[]{:S(2)}) async-start(), calls=%async_computation.19 | async-start | bytes 1310720 | tf_op jit(solution)/shard_map/reduce_scatter | solution.py:593
  1069.0 67.6 %collective-permute-start.77 = (bf16[512,2048]{1,0:T(8,128)(2,1)}, bf16[512,2048]{1,0:T(8,128)(2,1)}, u32[]{:S(2)}, u32[]{:S(2)}) collective-permute-start(bf16[512,2048]{1,0:T(8,128)(2,1)} %get-tuple-element.478), channel_id=1, source_target_pairs={{0,1},{1,0},{2,3},{3,2},{4,5},{5,4},{6,7},{7,6},{8,9},{9,8},{10,11... | collective-permute-start | bytes 6291464 | tf_op jit(solution)/shard_map/ppermute | solution.py:338
  1075.1 61.4 %collective-permute-start.79 = (bf16[512,2048]{1,0:T(8,128)(2,1)}, bf16[512,2048]{1,0:T(8,128)(2,1)}, u32[]{:S(2)}, u32[]{:S(2)}) collective-permute-start(bf16[512,2048]{1,0:T(8,128)(2,1)} %fusion.12), channel_id=1, source_target_pairs={{0,2},{2,0},{1,3},{3,1},{4,6},{6,4},{5,7},{7,5},{8,10},{10,8},{9,1... | collective-permute-start | bytes 6291464 | tf_op jit(solution)/shard_map/ppermute | solution.py:338
  1077.7 55.9 %collective-permute-start.80 = (bf16[4,64,2048]{2,1,0:T(8,128)(2,1)}, bf16[4,64,2048]{2,1,0:T(8,128)(2,1)}, u32[]{:S(2)}, u32[]{:S(2)}) collective-permute-start(bf16[4,64,2048]{2,1,0:T(8,128)(2,1)} %dynamic-slice_bitcast_fusion.3), channel_id=1, source_target_pairs={{0,4},{4,0},{1,5},{5,1},{2,6},{6,2},{3,7},{7,3},{8,12},{12,8},{9,1... | collective-permute-start | bytes 3145736 | tf_op jit(solution)/shard_map/ppermute | solution.py:338
  (176 other events, 3919.3 us)
Sparse Core Ops, SparseCore 0:
  35.2 100.4 all-gather.2
  138.5 88.7 all-gather.4
  517.2 145.8 reduce-scatter.6
  665.2 145.1 reduce-scatter.8
  842.7 144.3 reduce-scatter.10
  1032.1 31.0 reduce-scatter.12
  1065.6 42.6 reduce-scatter.14
  1143.4 25.6 reduce-scatter.16

commit v3 on v2

--- a/solution.py
+++ b/solution.py
@@ -171,82 +171,93 @@
     out[pl.ds(b * cap, cap), :] = (dot(s[:, :half], top[...]) + dot(s[:, half:], low[...])).astype(BF)
 
 
-def experts_grad_kernel(base, c00, c01, c10, c11, r0, r1, wd, *rest, cap):
-    og, dh = rest[-2:]
+def experts_grad_kernel(base, *refs, cap, groups):
+    pieces, wd, (og, dh) = refs[: 6 * groups], refs[6 * groups], refs[-2:]
     expert = base[1] + pl.program_id(0)
-
-    @pl.when(pl.program_id(1) == 0)
-    def _():
-        for b, (r, top, low) in enumerate(((r0, c00, c01), (r1, c10, c11))):
-            dispatch(og, b, selection(r[...], expert, cap), top, low, cap)
-
-    dh[...] = dot(og[...], wd[...], NT)
-
-
-def experts_in_kernel(base, f00, f01, f10, f11, r0, r1, g0, g1, dhu, wg, wu, *rest, cap):
-    buf, hg, dg, du, gg, weight, dots = rest[-7:]
-    f = pl.program_id(1)
+    for k in range(groups):
+
+        @pl.when(pl.program_id(1) == k)
+        def _():
+            c00, c01, c10, c11, r0, r1 = pieces[6 * k : 6 * k + 6]
+            for b, (r, top, low) in enumerate(((r0, c00, c01), (r1, c10, c11))):
+                dispatch(og, b, selection(r[...], expert, cap), top, low, cap)
+
+    ff = wd.shape[0]
+    for at in range(0, ff, 512):
+        cols = slice(at, min(at + 512, ff))
+        dh[:, cols] = dot(og[...], wd[cols, :], NT)
+
+
+def experts_in_kernel(base, *refs, cap, groups):
+    pieces, (dhu, wg, wu) = refs[: 8 * groups], refs[8 * groups : 8 * groups + 3]
+    buf, hg, dg, du, gg, weight, dots = refs[-7:]
     expert = base[1] + pl.program_id(0)
-
-    @pl.when(f == 0)
-    def _():
-        for b, (r, g, top, low) in enumerate(((r0, g0, f00, f01), (r1, g1, f10, f11))):
-            s = selection(r[...], expert, cap)
-            dispatch(buf, b, s, top, low, cap)
-            gate = pick_row(g[...], expert)
-            weight[pl.ds(b * cap, cap), :] = jnp.sum(jnp.where(s, gate, 0.0), axis=1, keepdims=True)
-        dots[...] = jnp.zeros_like(dots)
-
-    x = buf[...]
-    gate = dot(x, wg[...])
-    up = dot(x, wu[...])
-    dh = dhu[...]
-    w = weight[...]
-    sg = 1.0 / (1.0 + jnp.exp(-gate))
-    silu = gate * sg
-    hidden = (silu * up).astype(BF).astype(F32)
-    dots[...] += jnp.sum(hidden * dh, axis=1, keepdims=True)
-    dh = dh * w
-    hg[...] = (hidden * w).astype(BF)
-    dg[...] = (dh * up * (sg * (1.0 + gate * (1.0 - sg)))).astype(BF)
-    du[...] = (dh * silu).astype(BF)
-
-    @pl.when(f == pl.num_programs(1) - 1)
-    def _():
-        for b, r in enumerate((r0, r1)):
-            s = selection(r[...], expert, cap)
-            gg[b] = jnp.sum(jnp.where(s, dots[pl.ds(b * cap, cap), :], 0.0), axis=0, keepdims=True)
-
-
-def experts_call(kernel, group, groups, base, small, wide_ins, weights, wide_outs, gates, cap, local, before, flops):
-    tile = 512
+    for k in range(groups):
+
+        @pl.when(pl.program_id(1) == k)
+        def _():
+            f00, f01, f10, f11, r0, r1, g0, g1 = pieces[8 * k : 8 * k + 8]
+            for b, (r, g, top, low) in enumerate(((r0, g0, f00, f01), (r1, g1, f10, f11))):
+                s = selection(r[...], expert, cap)
+                dispatch(buf, b, s, top, low, cap)
+                gate = pick_row(g[...], expert)
+                weight[pl.ds(b * cap, cap), :] = jnp.sum(jnp.where(s, gate, 0.0), axis=1, keepdims=True)
+
+    ff = wg.shape[1]
+    total = None
+    for at in range(0, ff, 512):
+        cols = slice(at, min(at + 512, ff))
+        x = buf[...]
+        gate = dot(x, wg[:, cols])
+        up = dot(x, wu[:, cols])
+        dh = dhu[:, cols]
+        w = weight[...]
+        sg = 1.0 / (1.0 + jnp.exp(-gate))
+        silu = gate * sg
+        hidden = (silu * up).astype(BF).astype(F32)
+        part = jnp.sum(hidden * dh, axis=1, keepdims=True)
+        total = part if total is None else total + part
+        dh = dh * w
+        hg[:, cols] = (hidden * w).astype(BF)
+        dg[:, cols] = (dh * up * (sg * (1.0 + gate * (1.0 - sg)))).astype(BF)
+        du[:, cols] = (dh * silu).astype(BF)
+    dots[...] = total
+    for k in range(groups):
+
+        @pl.when(pl.program_id(1) == k)
+        def _():
+            for b, r in enumerate(pieces[8 * k + 4 : 8 * k + 6]):
+                s = selection(r[...], expert, cap)
+                gg[b] = jnp.sum(jnp.where(s, dots[pl.ds(b * cap, cap), :], 0.0), axis=0, keepdims=True)
+
+
+def experts_call(kernel, first, total, base, small, wide_ins, weights, wide_outs, gates, cap, local, before, flops):
+    groups = len(small)
     width = weights[-1].shape[1] if gates else weights[-1].shape[2]
     ff = weights[-1].shape[2] if gates else weights[-1].shape[1]
     rows = 2 * cap
-    tokens = small[0].shape[0] * 2
-    whole = lambda a: pl.BlockSpec(a.shape, lambda e, f, s: (0, 0), pipeline_mode=pl.Buffered(1))
-    wide = pl.BlockSpec((None, rows, width), lambda e, f, s: (e, group, 0))
-    thin = pl.BlockSpec((None, rows, tile), lambda e, f, s: (e, group, f))
-    if gates:
-        heavy = pl.BlockSpec((None, width, tile), lambda e, f, s: (s[0] + e, 0, f))
-    else:
-        heavy = pl.BlockSpec((None, tile, width), lambda e, f, s: (s[0] + e, f, 0))
+    tokens = small[0][0].shape[0] * 2
+    small = [a for group in small for a in group]
+    whole = lambda a: pl.BlockSpec(a.shape, lambda e, g, s: (0, 0), pipeline_mode=pl.Buffered(1))
+    wide = pl.BlockSpec((None, rows, width), lambda e, g, s: (e, first + g, 0))
+    thin = pl.BlockSpec((None, rows, ff), lambda e, g, s: (e, first + g, 0))
+    heavy = pl.BlockSpec((None, *weights[-1].shape[1:]), lambda e, g, s: (s[0] + e, 0, 0))
     shape = jax.ShapeDtypeStruct
-    outs = [shape((local, groups * rows, width if w else ff), t) for w, t in wide_outs]
+    outs = [shape((local, total * rows, width if w else ff), t) for w, t in wide_outs]
     out_specs = [wide if w else thin for w, _ in wide_outs]
     scratch = []
     if gates:
-        outs.append(shape((local, 2, 1, tokens), F32))
-        out_specs.append(pl.BlockSpec((None, 2, 1, tokens), lambda e, f, s: (e, 0, 0, 0)))
+        outs.append(shape((local, groups, 2, 1, tokens), F32))
+        out_specs.append(pl.BlockSpec((None, None, 2, 1, tokens), lambda e, g, s: (e, g, 0, 0, 0)))
         scratch = [pltpu.VMEM((rows, 1), F32)] * 2
     before = [] if before is None else before
     n = 1 + len(small) + len(wide_ins) + len(weights)
     return pl.pallas_call(
-        partial(kernel, cap=cap),
+        partial(kernel, cap=cap, groups=groups),
         out_shape=outs,
         grid_spec=pltpu.PrefetchScalarGridSpec(
             num_scalar_prefetch=1,
-            grid=(local, ff // tile),
+            grid=(local, groups),
             in_specs=[whole(a) for a in small]
             + [thin] * len(wide_ins)
             + [heavy] * len(weights)
@@ -257,25 +268,26 @@
         input_output_aliases={n + i: i for i in range(len(before))},
         compiler_params=pltpu.CompilerParams(vmem_limit_bytes=VMEM_LIMIT),
         cost_estimate=pl.CostEstimate(
-            flops=flops,
-            bytes_accessed=local * (len(weights) * width * ff * 2 + rows * (2 * width + 10 * ff)) + 4 * tokens * width,
-            transcendentals=local * rows * ff if gates else 0,
+            flops=groups * flops,
+            bytes_accessed=local * (len(weights) * width * ff * 2 + groups * rows * (2 * width + 10 * ff))
+            + groups * 4 * tokens * width,
+            transcendentals=groups * local * rows * ff if gates else 0,
         ),
     )(base, *small, *wide_ins, *weights, *before)
 
 
-def experts_grad(group, groups, base, cots, ranks, wd, cap, local, before):
-    flops = local * 2 * cap * wd.shape[2] * (2 * wd.shape[1] + 4 * cots[0].shape[0])
+def experts_grad(first, total, base, small, wd, cap, local, before):
+    flops = local * 2 * cap * wd.shape[2] * (2 * wd.shape[1] + 4 * small[0][0].shape[0])
     return experts_call(
-        experts_grad_kernel, group, groups, base, [*cots, *ranks], [], [wd], [(True, BF), (False, F32)],
+        experts_grad_kernel, first, total, base, small, [], [wd], [(True, BF), (False, F32)],
         False, cap, local, before, flops,
     )
 
 
-def experts_in(group, groups, base, feats, ranks, gates, dhu, wg, wu, cap, local, before):
-    flops = local * 2 * cap * wg.shape[1] * (4 * wg.shape[2] + 4 * feats[0].shape[0])
+def experts_in(first, total, base, small, dhu, wg, wu, cap, local, before):
+    flops = local * 2 * cap * wg.shape[1] * (4 * wg.shape[2] + 4 * small[0][0].shape[0])
     return experts_call(
-        experts_in_kernel, group, groups, base, [*feats, *ranks, *gates], [dhu], [wg, wu],
+        experts_in_kernel, first, total, base, small, [dhu], [wg, wu],
         [(True, BF), (False, BF), (False, BF), (False, BF)], True, cap, local, before, flops,
     )
 
@@ -467,7 +479,7 @@
 
     ranks_t = gather_pair(rank.T)
     ranks = {k: v.T for k, v in ranks_t.items()}
-    w3, normed, ranks_t = lax.optimization_barrier((w3, normed, ranks_t))
+    w3, normed, ranks_t, near[0] = tie(w3, normed, ranks_t, near[0])
 
     local_experts = w_gate.shape[0]
     mine = local_experts // 2
@@ -475,11 +487,15 @@
     both = lambda halves, dy, dx: [halves[h][dy, dx, dc] for dc in range(2) for h in range(2)]
     pair = lambda table, dy, dx: [table[dy, dx, dc] for dc in range(2)]
 
-    def cot_group(g, base, before):
-        dy, dx = spots[g]
-        return experts_grad(
-            g, len(spots), base, both(cots, dy, dx), pair(ranks_t, dy, dx), w_down, cap, mine, before
-        )
+    close, far = spots[:nx], spots[nx:]
+
+    def cot_call(chips, base, before):
+        small = [[*both(cots, *k), *pair(ranks_t, *k)] for k in chips]
+        return experts_grad(spots.index(chips[0]), len(spots), base, small, w_down, cap, mine, before)
+
+    def in_call(chips, base, before):
+        small = [[*both(feats, *k), *pair(ranks_t, *k), *pair(gates_t, *k)] for k in chips]
+        return experts_in(spots.index(chips[0]), len(spots), base, small, dhu, w_gate, w_up, cap, mine, before)
 
     def sum_group(stats):
         stats = stats.reshape(2, ng, token_count)
@@ -493,9 +509,8 @@
     squares = jnp.stack(
         [jnp.sum(raw[:, i * cols : (i + 1) * cols] ** 2, -1) for i in range(2)]
     )
-    cots = [{(0, dx, 0): v for dx, v in n.items()} for n in near]
-    for i in range(2):
-        cots[i][1, 0, 0] = shift(starts[i], "y", 1)
+    across = [shift(v, "y", 1) for v in starts]
+    squares, near[1] = tie(squares, near[1])
     squares = sum_group(squares)
     factor = lax.rsqrt(squares / width + EPS).T
 
@@ -516,14 +531,20 @@
         cosine,
         sine,
     )
-    for dx in range(1, nx):
-        cots[0][1, dx, 0] = shift(near[0][dx], "y", 1)
-        cots[1][1, dx, 0] = shift(cots[1][1, 0, 0], "x", dx)
-    in_turn = [inverse, inverse]
-    cots = [with_core(p) for p in cots]
+    second, across[0] = tie(inverse, across[0])
+    in_turn = [inverse, second]
     mixed = [attention(i, 1, inverse=in_turn[i])[0].reshape(ng, span, cols) for i in range(seqs)]
     mixed = [lax.all_to_all(a, GROUP, split_axis=0, concat_axis=0, tiled=True) for a in mixed]
-    cot_terms = cot_group(0, base, None)
+    mixed[0], across[1] = tie(mixed[0], across[1])
+    corner = [[shift(near[0][dx], "y", 1) for dx in range(1, nx)], [shift(across[1], "x", dx) for dx in range(1, nx)]]
+    mixed[1], corner = tie(mixed[1], corner)
+    cots = [{(0, dx, 0): v for dx, v in n.items()} for n in near]
+    for i in range(2):
+        cots[i][1, 0, 0] = across[i]
+        for dx in range(1, nx):
+            cots[i][1, dx, 0] = corner[i][dx - 1]
+    cots = [with_core(p) for p in cots]
+    cot_terms = cot_call(close, base, None)
     parts = []
     for i in range(seqs):
         a = mixed[i].transpose(1, 0, 2).reshape(span, width)
@@ -546,31 +567,22 @@
             row, feats[1][0, 0, 0] = tie(row, feats[1][0, 0, 0])
             feats[0] = dict(zip(feats[0], row))
     base_at, feats[1][0, 0, 0] = tie(base, feats[1][0, 0, 0])
-    for g in range(1, len(spots)):
-        if g == len(spots) - 1:
-            row = [feats[1][k] for k in feats[1]]
-            base_at, row, cot_terms = tie(base_at, row, cot_terms)
-            feats[1] = dict(zip(feats[1], row))
-        cot_terms = cot_group(g, base_at, cot_terms)
+    cot_terms = cot_call(far, base_at, cot_terms)
     for dx in range(1, nx):
         feats[0][1, dx, 0] = shift(feats[0][0, dx, 0], "y", 1)
         feats[1][1, dx, 0] = shift(feats[1][1, 0, 0], "x", dx)
     gates_t = gather_pair(router.T)
 
-    before, gate_terms = None, {}
     base_at, cot_terms = tie(base, cot_terms)
+    og, dhu = cot_terms
     feats = [with_core(p) for p in feats]
-    og, dhu = cot_terms
-    for g, (dy, dx) in enumerate(spots):
-        if g == 1:
-            row = [[p[k] for k in p] for p in feats]
-            base_at, row, before = tie(base_at, row, before)
-            feats = [dict(zip(p, v)) for p, v in zip(feats, row)]
-        *before, gg = experts_in(
-            g, len(spots), base_at, both(feats, dy, dx), pair(ranks_t, dy, dx), pair(gates_t, dy, dx), dhu, w_gate, w_up,
-            cap, mine, before,
-        )
-        gate_terms[dy, dx] = gg
+    *before, gg = in_call(close, base_at, None)
+    gate_terms = dict(zip(close, [gg[:, k] for k in range(nx)]))
+    row = [[p[k] for k in p] for p in feats]
+    base_at, row, before = tie(base_at, row, before)
+    feats = [dict(zip(p, v)) for p, v in zip(feats, row)]
+    *before, gg = in_call(far, base_at, before)
+    gate_terms |= dict(zip(far, [gg[:, k] for k in range(nx)]))
     buf, hg, dg, du = before
 
     def weight_grad(left, right):
@@ -634,8 +646,7 @@
     full = weight_grad(buf, dg)
     full, du, hops = tie(full, du, hops)
     straight = direct(back)
-    at, straight, full, scattered[0] = tie(base, straight, full, scattered[0])
-    scattered.append(over_r(full, 1))
+    at, straight = tie(base, straight)
     mix = {}
 
     def mix_group(i, at):
@@ -646,14 +657,19 @@
 
     last = last_hops(back, hops)
     for i in range(len(order)):
+        if i == 1:
+            at, full, scattered[0] = tie(at, full, scattered[0])
+            scattered.append(over_r(full, 1))
         if i == len(order) // 2:
             at, last = tie(at, last)
         at = mix_group(i, at)
     dffn = arrived(back, straight, last)
 
+    def parts_y(part):
+        return [lax.dynamic_index_in_dim(part, i, 1, keepdims=False) for i in (y, 1 - y)]
+
     def swap_y(part):
-        keep = lax.dynamic_index_in_dim(part, y, 1, keepdims=False)
-        give = lax.dynamic_index_in_dim(part, 1 - y, 1, keepdims=False)
+        keep, give = parts_y(part)
         return keep, shift(give, "y", 1)
 
     terms = jnp.stack([gate_terms[k] for k in spots])
@@ -693,9 +709,10 @@
     go = add_low(keep, shift(give, "c", 1))
     parted = [finish_part(scattered[0])]
     hops, straight = first_hops(mix), direct(mix)
-    dattended, go, full, scattered[1], hops, straight = tie(dattended, go, full, scattered[1], hops, straight)
+    dattended, go, full, scattered[1] = tie(dattended, go, full, scattered[1])
+    scattered.append(over_r(full, 1))
+    dattended, hops, straight = tie(dattended, hops, straight)
     last = last_hops(mix, hops)
-    scattered.append(over_r(full, 1))
     dquery, dkey, dvalue, means, gain_grads = attention(0, seqs, inverse, dattended)
 
     go = add_low(
@@ -721,26 +738,14 @@
 
     draws = [raw_grad(dquery, 0, query_g), raw_grad(dkey, 1, key_g), dvalue]
     g_pair = dot(normed, jnp.concatenate(draws[:2], axis=1), TN).astype(BF)
-    g_pair, thirds[0], go = tie(g_pair, thirds[0], go)
-    thirds.append(swap_y(g_pair.reshape(nr, 2, -1, 2 * cols)))
+    keep, give = parts_y(g_pair.reshape(nr, 2, -1, 2 * cols))
+    keep, give, thirds[0], draws = tie(keep, give, thirds[0], draws)
+    thirds.append((keep, shift(give, "y", 1)))
     draw = jnp.concatenate(draws, axis=1)
     dnormed = dot(draw, w3, NT)
     grad_attn_g = jnp.sum(dnormed * normed_n, axis=0)
-    thirds[0] = add_low(*thirds[0])
-    dnormed, thirds[1], go = tie(dnormed.astype(BF), thirds[1], go)
-    go = add_low(*swap_y(go.reshape(nr, 2, wrows, width)))
-    thirds[1], grad_attn_g = tie(add_low(*thirds[1]), grad_attn_g)
-    dnormed = dnormed.reshape(nx, 2, token_count, width)
-    dnormed = [add_low(dnormed[dx, 0], shift(dnormed[dx, 1], "c", 1)) for dx in range(nx)]
-    dnormed = sum(
-        (shift(dnormed[dx], "x", -dx) if dx else dnormed[0]).astype(F32) for dx in range(nx)
-    )
-    own_scale = lax.rsqrt(jnp.mean(own_tokens * own_tokens, axis=-1, keepdims=True) + EPS)
-    own_n = own_tokens * own_scale
-    gd = dnormed * attn_g
-    grad_input = dresid + own_scale * (gd - own_n * jnp.mean(gd * own_n, axis=-1, keepdims=True))
-    grad_input = grad_input.reshape(seqs, span, width)
-
+    g_value, scattered[2] = tie(add_low(*thirds[0]), scattered[2])
+    g_value = over_r(g_value, 0)
     spread = lambda v: lax.dynamic_update_slice(jnp.zeros((width,), F32), v, (me * cols,))
     sums = jnp.concatenate(
         [
@@ -754,13 +759,23 @@
     )
     for axis in ALL:
         sums = scatter_small(sums, axis)
-    thirds[0], scattered[2] = tie(thirds[0], scattered[2])
+    dnormed, thirds[1], go, sums, g_value = tie(dnormed.astype(BF), thirds[1], go, sums, g_value)
+    go = add_low(*swap_y(go.reshape(nr, 2, wrows, width)))
+    thirds[1] = add_low(*thirds[1])
+    dnormed = dnormed.reshape(nx, 2, token_count, width)
+    dnormed = [add_low(dnormed[dx, 0], shift(dnormed[dx, 1], "c", 1)) for dx in range(nx)]
+    dnormed = sum(
+        (shift(dnormed[dx], "x", -dx) if dx else dnormed[0]).astype(F32) for dx in range(nx)
+    )
+    own_scale = lax.rsqrt(jnp.mean(own_tokens * own_tokens, axis=-1, keepdims=True) + EPS)
+    own_n = own_tokens * own_scale
+    gd = dnormed * attn_g
+    grad_input = dresid + own_scale * (gd - own_n * jnp.mean(gd * own_n, axis=-1, keepdims=True))
+    grad_input = grad_input.reshape(seqs, span, width)
+
+    g_pair, go, scattered[2] = tie(over_r(thirds[1], 0), go, scattered[2])
+    go = over_r(go, 0)
     parted.append(finish_part(scattered[2]))
-    g_value = over_r(thirds[0], 0)
-    g_value, thirds[1] = tie(g_value, thirds[1])
-    g_pair = over_r(thirds[1], 0)
-    g_pair, go = tie(g_pair, go)
-    go = over_r(go, 0)
     g_pair = g_pair.reshape(ng, wrows, 2, cols)
     g_value = g_value.reshape(ng, wrows, 1, cols)
     go = go.reshape(wrows, width).astype(F32)

time: 1190 us -> 1150 us (0.966)
  Pallas kernels: 375 us -> 354 us
    ppermute x88, waiting for transfers between devices: 237 us -> 212 us  [shift(): return lax.ppermute(value, axis, [(i, (i + by) % n) for i in range(n)])]
    pallas_call x8 -> x4, Pallas kernels: 149 us -> 128 us  [experts_call(): pl.pallas_call(partial(kernel, cap=cap, groups=groups), out_shape=outs, g...]
    all_to_all x2, waiting for transfers between devices: 12.5 us -> 27.7 us  [local(): lax.all_to_all(a, GROUP, split_axis=0, concat_axis=0, tiled=True)]
    unnamed x245 -> x226, local copies, waits for them, and re-layouts: 27.6 us -> 31.4 us
  transfers between devices with their start and end apart: 101 -> 101, of which waited for: 25 -> 30; matrix products, arithmetic and copies ran while one was open for 29% -> 29% of each run, Pallas kernels for 30% -> 27%
where the time goes in v3:
time: 1150 us; the launch traced here: 1140 us
  Pallas kernels  354 us (31%)
  waiting for transfers between devices  260 us (23%)
  matrix products  163 us (14%)
  other arithmetic  128 us (11%)
  local copies, waits for them, and re-layouts  99.7 us (9%)
  starting transfers between devices  84.4 us (7%)
  blocking collectives  37.9 us (3%)
  between operations  16.5 us (1%)
    ppermute x88, waiting for transfers between devices, shift(): return lax.ppermute(value, axis, [(i, (i + by) % n) for i in range(n)])  212 us
    pallas_call x8, Pallas kernels, experts_out(): pl.pallas_call(partial(experts_out_kernel, cap=cap, forward=forward), out...  140 us
    pallas_call x4, Pallas kernels, experts_call(): pl.pallas_call(partial(kernel, cap=cap, groups=groups), out_shape=outs, g...  128 us
    pallas_call x3, Pallas kernels, attention_call(): pl.pallas_call(partial(kernel, first=first, blocks=blocks, rows=rows, sca...  86.5 us
    dot_general x11, matrix products, dot(): return lax.dot_general(a, b, (dims, ((), ())), preferred_element_type=F32)  79.8 us
    dot_general x3, matrix products, weight_grad(): lax.dot_general(left, right, (((1,), (1,)), ((0,), (0,))), preferred_elem...  78.4 us
    ppermute x88, starting transfers between devices, shift(): return lax.ppermute(value, axis, [(i, (i + by) % n) for i in range(n)])  64.6 us
    convert_element_type x18, other arithmetic, add_low(): return total.astype(BF)  60.2 us
  transfers between devices with their start and end apart: 101, of which 30 were waited for; matrix products, arithmetic and copies ran while one was open for 29% of the time, Pallas kernels for 27%

profile of v3, /device:TPU:0, one launch (start us, length us, event | category | flops | bytes accessed | tf_op | source)
XLA Modules:
  0.0 1144.3 jit_solution(17286337852410124243)
XLA Ops:
  18.5 16.5 %all_to_all.30 = bf16[4,64,1536]{2,1,0:T(8,128)(2,1)} all-to-all(bf16[4,64,1536]{2,1,0:T(8,128)(2,1)} %reshape.378), channel_id=1, replica_groups=mesh['r'=4,'y'=2,'x'=2,'c'=2] {'x','c'}, dimensions={0} | all-to-all | bytes 1572864 | tf_op jit(solution)/shard_map/all_to_all | solution.py:425
  45.8 38.8 %collective-permute-done.1 = bf16[2,256,2048]{2,1,0:T(8,128)(2,1)} collective-permute-done((bf16[2,256,2048]{2,1,0:T(8,128)(2,1)S(1)}, bf16[2,256,2048]{2,1,0:T(8,128)(2,1)}, u32[]{:S(2)}, u32[]{:S(2)}) %collective-permute-start.1) | collective-permute-done | bytes 2097184 | tf_op jit(solution)/shard_map/ppermute | solution.py:350
  143.2 17.5 %fusion.71 = f32[2048,1536]{1,0:T(8,128)S(1)} fusion(bf16[2048,2048]{1,0:T(8,128)(2,1)} %multiply_convert_fusion, bf16[2048,1536]{1,0:T(8,128)(2,1)} %all-gather.3.cloned.1.call-done), kind=kOutput, calls=%fused_computation.271 | convolution fusion | flops 12884901888 | bytes 27262976 | tf_op jit(solution)/shard_map/dot_general | solution.py:20
  166.0 11.1 psum.14
  178.5 15.5 %shard_map.263 = bf16[4,1,256,512]{3,2,1,0:T(8,128)(2,1)} custom-call(s32[4]{0:T(128)} %get-tuple-element.188.inv, s32[2]{0:T(128)} %lens.5, f32[4,2,256,1536]{3,2,1,0:T(8,128)} %bitcast.305, f32[4,2,256,1536]{3,2,1,0:T(8,128)} %bitcast.306, f32[4,2,256,1536]{3,2,1,0:T(8,128)} %bitcast.307, f32[4,2,256,2]{3,2,1,0:T(8,128)} %bitcast.321, f32[1,512]{1,0:T(1,128)} %bitcast.382, ...), custom_call_target="tpu_custom_call" | custom-call | flops 1342177280 | bytes 18874368 | tf_op jit(solution)/shard_map/pallas_call | solution.py:145
  199.7 16.3 %all-to-all-done.1 = bf16[4,256,512]{2,1,0:T(8,128)(2,1)S(1)} async-done(((bf16[4,256,512]{2,1,0:T(8,128)(2,1)}), bf16[4,256,512]{2,1,0:T(8,128)(2,1)S(1)}, u32[]{:S(2)}, u32[]{:S(2)}) %all-to-all-start.1) | async-done | bytes 1048608 | tf_op jit(solution)/shard_map/all_to_all | solution.py:537
  219.8 15.7 %shard_map.264 = bf16[4,1,256,512]{3,2,1,0:T(8,128)(2,1)} custom-call(s32[4]{0:T(128)} %get-tuple-element.188.inv, s32[2]{0:T(128)} %lens.5, f32[4,2,256,1536]{3,2,1,0:T(8,128)} %bitcast.308, f32[4,2,256,1536]{3,2,1,0:T(8,128)} %bitcast.309, f32[4,2,256,1536]{3,2,1,0:T(8,128)} %bitcast.310, f32[4,2,256,2]{3,2,1,0:T(8,128)} %bitcast.322, f32[1,512]{1,0:T(1,128)} %bitcast.383, ...), custom_call_target="tpu_custom_call" | custom-call | flops 1342177280 | bytes 18874368 | tf_op jit(solution)/shard_map/pallas_call | solution.py:145
  243.0 11.5 %all-to-all-done.2 = bf16[4,256,512]{2,1,0:T(8,128)(2,1)} async-done(((bf16[4,256,512]{2,1,0:T(8,128)(2,1)}), bf16[4,256,512]{2,1,0:T(8,128)(2,1)}, u32[]{:S(2)}, u32[]{:S(2)}) %all-to-all-start.2) | async-done | bytes 1048608 | tf_op jit(solution)/shard_map/all_to_all | solution.py:537
  271.0 21.9 %collective-permute-done.45.refs_14_ = f32[16,512]{1,0:T(8,128)S(1)} collective-permute-done((f32[16,512]{1,0:T(8,128)S(1)}, f32[16,512]{1,0:T(8,128)S(1)}, u32[]{:S(2)}, u32[]{:S(2)}) %collective-permute-start.45) | collective-permute-done | bytes 32800 | tf_op jit(solution)/shard_map/ppermute | solution.py:350
  309.6 23.6 %shard_map.265 = (bf16[2,2304,2048]{2,1,0:T(8,128)(2,1)}, f32[2,2304,1024]{2,1,0:T(8,128)}) custom-call(s32[3]{0:T(128)} %pad_add_fusion.1.base, bf16[256,2048]{1,0:T(8,128)(2,1)} %get-tuple-element.187.refs_0_, bf16[256,2048]{1,0:T(8,128)(2,1)} %get-tuple-element.201.refs_1_, bf16[256,2048]{1,0:T(8,128)(2,1)} %collective-permute-done.28.refs_2_, ...), custom_call_target="tpu_custom_call" | custom-call | flops 14495514624 | bytes 49807360 | tf_op jit(solution)/shard_map/pallas_call | solution.py:255
  337.1 23.8 %shard_map.266 = (bf16[2,2304,2048]{2,1,0:T(8,128)(2,1)}, f32[2,2304,1024]{2,1,0:T(8,128)}) custom-call(s32[3]{0:T(128)} %pad_add_fusion.1.base, bf16[256,2048]{1,0:T(8,128)(2,1)} %collective-permute-done.19.refs_0_, bf16[256,2048]{1,0:T(8,128)(2,1)} %collective-permute-done.18.refs_1_, ...), custom_call_target="tpu_custom_call", output_to_operand_aliasing={{0}: (14, {}), {1}: (15, {})} | custom-call | flops 14495514624 | bytes 49807360 | tf_op jit(solution)/shard_map/pallas_call | solution.py:255
  362.1 40.3 %shard_map.267 = (bf16[2,2304,2048]{2,1,0:T(8,128)(2,1)}, bf16[2,2304,1024]{2,1,0:T(8,128)(2,1)}, bf16[2,2304,1024]{2,1,0:T(8,128)(2,1)}, bf16[2,2304,1024]{2,1,0:T(8,128)(2,1)}, f32[2,2,2,1,512]{4,3,2,1,0:T(1,128)}) custom-call(s32[3]{0:T(128)} %pad_add_fusion.1.base, bf16[256,2048]{1,0:T(8,128)(2,1)} %copy-done.25, bf16[256,2048]{1,0:T(8,128)(2,1)} %copy-done.23, ...), custom_call_target="tpu_custom_call" | custom-call | flops 24159191040 | bytes 58195968 | tf_op jit(solution)/shard_map/pallas_call | solution.py:255
  404.3 40.2 %shard_map.268 = (bf16[2,2304,2048]{2,1,0:T(8,128)(2,1)}, bf16[2,2304,1024]{2,1,0:T(8,128)(2,1)}, bf16[2,2304,1024]{2,1,0:T(8,128)(2,1)}, bf16[2,2304,1024]{2,1,0:T(8,128)(2,1)}, f32[2,2,2,1,512]{4,3,2,1,0:T(1,128)}) custom-call(s32[3]{0:T(128)} %pad_add_fusion.1.base, ...), custom_call_target="tpu_custom_call", output_to_operand_aliasing={{0}: (20, {}), {1}: (21, {}), {2}: (22, {}), {3}: (23, {})} | custom-call | flops 24159191040 | bytes 58195968 | tf_op jit(solution)/shard_map/pallas_call | solution.py:255
  444.5 26.8 %convolution_convert_fusion.3 = bf16[2,2048,1024]{2,1,0:T(8,128)(2,1)} fusion(bf16[2,2304,2048]{2,1,0:T(8,128)(2,1)} %get-tuple-element.211, bf16[2,2304,1024]{2,1,0:T(8,128)(2,1)} %get-tuple-element.235.refs_0_), kind=kOutput, calls=%fused_computation.16 | convolution fusion | flops 19331547136 | bytes 36700160 | tf_op jit(solution)/shard_map/dot_general | solution.py:589
  471.3 20.9 %shard_map.269 = (bf16[512,2048]{1,0:T(8,128)(2,1)}, bf16[512,2048]{1,0:T(8,128)(2,1)}) custom-call(s32[3]{0:T(128)} %pad_add_fusion.1.base, bf16[2,2304,1024]{2,1,0:T(8,128)(2,1)} %get-tuple-element.237.refs_0_, bf16[2,2304,1024]{2,1,0:T(8,128)(2,1)} %get-tuple-element.300.refs_1_, f32[512,16]{1,0:T(8,128)} %bitcast.362, f32[512,16]{1,0:T(8,128)} %bitcast.364, ...), custom_call_target="tpu_custom_call" | custom-call | flops 12079595520 | bytes 25690112 | tf_op jit(solution)/shard_map/pallas_call | solution.py:330
  492.7 20.5 %shard_map.270 = (bf16[512,2048]{1,0:T(8,128)(2,1)}, bf16[512,2048]{1,0:T(8,128)(2,1)}) custom-call(s32[3]{0:T(128)} %pad_add_fusion.1.base, bf16[2,2304,1024]{2,1,0:T(8,128)(2,1)} %get-tuple-element.237.refs_0_, bf16[2,2304,1024]{2,1,0:T(8,128)(2,1)} %get-tuple-element.300.refs_1_, f32[512,16]{1,0:T(8,128)} %bitcast.354, f32[512,16]{1,0:T(8,128)} %bitcast.360, ...), custom_call_target="tpu_custom_call" | custom-call | flops 12079595520 | bytes 25690112 | tf_op jit(solution)/shard_map/pallas_call | solution.py:330
  516.3 20.9 %shard_map.271 = (bf16[512,2048]{1,0:T(8,128)(2,1)}, bf16[512,2048]{1,0:T(8,128)(2,1)}) custom-call(s32[3]{0:T(128)} %pad_add_fusion.1.base, bf16[2,2304,1024]{2,1,0:T(8,128)(2,1)} %get-tuple-element.237.refs_0_, bf16[2,2304,1024]{2,1,0:T(8,128)(2,1)} %get-tuple-element.300.refs_1_, f32[512,16]{1,0:T(8,128)} %bitcast.352, f32[512,16]{1,0:T(8,128)} %bitcast.358, ...), custom_call_target="tpu_custom_call" | custom-call | flops 12079595520 | bytes 25690112 | tf_op jit(solution)/shard_map/pallas_call | solution.py:330
  551.8 24.8 %convolution_convert_fusion.2 = bf16[2,2048,1024]{2,1,0:T(8,128)(2,1)} fusion(bf16[2,2304,2048]{2,1,0:T(8,128)(2,1)} %get-tuple-element.265, bf16[2,2304,1024]{2,1,0:T(8,128)(2,1)S(1)} %bitcast.315), kind=kOutput, calls=%fused_computation.15 | convolution fusion | flops 19331547136 | bytes 36700160 | tf_op jit(solution)/shard_map/dot_general | solution.py:589
  587.2 14.2 %shard_map.273 = (bf16[512,2048]{1,0:T(8,128)(2,1)}, bf16[512,2048]{1,0:T(8,128)(2,1)}) custom-call(s32[3]{0:T(128)} %pad_add_fusion.1.base, bf16[2,2304,1024]{2,1,0:T(8,128)(2,1)} %get-tuple-element.235.refs_0_, f32[512,16]{1,0:T(8,128)} %bitcast.363, f32[512,16]{1,0:T(8,128)} %bitcast.365, bf16[4,1024,2048]{2,1,0:T(8,128)(2,1)} %refs_3_.7), custom_call_target="tpu_custom_call" | custom-call | flops 7247757312 | bytes 14942208 | tf_op jit(solution)/shard_map/pallas_call | solution.py:330
  601.4 12.8 %reduce-scatter.7.cloned.1.call-done = bf16[2,512,1024]{2,1,0:T(8,128)(2,1)} async-done(((bf16[2,2048,1024]{2,1,0:T(8,128)(2,1)}), bf16[2,512,1024]{2,1,0:T(8,128)(2,1)}) %reduce-scatter.7.cloned.1.call-update) | async-done | bytes 2097168 | tf_op jit(solution)/shard_map/reduce_scatter | solution.py:605
  616.7 20.5 %shard_map.272 = (bf16[512,2048]{1,0:T(8,128)(2,1)}, bf16[512,2048]{1,0:T(8,128)(2,1)}) custom-call(s32[3]{0:T(128)} %pad_add_fusion.1.base, bf16[2,2304,1024]{2,1,0:T(8,128)(2,1)} %get-tuple-element.237.refs_0_, bf16[2,2304,1024]{2,1,0:T(8,128)(2,1)} %get-tuple-element.300.refs_1_, f32[512,16]{1,0:T(8,128)} %copy-done.40, f32[512,16]{1,0:T(8,128)} %bitcast.356, ...), custom_call_target="tpu_custom_call" | custom-call | flops 12079595520 | bytes 25690112 | tf_op jit(solution)/shard_map/pallas_call | solution.py:330
  657.6 14.2 %shard_map.274 = (bf16[512,2048]{1,0:T(8,128)(2,1)}, bf16[512,2048]{1,0:T(8,128)(2,1)}) custom-call(s32[3]{0:T(128)} %pad_add_fusion.1.base, bf16[2,2304,1024]{2,1,0:T(8,128)(2,1)} %get-tuple-element.235.refs_0_, f32[512,16]{1,0:T(8,128)} %bitcast.355, f32[512,16]{1,0:T(8,128)} %bitcast.361, bf16[4,1024,2048]{2,1,0:T(8,128)(2,1)} %refs_3_.7), custom_call_target="tpu_custom_call" | custom-call | flops 7247757312 | bytes 14942208 | tf_op jit(solution)/shard_map/pallas_call | solution.py:330
  680.0 14.2 %shard_map.275 = (bf16[512,2048]{1,0:T(8,128)(2,1)}, bf16[512,2048]{1,0:T(8,128)(2,1)}) custom-call(s32[3]{0:T(128)} %pad_add_fusion.1.base, bf16[2,2304,1024]{2,1,0:T(8,128)(2,1)} %get-tuple-element.235.refs_0_, f32[512,16]{1,0:T(8,128)} %bitcast.353, f32[512,16]{1,0:T(8,128)} %bitcast.359, bf16[4,1024,2048]{2,1,0:T(8,128)(2,1)} %refs_3_.7), custom_call_target="tpu_custom_call" | custom-call | flops 7247757312 | bytes 14942208 | tf_op jit(solution)/shard_map/pallas_call | solution.py:330
  694.2 14.2 %shard_map.276 = (bf16[512,2048]{1,0:T(8,128)(2,1)}, bf16[512,2048]{1,0:T(8,128)(2,1)}) custom-call(s32[3]{0:T(128)} %pad_add_fusion.1.base, bf16[2,2304,1024]{2,1,0:T(8,128)(2,1)} %get-tuple-element.235.refs_0_, f32[512,16]{1,0:T(8,128)} %copy-done.40, f32[512,16]{1,0:T(8,128)} %bitcast.357, bf16[4,1024,2048]{2,1,0:T(8,128)(2,1)} %refs_3_.7), custom_call_target="tpu_custom_call" | custom-call | flops 7247757312 | bytes 14942208 | tf_op jit(solution)/shard_map/pallas_call | solution.py:330
  740.5 26.9 %convolution_convert_fusion.1 = bf16[2,2048,1024]{2,1,0:T(8,128)(2,1)} fusion(bf16[2,2304,2048]{2,1,0:T(8,128)(2,1)} %get-tuple-element.265, bf16[2,2304,1024]{2,1,0:T(8,128)(2,1)} %get-tuple-element.300.refs_1_), kind=kOutput, calls=%fused_computation.14 | convolution fusion | flops 19331547136 | bytes 36700160 | tf_op jit(solution)/shard_map/dot_general | solution.py:589
  812.4 21.9 %collective-permute-done.64 = bf16[256,2048]{1,0:T(8,128)(2,1)} collective-permute-done((bf16[256,2048]{1,0:T(8,128)(2,1)}, bf16[256,2048]{1,0:T(8,128)(2,1)}, u32[]{:S(2)}, u32[]{:S(2)}) %collective-permute-start.64) | collective-permute-done | bytes 1048608 | tf_op jit(solution)/shard_map/ppermute | solution.py:350
  848.4 55.3 %shard_map.277 = (f32[4,2,256,512]{3,2,1,0:T(8,128)}, f32[4,2,256,512]{3,2,1,0:T(8,128)}, bf16[4,2,256,512]{3,2,1,0:T(8,128)(2,1)}, f32[4,2,256,2]{3,2,1,0:T(8,128)}, f32[2,2,512]{2,1,0:T(2,128)}) custom-call(s32[4]{0:T(128)} %get-tuple-element.188.inv, s32[2]{0:T(128)} %lens.5, f32[4,2,256,1536]{3,2,1,0:T(8,128)} %bitcast.311, ...), custom_call_target="tpu_custom_call" | custom-call | flops 6710886400 | bytes 18874368 | tf_op jit(solution)/shard_map/pallas_call | solution.py:145
  943.9 13.1 %fusion.21 = bf16[2048,1024]{1,0:T(8,128)(2,1)S(1)} fusion(bf16[2048,2048]{1,0:T(8,128)(2,1)} %multiply_convert_fusion, bf16[2048,512]{1,0:T(8,128)(2,1)S(1)} %get-tuple-element.328, bf16[2048,512]{1,0:T(8,128)(2,1)S(1)} %get-tuple-element.327), kind=kOutput, calls=%fused_computation.61 | convolution fusion | flops 8600420352 | bytes 16777216 | tf_op jit(solution)/shard_map/dot_general | solution.py:20
  961.6 20.9 %multiply_reduce_fusion = (f32[2048]{0:T(1024)S(1)}, bf16[2048,2048]{1,0:T(8,128)(2,1)}) fusion(f32[2048]{0:T(1024)S(1)} %bitcast.394, bf16[1,2,256,2048]{3,2,1,0:T(8,128)(2,1)} %bitcast.10, bf16[1,2,256,2048]{3,2,1,0:T(8,128)(2,1)} %bitcast.9, bf16[1,2,256,2048]{3,2,1,0:T(8,128)(2,1)} %bitcast.8, bf16[1,2,256,2048]{3,2,1,0:T(8,128)(2,1)S(1)} %bitcast.318, ...), kind=kOutput, calls=%fused_computation.1 | convolution fusion | flops 12937328640 | bytes 29376512 | tf_op jit(solution)/shard_map/dot_general | solution.py:20
  996.3 33.1 %collective-permute-done.80 = f32[256,20]{0,1:T(8,128)S(1)} collective-permute-done((f32[256,20]{0,1:T(8,128)S(1)}, f32[256,20]{0,1:T(8,128)S(1)}, u32[]{:S(2)}, u32[]{:S(2)}) %collective-permute-start.80) | collective-permute-done | bytes 20512 | tf_op jit(solution)/shard_map/ppermute | solution.py:350
  1074.9 17.3 %collective-permute-done.86 = bf16[4,64,2048]{2,1,0:T(8,128)(2,1)S(1)} collective-permute-done((bf16[4,64,2048]{2,1,0:T(8,128)(2,1)S(1)}, bf16[4,64,2048]{2,1,0:T(8,128)(2,1)S(1)}, u32[]{:S(2)}, u32[]{:S(2)}) %collective-permute-start.86) | collective-permute-done | bytes 1048608 | tf_op jit(solution)/shard_map/ppermute | solution.py:350
  1104.9 10.9 collective-permute-done.85
  (612 shorter events, 431.7 us)
Async XLA Ops:
  7.2 136.0 %all-gather.3.cloned.1.call-start = ((), (), s32[]{:S(2)}) async-start(), calls=%async_computation.12 | async-start | bytes 7077888 | tf_op jit(solution)/shard_map/all_gather | solution.py:426
  35.1 221.7 %all-gather.5.cloned.1.call-start = ((), (), s32[]{:S(2)}) async-start(), calls=%async_computation.13 | async-start | bytes 8650752 | tf_op jit(solution)/shard_map/all_gather | solution.py:432
  35.8 48.7 %collective-permute-start.1 = (bf16[2,256,2048]{2,1,0:T(8,128)(2,1)S(1)}, bf16[2,256,2048]{2,1,0:T(8,128)(2,1)}, u32[]{:S(2)}, u32[]{:S(2)}) collective-permute-start(bf16[2,256,2048]{2,1,0:T(8,128)(2,1)S(1)} %copy-done.1), channel_id=1, source_target_pairs={{0,2},{2,0},{1,3},{3,1},{4,6},{6,4},{5,7},{7,5},{8,10},{10,8},{9,1... | collective-permute-start | bytes 6291464 | tf_op jit(solution)/shard_map/ppermute | solution.py:350
  35.9 85.8 %collective-permute-start = (bf16[2,256,2048]{2,1,0:T(8,128)(2,1)S(1)}, bf16[2,256,2048]{2,1,0:T(8,128)(2,1)}, u32[]{:S(2)}, u32[]{:S(2)}) collective-permute-start(bf16[2,256,2048]{2,1,0:T(8,128)(2,1)S(1)} %copy-done.1), channel_id=1, source_target_pairs={{0,1},{1,0},{2,3},{3,2},{4,5},{5,4},{6,7},{7,6},{8,9},{9,8},{10,11... | collective-permute-start | bytes 6291464 | tf_op jit(solution)/shard_map/ppermute | solution.py:350
  36.5 76.4 %collective-permute-start.10 = (f32[16,512]{0,1:T(8,128)S(1)}, f32[16,512]{0,1:T(8,128)S(1)}, u32[]{:S(2)}, u32[]{:S(2)}) collective-permute-start(f32[16,512]{0,1:T(8,128)S(1)} %bitcast.348), channel_id=1, source_target_pairs={{0,2},{2,0},{1,3},{3,1},{4,6},{6,4},{5,7},{7,5},{8,10},{10,8},{9,1... | collective-permute-start | bytes 98312 | tf_op jit(solution)/shard_map/ppermute | solution.py:350
  38.5 78.3 %collective-permute-start.12 = (f32[16,512]{0,1:T(8,128)S(1)}, f32[16,512]{0,1:T(8,128)S(1)}, u32[]{:S(2)}, u32[]{:S(2)}) collective-permute-start(f32[16,512]{0,1:T(8,128)S(1)} %bitcast.349), channel_id=1, source_target_pairs={{0,4},{4,0},{1,5},{5,1},{2,6},{6,2},{3,7},{7,3},{8,12},{12,8},{9,1... | collective-permute-start | bytes 98312 | tf_op jit(solution)/shard_map/ppermute | solution.py:350
  40.9 46.6 %collective-permute-start.3 = (bf16[64,20]{0,1:T(8,128)(2,1)S(1)}, bf16[64,20]{0,1:T(8,128)(2,1)S(1)}, u32[]{:S(2)}, u32[]{:S(2)}) collective-permute-start(bf16[64,20]{0,1:T(8,128)(2,1)S(1)} %concatenate.79), channel_id=1, source_target_pairs={{0,1},{1,0},{2,3},{3,2},{4,5},{5,4},{6,7},{7,6},{8,9},{9,8},{10,11... | collective-permute-start | bytes 7688 | tf_op jit(solution)/shard_map/ppermute | solution.py:350
  135.4 64.3 %collective-permute-start.18 = (bf16[256,2048]{1,0:T(8,128)(2,1)}, bf16[256,2048]{1,0:T(8,128)(2,1)}, u32[]{:S(2)}, u32[]{:S(2)}) collective-permute-start(bf16[256,2048]{1,0:T(8,128)(2,1)} %get-tuple-element.201.refs_1_), channel_id=1, source_target_pairs={{0,4},{4,0},{1,5},{5,1},{2,6},{6,2},{3,7},{7,3},{8,12},{12,8},{9,1... | collective-permute-start | bytes 3145736 | tf_op jit(solution)/shard_map/ppermute | solution.py:350
  178.5 41.3 %collective-permute-start.19 = (bf16[256,2048]{1,0:T(8,128)(2,1)}, bf16[256,2048]{1,0:T(8,128)(2,1)}, u32[]{:S(2)}, u32[]{:S(2)}) collective-permute-start(bf16[256,2048]{1,0:T(8,128)(2,1)} %get-tuple-element.187.refs_0_), channel_id=1, source_target_pairs={{0,4},{4,0},{1,5},{5,1},{2,6},{6,2},{3,7},{7,3},{8,12},{12,8},{9,1... | collective-permute-start | bytes 3145736 | tf_op jit(solution)/shard_map/ppermute | solution.py:350
  197.6 44.8 %collective-permute-start.20 = (bf16[256,2048]{1,0:T(8,128)(2,1)}, bf16[256,2048]{1,0:T(8,128)(2,1)}, u32[]{:S(2)}, u32[]{:S(2)}) collective-permute-start(bf16[256,2048]{1,0:T(8,128)(2,1)} %collective-permute-done.16.refs_6_), channel_id=1, source_target_pairs={{0,4},{4,0},{1,5},{5,1},{2,6},{6,2},{3,7},{7,3},{8,12},{12,8},{9,1... | collective-permute-start | bytes 3145736 | tf_op jit(solution)/shard_map/ppermute | solution.py:350
  240.0 374.3 %reduce-scatter.7.cloned.1.call-start = ((), (), s32[]{:S(2)}) async-start(), calls=%async_computation.14 | async-start | bytes 10485760 | tf_op jit(solution)/shard_map/reduce_scatter | solution.py:605
  360.9 41.5 %collective-permute-start.48 = (f32[16,512]{1,0:T(8,128)S(1)}, f32[16,512]{1,0:T(8,128)S(1)}, u32[]{:S(2)}, u32[]{:S(2)}) collective-permute-start(f32[16,512]{1,0:T(8,128)S(1)} %collective-permute-done.47.refs_6_), channel_id=1, source_target_pairs={{0,1},{1,0},{2,3},{3,2},{4,5},{5,4},{6,7},{7,6},{8,9},{9,8},{10,11... | collective-permute-start | bytes 98312 | tf_op jit(solution)/shard_map/ppermute | solution.py:350
  361.0 41.5 %collective-permute-start.50 = (f32[16,512]{1,0:T(8,128)S(1)}, f32[16,512]{1,0:T(8,128)S(1)}, u32[]{:S(2)}, u32[]{:S(2)}) collective-permute-start(f32[16,512]{1,0:T(8,128)S(1)} %collective-permute-done.49.refs_14_), channel_id=1, source_target_pairs={{0,1},{1,0},{2,3},{3,2},{4,5},{5,4},{6,7},{7,6},{8,9},{9,8},{10,11... | collective-permute-start | bytes 98312 | tf_op jit(solution)/shard_map/ppermute | solution.py:350
  471.3 303.9 %reduce-scatter.9.cloned.1.call-start = ((), (), s32[]{:S(2)}) async-start(), calls=%async_computation.15 | async-start | bytes 10485760 | tf_op jit(solution)/shard_map/reduce_scatter | solution.py:605
  544.3 42.8 %collective-permute-start.56 = (bf16[256,2048]{1,0:T(8,128)(2,1)}, bf16[256,2048]{1,0:T(8,128)(2,1)S(1)}, u32[]{:S(2)}, u32[]{:S(2)}) collective-permute-start(bf16[256,2048]{1,0:T(8,128)(2,1)} %slice.167), channel_id=1, source_target_pairs={{0,4},{4,0},{1,5},{5,1},{2,6},{6,2},{3,7},{7,3},{8,12},{12,8},{9,1... | collective-permute-start | bytes 3145736 | tf_op jit(solution)/shard_map/ppermute | solution.py:350
  718.2 58.7 %collective-permute-start.68 = (bf16[512,2048]{1,0:T(8,128)(2,1)}, bf16[512,2048]{1,0:T(8,128)(2,1)}, u32[]{:S(2)}, u32[]{:S(2)}) collective-permute-start(bf16[512,2048]{1,0:T(8,128)(2,1)} %get-tuple-element.308), channel_id=1, source_target_pairs={{0,1},{1,0},{2,3},{3,2},{4,5},{5,4},{6,7},{7,6},{8,9},{9,8},{10,11... | collective-permute-start | bytes 6291464 | tf_op jit(solution)/shard_map/ppermute | solution.py:350
  718.2 64.1 %collective-permute-start.66 = (bf16[512,2048]{1,0:T(8,128)(2,1)}, bf16[512,2048]{1,0:T(8,128)(2,1)}, u32[]{:S(2)}, u32[]{:S(2)}) collective-permute-start(bf16[512,2048]{1,0:T(8,128)(2,1)} %get-tuple-element.306), channel_id=1, source_target_pairs={{0,1},{1,0},{2,3},{3,2},{4,5},{5,4},{6,7},{7,6},{8,9},{9,8},{10,11... | collective-permute-start | bytes 6291464 | tf_op jit(solution)/shard_map/ppermute | solution.py:350
  718.7 69.3 %collective-permute-start.63 = (bf16[512,2048]{1,0:T(8,128)(2,1)}, bf16[512,2048]{1,0:T(8,128)(2,1)}, u32[]{:S(2)}, u32[]{:S(2)}) collective-permute-start(bf16[512,2048]{1,0:T(8,128)(2,1)} %get-tuple-element.304), channel_id=1, source_target_pairs={{0,1},{1,0},{2,3},{3,2},{4,5},{5,4},{6,7},{7,6},{8,9},{9,8},{10,11... | collective-permute-start | bytes 6291464 | tf_op jit(solution)/shard_map/ppermute | solution.py:350
  740.5 246.0 %reduce-scatter.11.cloned.1.call-start = ((), (), s32[]{:S(2)}) async-start(), calls=%async_computation.16 | async-start | bytes 10485760 | tf_op jit(solution)/shard_map/reduce_scatter | solution.py:605
  776.5 258.1 %reduce-scatter.13.cloned.1.call-start = ((), (), s32[]{:S(2)}) async-start(), calls=%async_computation.17 | async-start | bytes 1310720 | tf_op jit(solution)/shard_map/reduce_scatter | solution.py:605
  791.8 42.5 %collective-permute-start.64 = (bf16[256,2048]{1,0:T(8,128)(2,1)}, bf16[256,2048]{1,0:T(8,128)(2,1)}, u32[]{:S(2)}, u32[]{:S(2)}) collective-permute-start(bf16[256,2048]{1,0:T(8,128)(2,1)} %get-tuple-element.483), channel_id=1, source_target_pairs={{0,2},{2,0},{1,3},{3,1},{4,6},{6,4},{5,7},{7,5},{8,10},{10,8},{9,1... | collective-permute-start | bytes 3145736 | tf_op jit(solution)/shard_map/ppermute | solution.py:350
  792.1 42.3 %collective-permute-start.65 = (bf16[256,2048]{1,0:T(8,128)(2,1)}, bf16[256,2048]{1,0:T(8,128)(2,1)}, u32[]{:S(2)}, u32[]{:S(2)}) collective-permute-start(bf16[256,2048]{1,0:T(8,128)(2,1)} %get-tuple-element.482), channel_id=1, source_target_pairs={{0,4},{4,0},{1,5},{5,1},{2,6},{6,2},{3,7},{7,3},{8,12},{12,8},{9,1... | collective-permute-start | bytes 3145736 | tf_op jit(solution)/shard_map/ppermute | solution.py:350
  799.1 111.9 %collective-permute-start.71 = (bf16[2,256,1024]{2,1,0:T(8,128)(2,1)}, bf16[2,256,1024]{2,1,0:T(8,128)(2,1)}, u32[]{:S(2)}, u32[]{:S(2)}) collective-permute-start(bf16[2,256,1024]{2,1,0:T(8,128)(2,1)} %get-tuple-element.480), channel_id=1, source_target_pairs={{0,4},{4,0},{1,5},{5,1},{2,6},{6,2},{3,7},{7,3},{8,12},{12,8},{9,1... | collective-permute-start | bytes 3145736 | tf_op jit(solution)/shard_map/ppermute | solution.py:350
  837.5 69.0 %collective-permute-start.70 = (bf16[8,64,2048]{2,1,0:T(8,128)(2,1)}, bf16[8,64,2048]{2,1,0:T(8,128)(2,1)}, u32[]{:S(2)}, u32[]{:S(2)}) collective-permute-start(bf16[8,64,2048]{2,1,0:T(8,128)(2,1)} %dynamic-slice_bitcast_fusion.2), channel_id=1, source_target_pairs={{0,2},{2,0},{1,3},{3,1},{4,6},{6,4},{5,7},{7,5},{8,10},{10,8},{9,1... | collective-permute-start | bytes 6291464 | tf_op jit(solution)/shard_map/ppermute | solution.py:350
  841.8 69.3 %collective-permute-start.74 = (bf16[256,2048]{1,0:T(8,128)(2,1)}, bf16[256,2048]{1,0:T(8,128)(2,1)}, u32[]{:S(2)}, u32[]{:S(2)}) collective-permute-start(bf16[256,2048]{1,0:T(8,128)(2,1)} %add_convert_fusion.10), channel_id=1, source_target_pairs={{0,2},{2,0},{1,3},{3,1},{4,6},{6,4},{5,7},{7,5},{8,10},{10,8},{9,1... | collective-permute-start | bytes 3145736 | tf_op jit(solution)/shard_map/ppermute | solution.py:350
  844.9 66.2 %collective-permute-start.73 = (bf16[256,2048]{1,0:T(8,128)(2,1)}, bf16[256,2048]{1,0:T(8,128)(2,1)S(1)}, u32[]{:S(2)}, u32[]{:S(2)}) collective-permute-start(bf16[256,2048]{1,0:T(8,128)(2,1)} %add_convert_fusion.11), channel_id=1, source_target_pairs={{0,4},{4,0},{1,5},{5,1},{2,6},{6,2},{3,7},{7,3},{8,12},{12,8},{9,1... | collective-permute-start | bytes 3145736 | tf_op jit(solution)/shard_map/ppermute | solution.py:350
  847.6 63.5 %collective-permute-start.72 = (bf16[2,256,1024]{2,1,0:T(8,128)(2,1)}, bf16[2,256,1024]{2,1,0:T(8,128)(2,1)S(1)}, u32[]{:S(2)}, u32[]{:S(2)}) collective-permute-start(bf16[2,256,1024]{2,1,0:T(8,128)(2,1)} %get-tuple-element.478), channel_id=1, source_target_pairs={{0,4},{4,0},{1,5},{5,1},{2,6},{6,2},{3,7},{7,3},{8,12},{12,8},{9,1... | collective-permute-start | bytes 3145736 | tf_op jit(solution)/shard_map/ppermute | solution.py:350
  982.5 52.1 %collective-permute-start.76 = (bf16[4,256,1024]{2,1,0:T(8,128)(2,1)}, bf16[4,256,1024]{2,1,0:T(8,128)(2,1)}, u32[]{:S(2)}, u32[]{:S(2)}) collective-permute-start(bf16[4,256,1024]{2,1,0:T(8,128)(2,1)} %get-tuple-element.331), channel_id=1, source_target_pairs={{0,4},{4,0},{1,5},{5,1},{2,6},{6,2},{3,7},{7,3},{8,12},{12,8},{9,1... | collective-permute-start | bytes 6291464 | tf_op jit(solution)/shard_map/ppermute | solution.py:350
  986.5 107.1 %reduce-scatter.15.cloned.1.call-start = ((), (), s32[]{:S(2)}) async-start(), calls=%async_computation.18 | async-start | bytes 2621440 | tf_op jit(solution)/shard_map/reduce_scatter | solution.py:605
  996.3 47.9 %collective-permute-start.61 = (bf16[512,2048]{1,0:T(8,128)(2,1)}, bf16[512,2048]{1,0:T(8,128)(2,1)}, u32[]{:S(2)}, u32[]{:S(2)}) collective-permute-start(bf16[512,2048]{1,0:T(8,128)(2,1)} %get-tuple-element.296), channel_id=1, source_target_pairs={{0,1},{1,0},{2,3},{3,2},{4,5},{5,4},{6,7},{7,6},{8,9},{9,8},{10,11... | collective-permute-start | bytes 6291464 | tf_op jit(solution)/shard_map/ppermute | solution.py:350
  1061.9 43.0 %collective-permute-start.83 = (bf16[512,2048]{1,0:T(8,128)(2,1)}, bf16[512,2048]{1,0:T(8,128)(2,1)}, u32[]{:S(2)}, u32[]{:S(2)}) collective-permute-start(bf16[512,2048]{1,0:T(8,128)(2,1)} %get-tuple-element.462), channel_id=1, source_target_pairs={{0,1},{1,0},{2,3},{3,2},{4,5},{5,4},{6,7},{7,6},{8,9},{9,8},{10,11... | collective-permute-start | bytes 6291464 | tf_op jit(solution)/shard_map/ppermute | solution.py:350
  1067.0 48.8 %collective-permute-start.85 = (bf16[512,2048]{1,0:T(8,128)(2,1)}, bf16[512,2048]{1,0:T(8,128)(2,1)}, u32[]{:S(2)}, u32[]{:S(2)}) collective-permute-start(bf16[512,2048]{1,0:T(8,128)(2,1)} %fusion.12), channel_id=1, source_target_pairs={{0,2},{2,0},{1,3},{3,1},{4,6},{6,4},{5,7},{7,5},{8,10},{10,8},{9,1... | collective-permute-start | bytes 6291464 | tf_op jit(solution)/shard_map/ppermute | solution.py:350
  (167 other events, 3478.8 us)
Sparse Core Ops, SparseCore 0:
  35.2 101.7 all-gather.2
  139.8 93.0 all-gather.4
  471.4 142.7 reduce-scatter.6
  616.4 145.1 reduce-scatter.8
  775.4 145.2 reduce-scatter.10
  986.7 26.7 reduce-scatter.12
  1044.4 43.4 reduce-scatter.14
  1107.3 28.1 reduce-scatter.16

commit v4 on v3

--- a/solution.py
+++ b/solution.py
@@ -757,11 +757,11 @@
         ],
         axis=1,
     )
-    for axis in ALL:
-        sums = scatter_small(sums, axis)
+    sums = scatter_small(sums, "r")
     dnormed, thirds[1], go, sums, g_value = tie(dnormed.astype(BF), thirds[1], go, sums, g_value)
     go = add_low(*swap_y(go.reshape(nr, 2, wrows, width)))
     thirds[1] = add_low(*thirds[1])
+    sums = scatter_small(sums, "y")
     dnormed = dnormed.reshape(nx, 2, token_count, width)
     dnormed = [add_low(dnormed[dx, 0], shift(dnormed[dx, 1], "c", 1)) for dx in range(nx)]
     dnormed = sum(
@@ -773,8 +773,10 @@
     grad_input = dresid + own_scale * (gd - own_n * jnp.mean(gd * own_n, axis=-1, keepdims=True))
     grad_input = grad_input.reshape(seqs, span, width)
 
-    g_pair, go, scattered[2] = tie(over_r(thirds[1], 0), go, scattered[2])
+    g_pair, go, scattered[2], sums = tie(over_r(thirds[1], 0), go, scattered[2], sums)
     go = over_r(go, 0)
+    for axis in ("x", "c"):
+        sums = scatter_small(sums, axis)
     parted.append(finish_part(scattered[2]))
     g_pair = g_pair.reshape(ng, wrows, 2, cols)
     g_value = g_value.reshape(ng, wrows, 1, cols)

time: 1150 us -> 1120 us (0.974)
  waiting for transfers between devices: 260 us -> 229 us
    ppermute x88, waiting for transfers between devices: 212 us -> 178 us  [shift(): return lax.ppermute(value, axis, [(i, (i + by) % n) for i in range(n)])]
    unnamed x226 -> x222, local copies, waits for them, and re-layouts: 31.4 us -> 29.5 us
  transfers between devices with their start and end apart: 101 -> 101, of which waited for: 30 -> 29; matrix products, arithmetic and copies ran while one was open for 29% -> 30% of each run, Pallas kernels for 27% -> 28%
where the time goes in v4:
time: 1120 us
  Pallas kernels  354 us (32%)
  waiting for transfers between devices  229 us (20%)
  matrix products  164 us (15%)
  other arithmetic  125 us (11%)
  local copies, waits for them, and re-layouts  99.6 us (9%)
  starting transfers between devices  87.4 us (8%)
  blocking collectives  39.3 us (4%)
  between operations  16.5 us (1%)
    ppermute x88, waiting for transfers between devices, shift(): return lax.ppermute(value, axis, [(i, (i + by) % n) for i in range(n)])  178 us
    pallas_call x8, Pallas kernels, experts_out(): pl.pallas_call(partial(experts_out_kernel, cap=cap, forward=forward), out...  140 us
    pallas_call x4, Pallas kernels, experts_call(): pl.pallas_call(partial(kernel, cap=cap, groups=groups), out_shape=outs, g...  128 us
    pallas_call x3, Pallas kernels, attention_call(): pl.pallas_call(partial(kernel, first=first, blocks=blocks, rows=rows, sca...  86.8 us
    dot_general x11, matrix products, dot(): return lax.dot_general(a, b, (dims, ((), ())), preferred_element_type=F32)  80.8 us
    dot_general x3, matrix products, weight_grad(): lax.dot_general(left, right, (((1,), (1,)), ((0,), (0,))), preferred_elem...  78.3 us
    ppermute x88, starting transfers between devices, shift(): return lax.ppermute(value, axis, [(i, (i + by) % n) for i in range(n)])  67.6 us
    convert_element_type x18, other arithmetic, add_low(): return total.astype(BF)  54.5 us
  transfers between devices with their start and end apart: 101, of which 29 were waited for; matrix products, arithmetic and copies ran while one was open for 30% of the time, Pallas kernels for 28%

profile of v4, /device:TPU:0, one launch (start us, length us, event | category | flops | bytes accessed | tf_op | source)
XLA Modules:
  0.0 1115.6 jit_solution(17785848818923673082)
XLA Ops:
  18.5 16.5 %all_to_all.30 = bf16[4,64,1536]{2,1,0:T(8,128)(2,1)} all-to-all(bf16[4,64,1536]{2,1,0:T(8,128)(2,1)} %reshape.378), channel_id=1, replica_groups=mesh['r'=4,'y'=2,'x'=2,'c'=2] {'x','c'}, dimensions={0} | all-to-all | bytes 1572864 | tf_op jit(solution)/shard_map/all_to_all | solution.py:425
  45.9 38.7 %collective-permute-done.1 = bf16[2,256,2048]{2,1,0:T(8,128)(2,1)} collective-permute-done((bf16[2,256,2048]{2,1,0:T(8,128)(2,1)S(1)}, bf16[2,256,2048]{2,1,0:T(8,128)(2,1)}, u32[]{:S(2)}, u32[]{:S(2)}) %collective-permute-start.1) | collective-permute-done | bytes 2097184 | tf_op jit(solution)/shard_map/ppermute | solution.py:350
  143.2 17.5 %fusion.71 = f32[2048,1536]{1,0:T(8,128)S(1)} fusion(bf16[2048,2048]{1,0:T(8,128)(2,1)} %multiply_convert_fusion, bf16[2048,1536]{1,0:T(8,128)(2,1)} %all-gather.3.cloned.1.call-done), kind=kOutput, calls=%fused_computation.271 | convolution fusion | flops 12884901888 | bytes 27262976 | tf_op jit(solution)/shard_map/dot_general | solution.py:20
  166.0 11.1 psum.14
  178.6 15.5 %shard_map.263 = bf16[4,1,256,512]{3,2,1,0:T(8,128)(2,1)} custom-call(s32[4]{0:T(128)} %get-tuple-element.189.inv, s32[2]{0:T(128)} %lens.5, f32[4,2,256,1536]{3,2,1,0:T(8,128)} %bitcast.305, f32[4,2,256,1536]{3,2,1,0:T(8,128)} %bitcast.306, f32[4,2,256,1536]{3,2,1,0:T(8,128)} %bitcast.307, f32[4,2,256,2]{3,2,1,0:T(8,128)} %bitcast.321, f32[1,512]{1,0:T(1,128)} %bitcast.382, ...), custom_call_target="tpu_custom_call" | custom-call | flops 1342177280 | bytes 18874368 | tf_op jit(solution)/shard_map/pallas_call | solution.py:145
  199.7 16.2 %all-to-all-done.1 = bf16[4,256,512]{2,1,0:T(8,128)(2,1)S(1)} async-done(((bf16[4,256,512]{2,1,0:T(8,128)(2,1)}), bf16[4,256,512]{2,1,0:T(8,128)(2,1)S(1)}, u32[]{:S(2)}, u32[]{:S(2)}) %all-to-all-start.1) | async-done | bytes 1048608 | tf_op jit(solution)/shard_map/all_to_all | solution.py:537
  219.9 15.6 %shard_map.264 = bf16[4,1,256,512]{3,2,1,0:T(8,128)(2,1)} custom-call(s32[4]{0:T(128)} %get-tuple-element.189.inv, s32[2]{0:T(128)} %lens.5, f32[4,2,256,1536]{3,2,1,0:T(8,128)} %bitcast.308, f32[4,2,256,1536]{3,2,1,0:T(8,128)} %bitcast.309, f32[4,2,256,1536]{3,2,1,0:T(8,128)} %bitcast.310, f32[4,2,256,2]{3,2,1,0:T(8,128)} %bitcast.322, f32[1,512]{1,0:T(1,128)} %bitcast.383, ...), custom_call_target="tpu_custom_call" | custom-call | flops 1342177280 | bytes 18874368 | tf_op jit(solution)/shard_map/pallas_call | solution.py:145
  243.0 11.5 %all-to-all-done.2 = bf16[4,256,512]{2,1,0:T(8,128)(2,1)} async-done(((bf16[4,256,512]{2,1,0:T(8,128)(2,1)}), bf16[4,256,512]{2,1,0:T(8,128)(2,1)}, u32[]{:S(2)}, u32[]{:S(2)}) %all-to-all-start.2) | async-done | bytes 1048608 | tf_op jit(solution)/shard_map/all_to_all | solution.py:537
  271.0 21.9 %collective-permute-done.45.refs_14_ = f32[16,512]{1,0:T(8,128)S(1)} collective-permute-done((f32[16,512]{1,0:T(8,128)S(1)}, f32[16,512]{1,0:T(8,128)S(1)}, u32[]{:S(2)}, u32[]{:S(2)}) %collective-permute-start.45) | collective-permute-done | bytes 32800 | tf_op jit(solution)/shard_map/ppermute | solution.py:350
  309.6 23.6 %shard_map.265 = (bf16[2,2304,2048]{2,1,0:T(8,128)(2,1)}, f32[2,2304,1024]{2,1,0:T(8,128)}) custom-call(s32[3]{0:T(128)} %pad_add_fusion.1.base, bf16[256,2048]{1,0:T(8,128)(2,1)} %get-tuple-element.188.refs_0_, bf16[256,2048]{1,0:T(8,128)(2,1)} %get-tuple-element.202.refs_1_, bf16[256,2048]{1,0:T(8,128)(2,1)} %collective-permute-done.28.refs_2_, ...), custom_call_target="tpu_custom_call" | custom-call | flops 14495514624 | bytes 49807360 | tf_op jit(solution)/shard_map/pallas_call | solution.py:255
  337.1 23.8 %shard_map.266 = (bf16[2,2304,2048]{2,1,0:T(8,128)(2,1)}, f32[2,2304,1024]{2,1,0:T(8,128)}) custom-call(s32[3]{0:T(128)} %pad_add_fusion.1.base, bf16[256,2048]{1,0:T(8,128)(2,1)} %collective-permute-done.19.refs_0_, bf16[256,2048]{1,0:T(8,128)(2,1)} %collective-permute-done.18.refs_1_, ...), custom_call_target="tpu_custom_call", output_to_operand_aliasing={{0}: (14, {}), {1}: (15, {})} | custom-call | flops 14495514624 | bytes 49807360 | tf_op jit(solution)/shard_map/pallas_call | solution.py:255
  362.1 40.3 %shard_map.267 = (bf16[2,2304,2048]{2,1,0:T(8,128)(2,1)}, bf16[2,2304,1024]{2,1,0:T(8,128)(2,1)}, bf16[2,2304,1024]{2,1,0:T(8,128)(2,1)}, bf16[2,2304,1024]{2,1,0:T(8,128)(2,1)}, f32[2,2,2,1,512]{4,3,2,1,0:T(1,128)}) custom-call(s32[3]{0:T(128)} %pad_add_fusion.1.base, bf16[256,2048]{1,0:T(8,128)(2,1)} %copy-done.26, bf16[256,2048]{1,0:T(8,128)(2,1)} %copy-done.24, ...), custom_call_target="tpu_custom_call" | custom-call | flops 24159191040 | bytes 58195968 | tf_op jit(solution)/shard_map/pallas_call | solution.py:255
  404.3 40.2 %shard_map.268 = (bf16[2,2304,2048]{2,1,0:T(8,128)(2,1)}, bf16[2,2304,1024]{2,1,0:T(8,128)(2,1)}, bf16[2,2304,1024]{2,1,0:T(8,128)(2,1)}, bf16[2,2304,1024]{2,1,0:T(8,128)(2,1)}, f32[2,2,2,1,512]{4,3,2,1,0:T(1,128)}) custom-call(s32[3]{0:T(128)} %pad_add_fusion.1.base, ...), custom_call_target="tpu_custom_call", output_to_operand_aliasing={{0}: (20, {}), {1}: (21, {}), {2}: (22, {}), {3}: (23, {})} | custom-call | flops 24159191040 | bytes 58195968 | tf_op jit(solution)/shard_map/pallas_call | solution.py:255
  444.5 26.8 %convolution_convert_fusion.3 = bf16[2,2048,1024]{2,1,0:T(8,128)(2,1)} fusion(bf16[2,2304,2048]{2,1,0:T(8,128)(2,1)} %get-tuple-element.212, bf16[2,2304,1024]{2,1,0:T(8,128)(2,1)} %get-tuple-element.236.refs_0_), kind=kOutput, calls=%fused_computation.16 | convolution fusion | flops 19331547136 | bytes 36700160 | tf_op jit(solution)/shard_map/dot_general | solution.py:589
  471.3 21.0 %shard_map.269 = (bf16[512,2048]{1,0:T(8,128)(2,1)}, bf16[512,2048]{1,0:T(8,128)(2,1)}) custom-call(s32[3]{0:T(128)} %pad_add_fusion.1.base, bf16[2,2304,1024]{2,1,0:T(8,128)(2,1)} %get-tuple-element.238.refs_0_, bf16[2,2304,1024]{2,1,0:T(8,128)(2,1)} %get-tuple-element.301.refs_1_, f32[512,16]{1,0:T(8,128)} %bitcast.362, f32[512,16]{1,0:T(8,128)} %bitcast.364, ...), custom_call_target="tpu_custom_call" | custom-call | flops 12079595520 | bytes 25690112 | tf_op jit(solution)/shard_map/pallas_call | solution.py:330
  492.8 20.5 %shard_map.270 = (bf16[512,2048]{1,0:T(8,128)(2,1)}, bf16[512,2048]{1,0:T(8,128)(2,1)}) custom-call(s32[3]{0:T(128)} %pad_add_fusion.1.base, bf16[2,2304,1024]{2,1,0:T(8,128)(2,1)} %get-tuple-element.238.refs_0_, bf16[2,2304,1024]{2,1,0:T(8,128)(2,1)} %get-tuple-element.301.refs_1_, f32[512,16]{1,0:T(8,128)} %bitcast.354, f32[512,16]{1,0:T(8,128)} %bitcast.360, ...), custom_call_target="tpu_custom_call" | custom-call | flops 12079595520 | bytes 25690112 | tf_op jit(solution)/shard_map/pallas_call | solution.py:330
  516.4 20.9 %shard_map.271 = (bf16[512,2048]{1,0:T(8,128)(2,1)}, bf16[512,2048]{1,0:T(8,128)(2,1)}) custom-call(s32[3]{0:T(128)} %pad_add_fusion.1.base, bf16[2,2304,1024]{2,1,0:T(8,128)(2,1)} %get-tuple-element.238.refs_0_, bf16[2,2304,1024]{2,1,0:T(8,128)(2,1)} %get-tuple-element.301.refs_1_, f32[512,16]{1,0:T(8,128)} %bitcast.352, f32[512,16]{1,0:T(8,128)} %bitcast.358, ...), custom_call_target="tpu_custom_call" | custom-call | flops 12079595520 | bytes 25690112 | tf_op jit(solution)/shard_map/pallas_call | solution.py:330
  551.9 24.8 %convolution_convert_fusion.2 = bf16[2,2048,1024]{2,1,0:T(8,128)(2,1)} fusion(bf16[2,2304,2048]{2,1,0:T(8,128)(2,1)} %get-tuple-element.266, bf16[2,2304,1024]{2,1,0:T(8,128)(2,1)S(1)} %bitcast.315), kind=kOutput, calls=%fused_computation.15 | convolution fusion | flops 19331547136 | bytes 36700160 | tf_op jit(solution)/shard_map/dot_general | solution.py:589
  587.2 14.2 %shard_map.273 = (bf16[512,2048]{1,0:T(8,128)(2,1)}, bf16[512,2048]{1,0:T(8,128)(2,1)}) custom-call(s32[3]{0:T(128)} %pad_add_fusion.1.base, bf16[2,2304,1024]{2,1,0:T(8,128)(2,1)} %get-tuple-element.236.refs_0_, f32[512,16]{1,0:T(8,128)} %bitcast.363, f32[512,16]{1,0:T(8,128)} %bitcast.365, bf16[4,1024,2048]{2,1,0:T(8,128)(2,1)} %refs_3_.7), custom_call_target="tpu_custom_call" | custom-call | flops 7247757312 | bytes 14942208 | tf_op jit(solution)/shard_map/pallas_call | solution.py:330
  601.5 12.7 %reduce-scatter.7.cloned.1.call-done = bf16[2,512,1024]{2,1,0:T(8,128)(2,1)} async-done(((bf16[2,2048,1024]{2,1,0:T(8,128)(2,1)}), bf16[2,512,1024]{2,1,0:T(8,128)(2,1)}) %reduce-scatter.7.cloned.1.call-update) | async-done | bytes 2097168 | tf_op jit(solution)/shard_map/reduce_scatter | solution.py:605
  616.7 20.6 %shard_map.272 = (bf16[512,2048]{1,0:T(8,128)(2,1)}, bf16[512,2048]{1,0:T(8,128)(2,1)}) custom-call(s32[3]{0:T(128)} %pad_add_fusion.1.base, bf16[2,2304,1024]{2,1,0:T(8,128)(2,1)} %get-tuple-element.238.refs_0_, bf16[2,2304,1024]{2,1,0:T(8,128)(2,1)} %get-tuple-element.301.refs_1_, f32[512,16]{1,0:T(8,128)} %copy-done.41, f32[512,16]{1,0:T(8,128)} %bitcast.356, ...), custom_call_target="tpu_custom_call" | custom-call | flops 12079595520 | bytes 25690112 | tf_op jit(solution)/shard_map/pallas_call | solution.py:330
  657.6 14.2 %shard_map.274 = (bf16[512,2048]{1,0:T(8,128)(2,1)}, bf16[512,2048]{1,0:T(8,128)(2,1)}) custom-call(s32[3]{0:T(128)} %pad_add_fusion.1.base, bf16[2,2304,1024]{2,1,0:T(8,128)(2,1)} %get-tuple-element.236.refs_0_, f32[512,16]{1,0:T(8,128)} %bitcast.355, f32[512,16]{1,0:T(8,128)} %bitcast.361, bf16[4,1024,2048]{2,1,0:T(8,128)(2,1)} %refs_3_.7), custom_call_target="tpu_custom_call" | custom-call | flops 7247757312 | bytes 14942208 | tf_op jit(solution)/shard_map/pallas_call | solution.py:330
  679.9 14.2 %shard_map.275 = (bf16[512,2048]{1,0:T(8,128)(2,1)}, bf16[512,2048]{1,0:T(8,128)(2,1)}) custom-call(s32[3]{0:T(128)} %pad_add_fusion.1.base, bf16[2,2304,1024]{2,1,0:T(8,128)(2,1)} %get-tuple-element.236.refs_0_, f32[512,16]{1,0:T(8,128)} %bitcast.353, f32[512,16]{1,0:T(8,128)} %bitcast.359, bf16[4,1024,2048]{2,1,0:T(8,128)(2,1)} %refs_3_.7), custom_call_target="tpu_custom_call" | custom-call | flops 7247757312 | bytes 14942208 | tf_op jit(solution)/shard_map/pallas_call | solution.py:330
  694.1 14.2 %shard_map.276 = (bf16[512,2048]{1,0:T(8,128)(2,1)}, bf16[512,2048]{1,0:T(8,128)(2,1)}) custom-call(s32[3]{0:T(128)} %pad_add_fusion.1.base, bf16[2,2304,1024]{2,1,0:T(8,128)(2,1)} %get-tuple-element.236.refs_0_, f32[512,16]{1,0:T(8,128)} %copy-done.41, f32[512,16]{1,0:T(8,128)} %bitcast.357, bf16[4,1024,2048]{2,1,0:T(8,128)(2,1)} %refs_3_.7), custom_call_target="tpu_custom_call" | custom-call | flops 7247757312 | bytes 14942208 | tf_op jit(solution)/shard_map/pallas_call | solution.py:330
  739.4 26.8 %convolution_convert_fusion.1 = bf16[2,2048,1024]{2,1,0:T(8,128)(2,1)} fusion(bf16[2,2304,2048]{2,1,0:T(8,128)(2,1)} %get-tuple-element.266, bf16[2,2304,1024]{2,1,0:T(8,128)(2,1)} %get-tuple-element.301.refs_1_), kind=kOutput, calls=%fused_computation.14 | convolution fusion | flops 19331547136 | bytes 36700160 | tf_op jit(solution)/shard_map/dot_general | solution.py:589
  800.1 10.6 collective-permute-done.69
  813.7 21.8 %collective-permute-done.64 = bf16[256,2048]{1,0:T(8,128)(2,1)} collective-permute-done((bf16[256,2048]{1,0:T(8,128)(2,1)}, bf16[256,2048]{1,0:T(8,128)(2,1)}, u32[]{:S(2)}, u32[]{:S(2)}) %collective-permute-start.64) | collective-permute-done | bytes 1048608 | tf_op jit(solution)/shard_map/ppermute | solution.py:350
  849.7 55.6 %shard_map.277 = (f32[4,2,256,512]{3,2,1,0:T(8,128)}, f32[4,2,256,512]{3,2,1,0:T(8,128)}, bf16[4,2,256,512]{3,2,1,0:T(8,128)(2,1)}, f32[4,2,256,2]{3,2,1,0:T(8,128)}, f32[2,2,512]{2,1,0:T(2,128)}) custom-call(s32[4]{0:T(128)} %get-tuple-element.189.inv, s32[2]{0:T(128)} %lens.5, f32[4,2,256,1536]{3,2,1,0:T(8,128)} %bitcast.311, ...), custom_call_target="tpu_custom_call" | custom-call | flops 6710886400 | bytes 18874368 | tf_op jit(solution)/shard_map/pallas_call | solution.py:145
  926.5 11.7 %psum.15 = f32[2,4,512]{2,1,0:T(4,128)S(1)} all-reduce(f32[2,4,512]{2,1,0:T(4,128)S(1)} %pad_maximum_fusion.8), channel_id=1, replica_groups=mesh['r'=4,'y'=2,'x'=2,'c'=2] {'x','c'}, use_global_device_ids=true, to_apply=%region_16.17 | all-reduce | flops 4096 | bytes 32768 | tf_op jit(solution)/shard_map/psum | solution.py:503
  946.8 13.1 %fusion.21 = bf16[2048,1024]{1,0:T(8,128)(2,1)S(1)} fusion(bf16[2048,2048]{1,0:T(8,128)(2,1)} %multiply_convert_fusion, bf16[2048,512]{1,0:T(8,128)(2,1)S(1)} %get-tuple-element.329, bf16[2048,512]{1,0:T(8,128)(2,1)S(1)} %get-tuple-element.328), kind=kOutput, calls=%fused_computation.61 | convolution fusion | flops 8600420352 | bytes 16777216 | tf_op jit(solution)/shard_map/dot_general | solution.py:20
  965.8 21.0 %multiply_reduce_fusion = (f32[2048]{0:T(1024)S(1)}, bf16[2048,2048]{1,0:T(8,128)(2,1)}) fusion(f32[2048]{0:T(1024)S(1)} %bitcast.394, bf16[1,2,256,2048]{3,2,1,0:T(8,128)(2,1)} %bitcast.10, bf16[1,2,256,2048]{3,2,1,0:T(8,128)(2,1)} %bitcast.9, bf16[1,2,256,2048]{3,2,1,0:T(8,128)(2,1)} %bitcast.8, bf16[1,2,256,2048]{3,2,1,0:T(8,128)(2,1)S(1)} %bitcast.318, ...), kind=kOutput, calls=%fused_computation.1 | convolution fusion | flops 12937328640 | bytes 29376512 | tf_op jit(solution)/shard_map/dot_general | solution.py:20
  995.8 13.0 %collective-permute-done.76 = bf16[4,256,1024]{2,1,0:T(8,128)(2,1)} collective-permute-done((bf16[4,256,1024]{2,1,0:T(8,128)(2,1)}, bf16[4,256,1024]{2,1,0:T(8,128)(2,1)}, u32[]{:S(2)}, u32[]{:S(2)}) %collective-permute-start.76) | collective-permute-done | bytes 2097184 | tf_op jit(solution)/shard_map/ppermute | solution.py:350
  (608 shorter events, 429.2 us)
Async XLA Ops:
  7.2 136.0 %all-gather.3.cloned.1.call-start = ((), (), s32[]{:S(2)}) async-start(), calls=%async_computation.12 | async-start | bytes 7077888 | tf_op jit(solution)/shard_map/all_gather | solution.py:426
  35.1 221.7 %all-gather.5.cloned.1.call-start = ((), (), s32[]{:S(2)}) async-start(), calls=%async_computation.13 | async-start | bytes 8650752 | tf_op jit(solution)/shard_map/all_gather | solution.py:432
  35.8 48.7 %collective-permute-start.1 = (bf16[2,256,2048]{2,1,0:T(8,128)(2,1)S(1)}, bf16[2,256,2048]{2,1,0:T(8,128)(2,1)}, u32[]{:S(2)}, u32[]{:S(2)}) collective-permute-start(bf16[2,256,2048]{2,1,0:T(8,128)(2,1)S(1)} %copy-done.1), channel_id=1, source_target_pairs={{0,2},{2,0},{1,3},{3,1},{4,6},{6,4},{5,7},{7,5},{8,10},{10,8},{9,1... | collective-permute-start | bytes 6291464 | tf_op jit(solution)/shard_map/ppermute | solution.py:350
  35.9 85.8 %collective-permute-start = (bf16[2,256,2048]{2,1,0:T(8,128)(2,1)S(1)}, bf16[2,256,2048]{2,1,0:T(8,128)(2,1)}, u32[]{:S(2)}, u32[]{:S(2)}) collective-permute-start(bf16[2,256,2048]{2,1,0:T(8,128)(2,1)S(1)} %copy-done.1), channel_id=1, source_target_pairs={{0,1},{1,0},{2,3},{3,2},{4,5},{5,4},{6,7},{7,6},{8,9},{9,8},{10,11... | collective-permute-start | bytes 6291464 | tf_op jit(solution)/shard_map/ppermute | solution.py:350
  36.5 76.4 %collective-permute-start.10 = (f32[16,512]{0,1:T(8,128)S(1)}, f32[16,512]{0,1:T(8,128)S(1)}, u32[]{:S(2)}, u32[]{:S(2)}) collective-permute-start(f32[16,512]{0,1:T(8,128)S(1)} %bitcast.348), channel_id=1, source_target_pairs={{0,2},{2,0},{1,3},{3,1},{4,6},{6,4},{5,7},{7,5},{8,10},{10,8},{9,1... | collective-permute-start | bytes 98312 | tf_op jit(solution)/shard_map/ppermute | solution.py:350
  38.5 78.3 %collective-permute-start.12 = (f32[16,512]{0,1:T(8,128)S(1)}, f32[16,512]{0,1:T(8,128)S(1)}, u32[]{:S(2)}, u32[]{:S(2)}) collective-permute-start(f32[16,512]{0,1:T(8,128)S(1)} %bitcast.349), channel_id=1, source_target_pairs={{0,4},{4,0},{1,5},{5,1},{2,6},{6,2},{3,7},{7,3},{8,12},{12,8},{9,1... | collective-permute-start | bytes 98312 | tf_op jit(solution)/shard_map/ppermute | solution.py:350
  40.9 46.6 %collective-permute-start.3 = (bf16[64,20]{0,1:T(8,128)(2,1)S(1)}, bf16[64,20]{0,1:T(8,128)(2,1)S(1)}, u32[]{:S(2)}, u32[]{:S(2)}) collective-permute-start(bf16[64,20]{0,1:T(8,128)(2,1)S(1)} %concatenate.79), channel_id=1, source_target_pairs={{0,1},{1,0},{2,3},{3,2},{4,5},{5,4},{6,7},{7,6},{8,9},{9,8},{10,11... | collective-permute-start | bytes 7688 | tf_op jit(solution)/shard_map/ppermute | solution.py:350
  135.4 64.3 %collective-permute-start.18 = (bf16[256,2048]{1,0:T(8,128)(2,1)}, bf16[256,2048]{1,0:T(8,128)(2,1)}, u32[]{:S(2)}, u32[]{:S(2)}) collective-permute-start(bf16[256,2048]{1,0:T(8,128)(2,1)} %get-tuple-element.202.refs_1_), channel_id=1, source_target_pairs={{0,4},{4,0},{1,5},{5,1},{2,6},{6,2},{3,7},{7,3},{8,12},{12,8},{9,1... | collective-permute-start | bytes 3145736 | tf_op jit(solution)/shard_map/ppermute | solution.py:350
  178.6 41.3 %collective-permute-start.19 = (bf16[256,2048]{1,0:T(8,128)(2,1)}, bf16[256,2048]{1,0:T(8,128)(2,1)}, u32[]{:S(2)}, u32[]{:S(2)}) collective-permute-start(bf16[256,2048]{1,0:T(8,128)(2,1)} %get-tuple-element.188.refs_0_), channel_id=1, source_target_pairs={{0,4},{4,0},{1,5},{5,1},{2,6},{6,2},{3,7},{7,3},{8,12},{12,8},{9,1... | collective-permute-start | bytes 3145736 | tf_op jit(solution)/shard_map/ppermute | solution.py:350
  197.6 44.8 %collective-permute-start.20 = (bf16[256,2048]{1,0:T(8,128)(2,1)}, bf16[256,2048]{1,0:T(8,128)(2,1)}, u32[]{:S(2)}, u32[]{:S(2)}) collective-permute-start(bf16[256,2048]{1,0:T(8,128)(2,1)} %collective-permute-done.16.refs_6_), channel_id=1, source_target_pairs={{0,4},{4,0},{1,5},{5,1},{2,6},{6,2},{3,7},{7,3},{8,12},{12,8},{9,1... | collective-permute-start | bytes 3145736 | tf_op jit(solution)/shard_map/ppermute | solution.py:350
  240.0 374.2 %reduce-scatter.7.cloned.1.call-start = ((), (), s32[]{:S(2)}) async-start(), calls=%async_computation.14 | async-start | bytes 10485760 | tf_op jit(solution)/shard_map/reduce_scatter | solution.py:605
  267.4 40.8 %collective-permute-start.27 = (bf16[256,2048]{1,0:T(8,128)(2,1)}, bf16[256,2048]{1,0:T(8,128)(2,1)}, u32[]{:S(2)}, u32[]{:S(2)}) collective-permute-start(bf16[256,2048]{1,0:T(8,128)(2,1)} %collective-permute-done.21.refs_7_), channel_id=1, source_target_pairs={{0,1},{1,0},{2,3},{3,2},{4,5},{5,4},{6,7},{7,6},{8,9},{9,8},{10,11... | collective-permute-start | bytes 3145736 | tf_op jit(solution)/shard_map/ppermute | solution.py:350
  360.9 41.5 %collective-permute-start.48 = (f32[16,512]{1,0:T(8,128)S(1)}, f32[16,512]{1,0:T(8,128)S(1)}, u32[]{:S(2)}, u32[]{:S(2)}) collective-permute-start(f32[16,512]{1,0:T(8,128)S(1)} %collective-permute-done.47.refs_6_), channel_id=1, source_target_pairs={{0,1},{1,0},{2,3},{3,2},{4,5},{5,4},{6,7},{7,6},{8,9},{9,8},{10,11... | collective-permute-start | bytes 98312 | tf_op jit(solution)/shard_map/ppermute | solution.py:350
  361.0 41.5 %collective-permute-start.50 = (f32[16,512]{1,0:T(8,128)S(1)}, f32[16,512]{1,0:T(8,128)S(1)}, u32[]{:S(2)}, u32[]{:S(2)}) collective-permute-start(f32[16,512]{1,0:T(8,128)S(1)} %collective-permute-done.49.refs_14_), channel_id=1, source_target_pairs={{0,1},{1,0},{2,3},{3,2},{4,5},{5,4},{6,7},{7,6},{8,9},{9,8},{10,11... | collective-permute-start | bytes 98312 | tf_op jit(solution)/shard_map/ppermute | solution.py:350
  361.5 40.9 %collective-permute-start.42 = (bf16[256,2048]{1,0:T(8,128)(2,1)}, bf16[256,2048]{1,0:T(8,128)(2,1)S(1)}, u32[]{:S(2)}, u32[]{:S(2)}) collective-permute-start(bf16[256,2048]{1,0:T(8,128)(2,1)} %collective-permute-done.38.refs_1_), channel_id=1, source_target_pairs={{0,1},{1,0},{2,3},{3,2},{4,5},{5,4},{6,7},{7,6},{8,9},{9,8},{10,11... | collective-permute-start | bytes 3145736 | tf_op jit(solution)/shard_map/ppermute | solution.py:350
  361.6 40.8 %collective-permute-start.36 = (bf16[256,2048]{1,0:T(8,128)(2,1)}, bf16[256,2048]{1,0:T(8,128)(2,1)S(1)}, u32[]{:S(2)}, u32[]{:S(2)}) collective-permute-start(bf16[256,2048]{1,0:T(8,128)(2,1)} %collective-permute-done.32.refs_8_), channel_id=1, source_target_pairs={{0,1},{1,0},{2,3},{3,2},{4,5},{5,4},{6,7},{7,6},{8,9},{9,8},{10,11... | collective-permute-start | bytes 3145736 | tf_op jit(solution)/shard_map/ppermute | solution.py:350
  471.3 302.7 %reduce-scatter.9.cloned.1.call-start = ((), (), s32[]{:S(2)}) async-start(), calls=%async_computation.15 | async-start | bytes 10485760 | tf_op jit(solution)/shard_map/reduce_scatter | solution.py:605
  544.4 42.8 %collective-permute-start.56 = (bf16[256,2048]{1,0:T(8,128)(2,1)}, bf16[256,2048]{1,0:T(8,128)(2,1)S(1)}, u32[]{:S(2)}, u32[]{:S(2)}) collective-permute-start(bf16[256,2048]{1,0:T(8,128)(2,1)} %slice.167), channel_id=1, source_target_pairs={{0,4},{4,0},{1,5},{5,1},{2,6},{6,2},{3,7},{7,3},{8,12},{12,8},{9,1... | collective-permute-start | bytes 3145736 | tf_op jit(solution)/shard_map/ppermute | solution.py:350
  739.4 226.3 %reduce-scatter.11.cloned.1.call-start = ((), (), s32[]{:S(2)}) async-start(), calls=%async_computation.16 | async-start | bytes 10485760 | tf_op jit(solution)/shard_map/reduce_scatter | solution.py:605
  775.3 233.5 %reduce-scatter.13.cloned.1.call-start = ((), (), s32[]{:S(2)}) async-start(), calls=%async_computation.17 | async-start | bytes 1310720 | tf_op jit(solution)/shard_map/reduce_scatter | solution.py:605
  791.8 43.7 %collective-permute-start.64 = (bf16[256,2048]{1,0:T(8,128)(2,1)}, bf16[256,2048]{1,0:T(8,128)(2,1)}, u32[]{:S(2)}, u32[]{:S(2)}) collective-permute-start(bf16[256,2048]{1,0:T(8,128)(2,1)} %get-tuple-element.485), channel_id=1, source_target_pairs={{0,2},{2,0},{1,3},{3,1},{4,6},{6,4},{5,7},{7,5},{8,10},{10,8},{9,1... | collective-permute-start | bytes 3145736 | tf_op jit(solution)/shard_map/ppermute | solution.py:350
  791.8 43.7 %collective-permute-start.65 = (bf16[256,2048]{1,0:T(8,128)(2,1)}, bf16[256,2048]{1,0:T(8,128)(2,1)}, u32[]{:S(2)}, u32[]{:S(2)}) collective-permute-start(bf16[256,2048]{1,0:T(8,128)(2,1)} %get-tuple-element.484), channel_id=1, source_target_pairs={{0,4},{4,0},{1,5},{5,1},{2,6},{6,2},{3,7},{7,3},{8,12},{12,8},{9,1... | collective-permute-start | bytes 3145736 | tf_op jit(solution)/shard_map/ppermute | solution.py:350
  799.2 113.4 %collective-permute-start.71 = (bf16[2,256,1024]{2,1,0:T(8,128)(2,1)}, bf16[2,256,1024]{2,1,0:T(8,128)(2,1)}, u32[]{:S(2)}, u32[]{:S(2)}) collective-permute-start(bf16[2,256,1024]{2,1,0:T(8,128)(2,1)} %get-tuple-element.482), channel_id=1, source_target_pairs={{0,4},{4,0},{1,5},{5,1},{2,6},{6,2},{3,7},{7,3},{8,12},{12,8},{9,1... | collective-permute-start | bytes 3145736 | tf_op jit(solution)/shard_map/ppermute | solution.py:350
  838.6 69.3 %collective-permute-start.70 = (bf16[8,64,2048]{2,1,0:T(8,128)(2,1)}, bf16[8,64,2048]{2,1,0:T(8,128)(2,1)}, u32[]{:S(2)}, u32[]{:S(2)}) collective-permute-start(bf16[8,64,2048]{2,1,0:T(8,128)(2,1)} %dynamic-slice_bitcast_fusion.2), channel_id=1, source_target_pairs={{0,2},{2,0},{1,3},{3,1},{4,6},{6,4},{5,7},{7,5},{8,10},{10,8},{9,1... | collective-permute-start | bytes 6291464 | tf_op jit(solution)/shard_map/ppermute | solution.py:350
  843.0 69.6 %collective-permute-start.74 = (bf16[256,2048]{1,0:T(8,128)(2,1)}, bf16[256,2048]{1,0:T(8,128)(2,1)}, u32[]{:S(2)}, u32[]{:S(2)}) collective-permute-start(bf16[256,2048]{1,0:T(8,128)(2,1)} %add_convert_fusion.10), channel_id=1, source_target_pairs={{0,2},{2,0},{1,3},{3,1},{4,6},{6,4},{5,7},{7,5},{8,10},{10,8},{9,1... | collective-permute-start | bytes 3145736 | tf_op jit(solution)/shard_map/ppermute | solution.py:350
  846.1 66.5 %collective-permute-start.73 = (bf16[256,2048]{1,0:T(8,128)(2,1)}, bf16[256,2048]{1,0:T(8,128)(2,1)}, u32[]{:S(2)}, u32[]{:S(2)}) collective-permute-start(bf16[256,2048]{1,0:T(8,128)(2,1)} %add_convert_fusion.11), channel_id=1, source_target_pairs={{0,4},{4,0},{1,5},{5,1},{2,6},{6,2},{3,7},{7,3},{8,12},{12,8},{9,1... | collective-permute-start | bytes 3145736 | tf_op jit(solution)/shard_map/ppermute | solution.py:350
  848.7 64.0 %collective-permute-start.72 = (bf16[2,256,1024]{2,1,0:T(8,128)(2,1)}, bf16[2,256,1024]{2,1,0:T(8,128)(2,1)}, u32[]{:S(2)}, u32[]{:S(2)}) collective-permute-start(bf16[2,256,1024]{2,1,0:T(8,128)(2,1)} %get-tuple-element.480), channel_id=1, source_target_pairs={{0,4},{4,0},{1,5},{5,1},{2,6},{6,2},{3,7},{7,3},{8,12},{12,8},{9,1... | collective-permute-start | bytes 3145736 | tf_op jit(solution)/shard_map/ppermute | solution.py:350
  908.0 109.7 %collective-permute-start.61 = (bf16[512,2048]{1,0:T(8,128)(2,1)}, bf16[512,2048]{1,0:T(8,128)(2,1)}, u32[]{:S(2)}, u32[]{:S(2)}) collective-permute-start(bf16[512,2048]{1,0:T(8,128)(2,1)} %get-tuple-element.297), channel_id=1, source_target_pairs={{0,1},{1,0},{2,3},{3,2},{4,5},{5,4},{6,7},{7,6},{8,9},{9,8},{10,11... | collective-permute-start | bytes 6291464 | tf_op jit(solution)/shard_map/ppermute | solution.py:350
  963.6 45.2 %collective-permute-start.76 = (bf16[4,256,1024]{2,1,0:T(8,128)(2,1)}, bf16[4,256,1024]{2,1,0:T(8,128)(2,1)}, u32[]{:S(2)}, u32[]{:S(2)}) collective-permute-start(bf16[4,256,1024]{2,1,0:T(8,128)(2,1)} %get-tuple-element.332), channel_id=1, source_target_pairs={{0,4},{4,0},{1,5},{5,1},{2,6},{6,2},{3,7},{7,3},{8,12},{12,8},{9,1... | collective-permute-start | bytes 6291464 | tf_op jit(solution)/shard_map/ppermute | solution.py:350
  965.8 99.2 %reduce-scatter.15.cloned.1.call-start = ((), (), s32[]{:S(2)}) async-start(), calls=%async_computation.18 | async-start | bytes 2621440 | tf_op jit(solution)/shard_map/reduce_scatter | solution.py:605
  1027.5 49.0 %collective-permute-start.80 = (bf16[512,2048]{1,0:T(8,128)(2,1)}, bf16[512,2048]{1,0:T(8,128)(2,1)}, u32[]{:S(2)}, u32[]{:S(2)}) collective-permute-start(bf16[512,2048]{1,0:T(8,128)(2,1)} %get-tuple-element.464), channel_id=1, source_target_pairs={{0,1},{1,0},{2,3},{3,2},{4,5},{5,4},{6,7},{7,6},{8,9},{9,8},{10,11... | collective-permute-start | bytes 6291464 | tf_op jit(solution)/shard_map/ppermute | solution.py:350
  1032.6 49.4 %collective-permute-start.82 = (bf16[512,2048]{1,0:T(8,128)(2,1)}, bf16[512,2048]{1,0:T(8,128)(2,1)}, u32[]{:S(2)}, u32[]{:S(2)}) collective-permute-start(bf16[512,2048]{1,0:T(8,128)(2,1)} %fusion.12), channel_id=1, source_target_pairs={{0,2},{2,0},{1,3},{3,1},{4,6},{6,4},{5,7},{7,5},{8,10},{10,8},{9,1... | collective-permute-start | bytes 6291464 | tf_op jit(solution)/shard_map/ppermute | solution.py:350
  (165 other events, 3417.9 us)
Sparse Core Ops, SparseCore 0:
  35.2 101.7 all-gather.2
  139.8 92.8 all-gather.4
  471.4 142.7 reduce-scatter.6
  616.4 145.1 reduce-scatter.8
  774.2 145.2 reduce-scatter.10
  965.9 29.5 reduce-scatter.12
  1017.8 45.4 reduce-scatter.14
  1078.9 27.8 reduce-scatter.16
